TPU v7x, 256 devices: a whole 4x4x8 slice. The times are simulated.
256 devices in a mesh: replica: 16 (over x, z_lo), pipe: 2 (over core), tensor: 8 (over y, z_hi).
Axes of the slice: x: 4, y: 4, z: 8 (z_hi: 2, z_lo: 4; z = z_hi * 4 + z_lo), core: 2. Of those that a mesh axis runs over, the one named last changes fastest.
Arguments:
- patches: bfloat16 [192, 4, 32, 1280], P('replica', 'pipe', None, 'tensor'), may hold values from -6 to 6
- tile_counts: int32 [192], replicated, may hold values from 1 to 4
- ln_gain: float32 [1280], replicated, may hold values from 0.1 to 1.9
- enc_qkv: bfloat16 [1280, 3, 1280], P(None, None, 'tensor'), may hold values from -0.15625 to 0.15625
- enc_out_w: bfloat16 [1280, 1280], P('tensor'), may hold values from -0.15625 to 0.15625
- proj_w: bfloat16 [1280, 8192], P(None, 'tensor'), may hold values from -0.15625 to 0.15625
- cross_kv_w: bfloat16 [8192, 2, 1024], P('tensor'), may hold values from -0.09375 to 0.09375
- k_gain: float32 [128], replicated, may hold values from 0.1 to 1.9
- plan: int32 [192, 1], replicated, may hold values from 0 to 15; in each aligned block of 12 rows (0 to 11, 12 to 23, ...) at most 2 rows name the same one
- row_pick: int32 [1024], P(('replica', 'pipe')), may hold values from 0 to 4095
- q_cross: bfloat16 [2, 1024, 8192], P(None, ('replica', 'pipe'), 'tensor'), may hold values from -6 to 6
- q_self: bfloat16 [2, 1024, 8192], P(None, ('replica', 'pipe'), 'tensor'), may hold values from -6 to 6
- cache_kv: bfloat16 [1024, 32, 2, 1024], P(('replica', 'pipe'), None, None, 'tensor'), may hold values from -6 to 6
- new_kv: bfloat16 [2, 1024, 2, 1024], P(None, ('replica', 'pipe'), None, 'tensor'), may hold values from -6 to 6
- kv_len: int32 [1024], P(('replica', 'pipe')), may hold values from 1 to 32
Outputs:
- cross_out: bfloat16 [2, 1024, 8192], P(None, ('replica', 'pipe'), 'tensor')
- self_out: bfloat16 [2, 1024, 8192], P(None, ('replica', 'pipe'), 'tensor')
Inputs may be any that keep to these rules, and one draw needn't show every extreme that they name: `plan`: among the 12 images g * 12 to (g + 1) * 12 - 1 of one encoder group at most 2 have one replica, exactly 2 in some group; every replica is named by some image.
All inputs are finite; a program needn't handle non-finite values.
Results may differ from a plain program's by a relative error of at most 0.03.
Values may be sent and summed in bfloat16 or wider, within the bound.
No kernel may reach another device: no remote copies, remote signals or barrier semaphores. Data moves between devices by JAX's collectives and lax.ppermute only.
A program may use at most 128 MiB of HBM per device.

v0:
```python
import jax
import jax.numpy as jnp
from jax import lax
from jax.sharding import PartitionSpec as P

HEADS = 64
KV_HEADS = 8
HD = 128
ENC_W = 1280
ENC_HEADS = 16
CAP = 2
STEPS = 2
LMAX = 32


def norm_rows(values, gain):
    middle = jnp.mean(values, -1, keepdims=True)
    centred = values - middle
    spread = jnp.mean(centred * centred, -1, keepdims=True)
    return centred * lax.rsqrt(spread + 1e-06) * gain


def attend(query, keys, values, valid):
    scores = jnp.einsum(
        "bkgd,btkd->bkgt", query, keys, preferred_element_type=jnp.float32
    ) * query.shape[-1] ** (-0.5)
    scores = jnp.where(valid[:, None, None, :], scores, -1e30)
    highest = jnp.max(scores, -1, keepdims=True)
    weights = jnp.exp(scores - highest)
    probs = (weights / jnp.sum(weights, -1, keepdims=True)).astype(jnp.bfloat16)
    mixed = jnp.einsum("bkgt,btkd->bkgd", probs, values, preferred_element_type=jnp.float32)
    return mixed.astype(jnp.bfloat16)


def shards(
    patches,
    tile_counts,
    ln_gain,
    enc_qkv,
    enc_out_w,
    proj_w,
    cross_kv_w,
    k_gain,
    plan,
    row_pick,
    q_cross,
    q_self,
    cache_kv,
    new_kv,
    kv_len,
):
    replicas = lax.axis_size("replica")
    pipes = lax.axis_size("pipe")
    group = lax.axis_index("replica")
    images, held_tiles, tile_rows, width_part = patches.shape
    head_dim = ENC_W // ENC_HEADS
    enc_rows_count = images * held_tiles * tile_rows
    all_keys = held_tiles * pipes * tile_rows
    gathered = lax.all_gather(patches, "tensor", axis=3, tiled=True)
    whole_rows = gathered.astype(jnp.float32).reshape(enc_rows_count, ENC_W)
    normed = norm_rows(whole_rows, ln_gain).astype(jnp.bfloat16)
    local_heads = enc_qkv.shape[2] // head_dim
    projected = jnp.dot(
        normed, enc_qkv.reshape(ENC_W, -1), preferred_element_type=jnp.float32
    ).astype(jnp.bfloat16)
    projected = projected.reshape(images, held_tiles * tile_rows, 3, local_heads * head_dim)
    queries = projected[:, :, 0].reshape(images, held_tiles * tile_rows, local_heads, head_dim)
    key_part = projected[:, :, 1].reshape(images, held_tiles, tile_rows, local_heads * head_dim)
    value_part = projected[:, :, 2].reshape(images, held_tiles, tile_rows, local_heads * head_dim)
    key_all, value_all = (
        lax.all_gather(key_part, "pipe", axis=1, tiled=True),
        lax.all_gather(value_part, "pipe", axis=1, tiled=True),
    )
    key_all = key_all.reshape(images, all_keys, local_heads, head_dim)
    value_all = value_all.reshape(images, all_keys, local_heads, head_dim)
    counts_local = lax.dynamic_slice_in_dim(tile_counts, group * images, images)
    tile_valid = (jnp.arange(all_keys) // tile_rows)[None, :] < counts_local[:, None]
    scores = jnp.einsum(
        "iqhd,ikhd->ihqk", queries, key_all, preferred_element_type=jnp.float32
    ) * head_dim ** (-0.5)
    scores = jnp.where(tile_valid[:, None, None, :], scores, -1e30)
    highest = jnp.max(scores, -1, keepdims=True)
    weights = jnp.exp(scores - highest)
    probs = (weights / jnp.sum(weights, -1, keepdims=True)).astype(jnp.bfloat16)
    mixed = jnp.einsum("ihqk,ikhd->iqhd", probs, value_all, preferred_element_type=jnp.float32)
    mixed = mixed.astype(jnp.bfloat16).reshape(enc_rows_count, local_heads * head_dim)
    partial_value = jnp.dot(mixed, enc_out_w, preferred_element_type=jnp.float32)
    shard = lax.psum_scatter(
        partial_value.astype(jnp.bfloat16), "tensor", scatter_dimension=1, tiled=True
    ).astype(jnp.float32)
    encoded = (patches.astype(jnp.float32).reshape(enc_rows_count, width_part) + shard).astype(
        jnp.bfloat16
    )
    vision = jnp.dot(
        lax.all_gather(encoded, "tensor", axis=1, tiled=True),
        proj_w,
        preferred_element_type=jnp.float32,
    )
    vision = vision.astype(jnp.bfloat16)
    model_part = vision.shape[1]
    partial_kv = jnp.dot(
        vision, cross_kv_w.reshape(model_part, -1), preferred_element_type=jnp.float32
    )
    partial_kv = partial_kv.reshape(enc_rows_count, 2, -1)
    summed = lax.psum_scatter(
        partial_kv.astype(jnp.bfloat16), "tensor", scatter_dimension=2, tiled=True
    ).astype(jnp.float32)
    kv_width = summed.shape[2]
    kv_local = kv_width // HD
    key_heads = summed[:, 0].reshape(enc_rows_count, kv_local, HD)
    key_heads = (
        key_heads * lax.rsqrt(jnp.mean(key_heads * key_heads, -1, keepdims=True) + 1e-05) * k_gain
    )
    packed = jnp.stack([key_heads.reshape(enc_rows_count, kv_width), summed[:, 1]], 1).astype(
        jnp.bfloat16
    )
    packed = packed.reshape(images, held_tiles, tile_rows, 2, kv_width)
    destination = plan[:, 0]
    grouped = destination.reshape(replicas, images)
    earlier = jnp.arange(images)[:, None] < jnp.arange(images)[None, :]
    same_dest = grouped[:, :, None] == grouped[:, None, :]
    ranks = jnp.sum((same_dest & earlier[None]).astype(jnp.int32), 1)
    my_dest = lax.dynamic_index_in_dim(grouped, group, 0, keepdims=False)
    my_rank = lax.dynamic_index_in_dim(ranks, group, 0, keepdims=False)
    selector = (my_dest[None, None, :] == jnp.arange(replicas)[:, None, None]) & (
        my_rank[None, None, :] == jnp.arange(CAP)[None, :, None]
    )
    outgoing = jnp.einsum(
        "jci,iotxf->jcotxf",
        selector.astype(jnp.bfloat16),
        packed,
        preferred_element_type=jnp.float32,
    ).astype(jnp.bfloat16)
    mine = (destination == group).astype(jnp.int32)
    count = jnp.sum(mine)
    before = jnp.cumsum(mine) - mine
    wanted = row_pick % count
    hit = (mine[None, :] == 1) & (before[None, :] == wanted[:, None])
    chosen = jnp.sum(jnp.where(hit, jnp.arange(replicas * images, dtype=jnp.int32)[None, :], 0), 1)
    source_rows = chosen // images
    slot_rows = jnp.take(ranks.reshape(-1), chosen)
    counts_rows = jnp.take(tile_counts, chosen)
    slot_ids = source_rows * CAP + slot_rows
    rows_here = row_pick.shape[0]
    doubled = jnp.broadcast_to(outgoing[:, None], (replicas, pipes) + outgoing.shape[1:])
    doubled = doubled.reshape((replicas * pipes,) + outgoing.shape[1:])
    arrived = lax.all_to_all(doubled, ("replica", "pipe"), split_axis=0, concat_axis=0, tiled=True)
    arrived = arrived.reshape((replicas, pipes) + outgoing.shape[1:])
    slots_kv = jnp.moveaxis(arrived, 1, 2).reshape(replicas * CAP, all_keys, 2, kv_width)
    group_size = HEADS // KV_HEADS
    block = min(32, rows_here)
    blocks = rows_here // block

    def rows_first(array):
        return array.reshape((blocks, block) + array.shape[1:])

    def steps_first(array):
        shaped = array.reshape((array.shape[0], blocks, block) + array.shape[2:])
        return jnp.moveaxis(shaped, 1, 0)

    def decode_block(pieces):
        ids, counts_block, lengths, cross_q, self_q, cache_block, fresh_all = pieces
        picked = jnp.take(slots_kv, ids, axis=0).reshape(block, all_keys, 2, kv_local, HD)
        valid_cross = (jnp.arange(all_keys) // tile_rows)[None, :] < counts_block[:, None]
        cache_valid = jnp.arange(LMAX)[None, :] < lengths[:, None]
        cross_list = []
        self_list = []
        for step_index in range(STEPS):
            query = cross_q[step_index].reshape(block, kv_local, group_size, HD)
            result = attend(query, picked[:, :, 0], picked[:, :, 1], valid_cross)
            cross_list.append(result.reshape(block, kv_local * group_size * HD))
            fresh = jnp.moveaxis(fresh_all[: step_index + 1], 0, 1)
            joined = jnp.concatenate([cache_block, fresh], 1).reshape(
                block, LMAX + step_index + 1, 2, kv_local, HD
            )
            valid_self = jnp.concatenate([cache_valid, jnp.ones((block, step_index + 1), bool)], 1)
            query = self_q[step_index].reshape(block, kv_local, group_size, HD)
            result = attend(query, joined[:, :, 0], joined[:, :, 1], valid_self)
            self_list.append(result.reshape(block, kv_local * group_size * HD))
        return (jnp.stack(cross_list), jnp.stack(self_list))

    pieces = (
        rows_first(slot_ids),
        rows_first(counts_rows),
        rows_first(kv_len),
        steps_first(q_cross),
        steps_first(q_self),
        rows_first(cache_kv),
        steps_first(new_kv),
    )
    cross_blocks, self_blocks = lax.map(decode_block, pieces)
    out_width = q_cross.shape[2]
    cross_out = jnp.moveaxis(cross_blocks, 0, 1).reshape(STEPS, rows_here, out_width)
    self_out = jnp.moveaxis(self_blocks, 0, 1).reshape(STEPS, rows_here, out_width)
    return (cross_out, self_out)


def solution(mesh):
    in_specs = (
        P("replica", "pipe", None, "tensor"),
        P(),
        P(),
        P(None, None, "tensor"),
        P("tensor", None),
        P(None, "tensor"),
        P("tensor", None, None),
        P(),
        P(),
        P(("replica", "pipe")),
        P(None, ("replica", "pipe"), "tensor"),
        P(None, ("replica", "pipe"), "tensor"),
        P(("replica", "pipe"), None, None, "tensor"),
        P(None, ("replica", "pipe"), None, "tensor"),
        P(("replica", "pipe")),
    )
    out_specs = (P(None, ("replica", "pipe"), "tensor"), P(None, ("replica", "pipe"), "tensor"))
    return jax.shard_map(shards, mesh=mesh, in_specs=in_specs, out_specs=out_specs, check_vma=False)
```

profile of v0, /device:TPU:1, one launch (start us, length us, event | category | flops | bytes accessed | tf_op | source)
XLA Modules:
  0.0 606.4 jit_solution(10880072516003066822)
XLA Ops:
  7.2 3.3 copy.112
  10.8 168.5 %all-gather.3.cloned.1.call-done = bf16[12,2,32,1280]{2,1,0,3:T(2,128)(2,1)} async-done(((bf16[12,2,32,160]{2,1,0,3:T(2,128)(2,1)}), bf16[12,2,32,1280]{2,1,0,3:T(2,128)(2,1)}) %all-gather.3.cloned.1.call-update) | async-done | bytes 1966096 | tf_op jit(solution)/shard_map/all_gather | solution.py:59
  179.2 15.7 %copy.113 = bf16[12,2,32,1280]{3,2,1,0:T(8,128)(2,1)} copy(bf16[12,2,32,1280]{2,1,0,3:T(2,128)(2,1)} %all-gather.3.cloned.1.call-done) | data formatting | bytes 3932160 | tf_op jit(solution)/shard_map/all_gather | solution.py:59
  194.9 2.0 convert_reduce_fusion
  199.0 2.0 convolution_convert_fusion.4
  202.4 2.2 reshape.477
  204.6 7.2 %slice_reduce_fusion = (bf16[12,64,160]{2,1,0:T(8,128)(2,1)}, bf16[12,64,1,160]{3,2,1,0:T(2,128)(2,1)S(1)}, bf16[12,64,1,160]{3,2,1,0:T(2,128)(2,1)}) fusion(bf16[12,64,3,160]{3,2,1,0:T(4,128)(2,1)} %reshape.477), kind=kLoop, calls=%fused_computation.54 | loop fusion | bytes 1474560 | tf_op jit(solution)/shard_map/slice | solution.py:67
  211.9 3.1 all_gather.14
  220.8 2.5 all_gather.13
  223.3 3.1 reshape.478
  226.4 4.6 fusion.14
  232.6 3.0 convolution_convert_fusion
  237.8 85.1 %reduce-scatter.5.cloned.1.call-done = bf16[768,160]{0,1:T(8,128)(2,1)} async-done(((bf16[768,1280]{0,1:T(8,128)(2,1)}), bf16[768,160]{0,1:T(8,128)(2,1)}) %reduce-scatter.5.cloned.1.call-update) | async-done | bytes 245776 | tf_op jit(solution)/shard_map/reduce_scatter | solution.py:88
  325.0 5.6 copy.139
  330.6 6.4 %copy.120 = bf16[2048,1024]{1,0:T(8,128)(2,1)} copy(bf16[2048,1024]{0,1:T(8,128)(2,1)} %bitcast.128) | data formatting | bytes 8388608 | tf_op jit(solution)/shard_map/dot_general | solution.py:101
  337.0 58.8 %all-gather.5.cloned.1.call-done = bf16[768,1280]{0,1:T(8,128)(2,1)} async-done(((bf16[768,160]{0,1:T(8,128)(2,1)}), bf16[768,1280]{0,1:T(8,128)(2,1)}) %all-gather.5.cloned.1.call-update) | async-done | bytes 1966096 | tf_op jit(solution)/shard_map/all_gather | solution.py:95
  395.7 9.3 %convolution_convert_fusion.1 = bf16[768,2,1024]{2,0,1:T(8,128)(2,1)} fusion(bf16[2,1024,1024]{2,1,0:T(8,128)(2,1)} %bitcast.135, bf16[768,1280]{0,1:T(8,128)(2,1)} %all-gather.5.cloned.1.call-done, bf16[1280,1024]{1,0:T(8,128)(2,1)S(1)} %copy-done), kind=kOutput, calls=%fused_computation.16 | convolution fusion | flops 5236850688 | bytes 11927552 | tf_op jit(solution)/shard_map/dot_general | solution.py:101
  405.1 8.7 %copy.132 = bf16[768,2,1024]{0,1,2:T(2,128)(2,1)} copy(bf16[768,2,1024]{2,0,1:T(8,128)(2,1)} %convolution_convert_fusion.1) | data formatting | bytes 6291456
  413.8 4.2 copy.140
  421.8 101.9 %reduce-scatter.7.cloned.1.call-done = bf16[128,1536]{1,0:T(8,128)(2,1)} async-done(((bf16[1024,1536]{1,0:T(8,128)(2,1)}), bf16[128,1536]{1,0:T(8,128)(2,1)}) %reduce-scatter.7.cloned.1.call-update) | async-done | bytes 393232
  529.5 7.0 %all-to-all-start = ((bf16[32,2,2,32,2,128]{5,3,4,2,1,0:T(8,128)(2,1)}), bf16[32,2,2,32,2,128]{5,3,4,2,1,0:T(8,128)(2,1)S(1)}, u32[]{:S(2)}, u32[]{:S(2)}) async-start(bf16[32,2,2,32,2,128]{5,3,4,2,1,0:T(8,128)(2,1)} %bitcast.132), calls=%async_computation.1 | async-start | bytes 4194304 | tf_op jit(solution)/shard_map/all_to_all | solution.py:147
  541.9 2.1 convolution_convert_fusion.7
  546.8 39.4 %all-to-all-done = bf16[32,2,2,32,2,128]{5,3,4,2,1,0:T(8,128)(2,1)S(1)} async-done(((bf16[32,2,2,32,2,128]{5,3,4,2,1,0:T(8,128)(2,1)}), bf16[32,2,2,32,2,128]{5,3,4,2,1,0:T(8,128)(2,1)S(1)}, u32[]{:S(2)}, u32[]{:S(2)}) %all-to-all-start) | async-done | bytes 2097184 | tf_op jit(solution)/shard_map/all_to_all | solution.py:147
  588.3 2.5 gather_fusion
  (137 shorter events, 42.7 us)
Async XLA Ops:
  7.2 388.6 %copy-start = (bf16[1280,1024]{1,0:T(8,128)(2,1)S(1)}, bf16[1280,1024]{1,0:T(8,128)(2,1)}, u32[]{:S(2)}) copy-start(bf16[1280,1024]{1,0:T(8,128)(2,1)} %param.22) | copy-start | bytes 7864324
  7.2 3.4 copy-start.2
  7.2 172.0 %all-gather.3.cloned.1.call-start = ((), (), s32[]{:S(2)}) async-start(), calls=%async_computation.3 | async-start | bytes 8847360 | tf_op jit(solution)/shard_map/all_gather | solution.py:59
  10.5 312.4 %reduce-scatter.5.cloned.1.call-start = ((), (), s32[]{:S(2)}) async-start(), calls=%async_computation.4 | async-start | bytes 2211840 | tf_op jit(solution)/shard_map/reduce_scatter | solution.py:88
  194.9 2.1 copy-start.3
  194.9 2.8 copy-start.11
  197.7 1.3 copy-start.16
  218.2 2.5 copy-start.4
  235.6 160.1 %all-gather.5.cloned.1.call-start = ((), (), s32[]{:S(2)}) async-start(), calls=%async_computation.5 | async-start | bytes 2211840 | tf_op jit(solution)/shard_map/all_gather | solution.py:95
  324.7 198.9 %reduce-scatter.7.cloned.1.call-start = ((), (), s32[]{:S(2)}) async-start(), calls=%async_computation.6 | async-start | bytes 3538944
  417.9 0.7 copy-start.12
  417.9 3.6 copy-start.15
  418.0 3.7 copy-start.14
  418.0 107.9 %copy-start.13 = (f32[128]{0:T(128)S(1)}, f32[128]{0:T(128)}, u32[]{:S(2)}) copy-start(f32[128]{0:T(128)} %param.24) | copy-start | bytes 1540
  529.5 7.1 %copy-start.9 = (bf16[2,32,2,128]{3,2,1,0:T(2,128)(2,1)S(1)}, bf16[2,32,2,128]{3,2,1,0:T(2,128)(2,1)}, u32[]{:S(2)}) copy-start(bf16[2,32,2,128]{3,2,1,0:T(2,128)(2,1)} %param.30) | copy-start | bytes 98308
  529.5 9.4 %copy-start.8 = (bf16[2,32,1024]{2,1,0:T(8,128)(2,1)S(1)}, bf16[2,32,1024]{2,1,0:T(8,128)(2,1)}, u32[]{:S(2)}) copy-start(bf16[2,32,1024]{2,1,0:T(8,128)(2,1)} %param.27) | copy-start | bytes 393220
  529.5 10.1 %copy-start.6 = (bf16[32,32,2,128]{3,2,1,0:T(2,128)(2,1)S(1)}, bf16[32,32,2,128]{3,2,1,0:T(2,128)(2,1)}, u32[]{:S(2)}) copy-start(bf16[32,32,2,128]{3,2,1,0:T(2,128)(2,1)} %param.29) | copy-start | bytes 1572868
  529.5 56.7 %all-to-all-start = ((bf16[32,2,2,32,2,128]{5,3,4,2,1,0:T(8,128)(2,1)}), bf16[32,2,2,32,2,128]{5,3,4,2,1,0:T(8,128)(2,1)S(1)}, u32[]{:S(2)}, u32[]{:S(2)}) async-start(bf16[32,2,2,32,2,128]{5,3,4,2,1,0:T(8,128)(2,1)} %bitcast.132), calls=%async_computation.1 | async-start | bytes 4194304 | tf_op jit(solution)/shard_map/all_to_all | solution.py:147
  536.5 3.2 slice-start
  541.0 0.7 copy-start.7
  590.8 1.6 copy-start.10
  591.1 1.4 copy-start.5
  593.3 6.6 %copy-start.1 = (bf16[1280,1024]{1,0:T(8,128)(2,1)S(1)}, bf16[1280,1024]{1,0:T(8,128)(2,1)}, u32[]{:S(2)}) copy-start(bf16[1280,1024]{1,0:T(8,128)(2,1)} %param.22) | copy-start | bytes 7864324
Sparse Core Ops, SparseCore 0:
  10.6 168.5 all-gather.2
  235.8 87.0 reduce-scatter.4
  325.5 70.1 all-gather.4
  418.1 105.5 reduce-scatter.6
where the time goes:
time: 608 us; the launch traced here: 606 us
  waiting for transfers between devices  454 us (75%)
  local copies, waits for them, and re-layouts  81.4 us (13%)
  matrix products  30.7 us (5%)
  between operations  15.6 us (3%)
  other arithmetic  12.1 us (2%)
  starting transfers between devices  7.3 us (1%)
    all_gather x1, waiting for transfers between devices, shards(): gathered = lax.all_gather(patches, 'tensor', axis=3, tiled=True)  168 us
    unnamed x5, waiting for transfers between devices  102 us
    reduce_scatter x1, waiting for transfers between devices, shards(): lax.psum_scatter(partial_value.astype(jnp.bfloat16), 'tensor', scatter_di...  85.1 us
    all_gather x1, waiting for transfers between devices, shards(): lax.all_gather(encoded, 'tensor', axis=1, tiled=True)  58.8 us
    all_to_all x1, waiting for transfers between devices, shards(): lax.all_to_all(doubled, ('replica', 'pipe'), split_axis=0, concat_axis=0,...  39.4 us
    unnamed x53, local copies, waits for them, and re-layouts  28.9 us
    all_gather x1, local copies, waits for them, and re-layouts, shards(): gathered = lax.all_gather(patches, 'tensor', axis=3, tiled=True)  15.7 us
  transfers between devices with their start and end apart: 5, of which 5 were waited for; matrix products, arithmetic and copies ran while one was open for 4% of the time, Pallas kernels for 0%

commit v1 on v0

v1 whole, which is shorter than its diff:
```python
import functools

import jax
import jax.numpy as jnp
from jax import lax
from jax.experimental import pallas as pl
from jax.experimental.pallas import tpu as pltpu
from jax.sharding import PartitionSpec as P

HEADS = 64
KV_HEADS = 8
HD = 128
ENC_W = 1280
ENC_HEADS = 16
CAP = 2
STEPS = 2
LMAX = 32
TT = 32
LIMIT = 48 * 1024 * 1024
BF = jnp.bfloat16
F32 = jnp.float32

VMEM = pl.BlockSpec(memory_space=pltpu.VMEM)
SMEM = pl.BlockSpec(memory_space=pltpu.SMEM)
ANY = pl.BlockSpec(memory_space=pl.ANY)


def call(kernel, outs, in_specs, scratch, flops, moved, name):
    return pl.pallas_call(
        kernel,
        out_shape=outs,
        in_specs=in_specs,
        out_specs=jax.tree.map(lambda _: VMEM, outs),
        scratch_shapes=scratch,
        compiler_params=pltpu.CompilerParams(vmem_limit_bytes=LIMIT),
        cost_estimate=pl.CostEstimate(flops=flops, bytes_accessed=moved, transcendentals=0),
        name=name,
    )


def shape_of(shape, dtype):
    return jax.ShapeDtypeStruct(shape, dtype)


def dot(a, b, dims):
    return lax.dot_general(a, b, (dims, ((), ())), preferred_element_type=F32)


def turn_kernel(x_ref, out_ref):
    width = x_ref.shape[1]
    row = lax.broadcasted_iota(jnp.int32, (width, width), 0)
    col = lax.broadcasted_iota(jnp.int32, (width, width), 1)
    eye = jnp.where(row == col, 1.0, 0.0).astype(BF)
    out_ref[...] = dot(eye, x_ref[...], ((1,), (1,))).astype(BF)


def qkv_kernel(off_ref, *refs):
    shards = refs[:8]
    w_ref, gain_ref, q_ref, kv_ref, normed = refs[8:]
    part = shards[0].shape[0]
    width = part * 8
    total = jnp.zeros((1, shards[0].shape[1]), F32)
    for s in shards:
        total += jnp.sum(s[...].astype(F32), 0, keepdims=True)
    mean = total / width
    total = jnp.zeros_like(mean)
    for s in shards:
        c = s[...].astype(F32) - mean
        total += jnp.sum(c * c, 0, keepdims=True)
    scale = lax.rsqrt(total / width + 1e-06)
    for i, s in enumerate(shards):
        at = pl.ds(pl.multiple_of(off_ref[i] * part, 16), part)
        c = s[...].astype(F32) - mean
        normed[at, :] = (c * scale * gain_ref[at, :]).astype(BF)
    out = jnp.dot(w_ref[...], normed[...], preferred_element_type=F32).astype(BF)
    q_ref[...] = out[:part]
    kv_ref[...] = out[part:]


def attend_kernel(count_ref, pipe_ref, q_ref, own_ref, other_ref, out_ref):
    part, rows = q_ref.shape
    heads = 2
    hd = part // heads
    pipe = pipe_ref[0]
    key = lax.broadcasted_iota(jnp.int32, (256, 1), 0)
    from_other = key // 128
    key_image = (key % 128) // 64
    tile = 2 * jnp.where(from_other == 1, 1 - pipe, pipe) + (key % 64) // TT
    lane_image = lax.broadcasted_iota(jnp.int32, (1, 128), 1) // 64
    for j in range(rows // 128):
        lanes = slice(j * 128, (j + 1) * 128)
        count = jnp.where(lane_image == 0, count_ref[2 * j], count_ref[2 * j + 1])
        valid = (key_image == lane_image) & (tile < count)
        for h in range(heads):
            k_at = slice(h * hd, (h + 1) * hd)
            v_at = slice(part + h * hd, part + (h + 1) * hd)
            keys = jnp.concatenate([own_ref[k_at, lanes], other_ref[k_at, lanes]], 1)
            values = jnp.concatenate([own_ref[v_at, lanes], other_ref[v_at, lanes]], 1)
            scores = dot(keys, q_ref[k_at, lanes], ((0,), (0,))) * hd ** (-0.5)
            scores = jnp.where(valid, scores, -1e30)
            weights = jnp.exp(scores - jnp.max(scores, 0, keepdims=True))
            probs = (weights / jnp.sum(weights, 0, keepdims=True)).astype(BF)
            out_ref[k_at, lanes] = jnp.dot(values, probs, preferred_element_type=F32).astype(BF)


def fill(off_ref, shards, full, sems):
    part = shards[0].shape[0]
    copies = []
    for i, s in enumerate(shards):
        at = pl.ds(pl.multiple_of(off_ref[i] * part, 16), part)
        copies.append(pltpu.make_async_copy(s, full.at[at, :], sems.at[i]))
    for c in copies:
        c.start()
    for c in copies:
        c.wait()


def own_term_kernel(off_ref, *refs):
    shards = refs[:8]
    w_ref, out_ref, full, sems = refs[8:]
    fill(off_ref, shards, full, sems)
    out_ref[...] = jnp.dot(w_ref[...], full[...], preferred_element_type=F32)


def memory_kernel(off_ref, pick_ref, *refs):
    shards = refs[:8]
    w_ref, own_ref, gain_ref, out_ref, full, rows_ref, sems = refs[8:]
    fill(off_ref, shards, full, sems)
    kv = jnp.dot(w_ref[...], full[...], preferred_element_type=F32) + own_ref[...]
    keys = kv[:HD]
    keys = keys * lax.rsqrt(jnp.mean(keys * keys, 0, keepdims=True) + 1e-05) * gain_ref[...]
    rows_ref[:, :HD] = jnp.transpose(keys).astype(BF)
    rows_ref[:, HD:] = jnp.transpose(kv[HD:]).astype(BF)
    for i in range(out_ref.shape[0] // 64):
        at = pl.ds(pl.multiple_of(pick_ref[i] * 64, 64), 64)
        out_ref[i * 64 : (i + 1) * 64, :] = rows_ref[at, :]


def finish(score_ref, mixed_ref, valid, out_ref):
    rows = out_ref.shape[1]
    scores = jnp.where(valid, score_ref[...] * HD ** (-0.5), -1e30)
    weights = jnp.exp(scores - jnp.max(scores, 1, keepdims=True))
    return (weights / jnp.sum(weights, 1, keepdims=True)).astype(BF)


def spread(mixed_ref, out_ref):
    group = out_ref.shape[2] // HD
    for s in range(STEPS):
        for h in range(group):
            out_ref[s, :, h * HD : (h + 1) * HD] = mixed_ref[:, s * group + h, :].astype(BF)


def cross_kernel(slot_ref, pipe_ref, count_ref, q_ref, own_ref, other_ref, out_ref, score_ref, prob_ref, mixed_ref):
    rows, per = q_ref.shape[0], q_ref.shape[1]
    pipe = pipe_ref[0]
    for b in range(rows):
        at = pl.ds(pl.multiple_of(slot_ref[b] * 64, 64), 64)
        keys = jnp.concatenate([own_ref[at, :HD], other_ref[at, :HD]], 0)
        score_ref[b * per : (b + 1) * per, :] = dot(q_ref[b], keys, ((1,), (1,)))
    lane = lax.broadcasted_iota(jnp.int32, (1, 128), 1)
    tile = 2 * jnp.where(lane >= 64, 1 - pipe, pipe) + (lane % 64) // TT
    prob_ref[...] = finish(score_ref, mixed_ref, tile < count_ref[...], out_ref)
    for b in range(rows):
        at = pl.ds(pl.multiple_of(slot_ref[b] * 64, 64), 64)
        values = jnp.concatenate([own_ref[at, HD:], other_ref[at, HD:]], 0)
        mixed_ref[b] = jnp.dot(
            prob_ref[b * per : (b + 1) * per, :], values, preferred_element_type=F32
        )
    spread(mixed_ref, out_ref)


def self_kernel(len_ref, q_ref, kv_ref, out_ref, score_ref, prob_ref, mixed_ref):
    rows, per = q_ref.shape[0], q_ref.shape[1]
    for b in range(rows):
        score_ref[b * per : (b + 1) * per, :] = dot(q_ref[b], kv_ref[b, :, :HD], ((1,), (1,)))
    spots = kv_ref.shape[1]
    lane = lax.broadcasted_iota(jnp.int32, (1, spots), 1)
    step = (lax.broadcasted_iota(jnp.int32, (rows * per, 1), 0) % per) // (per // STEPS)
    valid = (lane < len_ref[...]) | ((lane >= LMAX) & (lane <= LMAX + step))
    prob_ref[...] = finish(score_ref, mixed_ref, valid, out_ref)
    for b in range(rows):
        mixed_ref[b] = jnp.dot(
            prob_ref[b * per : (b + 1) * per, :], kv_ref[b, :, HD:], preferred_element_type=F32
        )
    spread(mixed_ref, out_ref)


ZX = [(t, t ^ 1) for t in range(8)]


def y_perm(d):
    return [(t, (t + 2 * d) % 8) for t in range(8)]


def gather8(s):
    p1, p2, p3 = y_perm(1), y_perm(2), y_perm(3)
    z = lax.ppermute(s, "tensor", ZX)
    a, b, c = (lax.ppermute(s, "tensor", p) for p in (p1, p3, p2))
    za, zb, zc = (lax.ppermute(z, "tensor", p) for p in (p1, p3, p2))
    return (s, z, a, b, c, za, zb, zc)


def gather_order(t):
    a, b, c = (t + 6) % 8, (t + 2) % 8, (t + 4) % 8
    return jnp.stack([t, t ^ 1, a, b, c, a ^ 1, b ^ 1, c ^ 1]).astype(jnp.int32)


def fold_weights(enc_out_w, proj_w, cross_kv_w, u, tensor):
    y, zh = tensor // 2, tensor % 2
    per = ENC_W // 32
    few = per // 8
    mine = lax.dynamic_slice_in_dim(enc_out_w, u * few, few)
    other = lax.ppermute(mine, "tensor", ZX)
    pair = jnp.where(zh == 0, jnp.stack([mine, other]), jnp.stack([other, mine]))
    rel = jnp.stack([pair] + [lax.ppermute(pair, "tensor", y_perm(d)) for d in (1, 2, 3)])
    whole = jnp.take(rel, (y - jnp.arange(4)) % 4, axis=0).reshape(per, ENC_W)
    folded = jnp.dot(whole, proj_w, preferred_element_type=F32).astype(BF)
    left = jnp.concatenate([lax.dynamic_slice_in_dim(proj_w, u * per, per), folded], 0)
    part = jnp.einsum(
        "rk,kcn->crn", left, cross_kv_w, preferred_element_type=F32
    ).astype(BF)
    part = part.reshape(2, 2 * per, 4, 2, HD).transpose(3, 2, 1, 0, 4).reshape(2, 4, 2 * per, 2 * HD)
    keep = lax.dynamic_index_in_dim(part, zh, 0, keepdims=False)
    send = lax.dynamic_index_in_dim(part, 1 - zh, 0, keepdims=False)
    half = keep.astype(F32) + lax.ppermute(send, "tensor", ZX).astype(F32)
    total = lax.dynamic_index_in_dim(half, y, 0, keepdims=False)
    half = half.astype(BF)
    for d in (1, 2, 3):
        block = lax.dynamic_index_in_dim(half, (y + d) % 4, 0, keepdims=False)
        total = total + lax.ppermute(block, "tensor", y_perm(d)).astype(F32)
    return total.astype(BF)


def spread_weights(piece, replica, pipe):
    x, zl = replica // 4, replica % 4
    zs = [piece] + [
        lax.ppermute(piece, "replica", [(r, r // 4 * 4 + (r + d) % 4) for r in range(16)])
        for d in (1, 2, 3)
    ]
    line = jnp.take(jnp.stack(zs), (zl - jnp.arange(4)) % 4, axis=0)
    xs = [line] + [
        lax.ppermute(line, "replica", [(r, (r + 4 * d) % 16) for r in range(16)])
        for d in (1, 2, 3)
    ]
    plane = jnp.take(jnp.stack(xs), (x - jnp.arange(4)) % 4, axis=0)
    other = lax.ppermute(plane, "pipe", [(0, 1), (1, 0)])
    both = jnp.where(pipe == 0, jnp.stack([plane, other], 2), jnp.stack([other, plane], 2))
    per = piece.shape[0] // 2
    both = both.reshape(32, 2, per, 2 * HD)
    first = both[:, 0].reshape(ENC_W, 2 * HD)
    second = both[:, 1].reshape(32, 8, per // 8, 2 * HD).transpose(1, 0, 2, 3).reshape(ENC_W, 2 * HD)
    return first.T, second.T


def shards(
    patches,
    tile_counts,
    ln_gain,
    enc_qkv,
    enc_out_w,
    proj_w,
    cross_kv_w,
    k_gain,
    plan,
    row_pick,
    q_cross,
    q_self,
    cache_kv,
    new_kv,
    kv_len,
):
    replicas = 16
    group = lax.axis_index("replica")
    pipe = lax.axis_index("pipe")
    tensor = lax.axis_index("tensor")
    images, held, tile_rows, part = patches.shape
    rows = images * held * tile_rows
    order = gather_order(tensor)
    pipe_at = pipe.reshape(1).astype(jnp.int32)

    turned = call(
        turn_kernel, shape_of((part, rows), BF), [VMEM], [], 2 * rows * part * part, 4 * rows * part, "turn"
    )(patches.reshape(rows, part))
    xs = gather8(turned)

    u = group * 2 + pipe
    piece = fold_weights(enc_out_w, proj_w, cross_kv_w, u, tensor)
    w_own, w_mixed = spread_weights(piece, group, pipe)

    rows_here = row_pick.shape[0]
    steps_heads = q_self.shape[0] * q_self.shape[2] // HD

    def heads_of(q):
        return q.reshape(STEPS, rows_here, -1, HD).transpose(1, 0, 2, 3).reshape(rows_here, steps_heads, HD)

    spots = 48
    joined = jnp.concatenate(
        [
            cache_kv.reshape(rows_here, LMAX, 2 * HD),
            jnp.moveaxis(new_kv, 0, 1).reshape(rows_here, STEPS, 2 * HD),
            jnp.zeros((rows_here, spots - LMAX - STEPS, 2 * HD), BF),
        ],
        1,
    )

    def per_head(values):
        return jnp.repeat(values.astype(jnp.int32), steps_heads).reshape(rows_here * steps_heads, 1)

    def scratch(n):
        return [
            pltpu.VMEM((rows_here * steps_heads, n), F32),
            pltpu.VMEM((rows_here * steps_heads, n), BF),
            pltpu.VMEM((rows_here, steps_heads, HD), F32),
        ]

    self_out = call(
        self_kernel,
        shape_of(q_self.shape, BF),
        [VMEM] * 3,
        scratch(spots),
        4 * rows_here * 16 * 128 * 128,
        4 * 1024 * 1024,
        "self_attend",
    )(per_head(kv_len), heads_of(q_self), joined)

    turned_w = enc_qkv.transpose(1, 2, 0).reshape(3 * part, ENC_W)
    q, kv = call(
        qkv_kernel,
        (shape_of((part, rows), BF), shape_of((2 * part, rows), BF)),
        [SMEM] + [VMEM] * 10,
        [pltpu.VMEM((ENC_W, rows), BF)],
        2 * rows * ENC_W * 3 * part,
        6 * 1024 * 1024,
        "qkv",
    )(order, *xs, turned_w, ln_gain.reshape(ENC_W, 1))
    kv_other = lax.ppermute(kv, "pipe", [(0, 1), (1, 0)])
    counts_local = lax.dynamic_slice_in_dim(tile_counts, group * images, images)
    mixed = call(
        attend_kernel,
        shape_of((part, rows), BF),
        [SMEM, SMEM, VMEM, VMEM, VMEM],
        [],
        4 * rows * 256 * part,
        2 * 1024 * 1024,
        "encoder_attend",
    )(counts_local, pipe_at, q, kv, kv_other)

    own_term = call(
        own_term_kernel,
        shape_of((2 * HD, rows), F32),
        [SMEM] + [ANY] * 8 + [VMEM],
        [pltpu.VMEM((ENC_W, rows), BF), pltpu.SemaphoreType.DMA((8,))],
        2 * rows * ENC_W * 2 * HD,
        4 * 1024 * 1024,
        "own_term",
    )(order, *xs, w_own)

    ms = gather8(mixed)

    destination = plan[:, 0]
    grouped = destination.reshape(replicas, images)
    earlier = jnp.arange(images)[:, None] < jnp.arange(images)[None, :]
    same_dest = grouped[:, :, None] == grouped[:, None, :]
    ranks = jnp.sum((same_dest & earlier[None]).astype(jnp.int32), 1)
    my_dest = lax.dynamic_index_in_dim(grouped, group, 0, keepdims=False)
    my_rank = lax.dynamic_index_in_dim(ranks, group, 0, keepdims=False)
    spot = my_dest * CAP + my_rank
    picks = jnp.sum(
        jnp.where(
            spot[None, :] == jnp.arange(replicas * CAP)[:, None],
            jnp.arange(images, dtype=jnp.int32)[None, :],
            0,
        ),
        1,
    ).astype(jnp.int32)
    mine = (destination == group).astype(jnp.int32)
    count = jnp.sum(mine)
    before = jnp.cumsum(mine) - mine
    wanted = row_pick % count
    hit = (mine[None, :] == 1) & (before[None, :] == wanted[:, None])
    every = jnp.arange(replicas * images, dtype=jnp.int32)
    slot_of = (every // images) * CAP + ranks.reshape(-1)
    slot_ids = jnp.sum(jnp.where(hit, slot_of[None, :], 0), 1).astype(jnp.int32)
    counts_rows = jnp.sum(jnp.where(hit, tile_counts[None, :], 0), 1).astype(jnp.int32)

    slots = call(
        memory_kernel,
        shape_of((replicas * CAP * held * tile_rows, 2 * HD), BF),
        [SMEM, SMEM] + [ANY] * 8 + [VMEM] * 3,
        [
            pltpu.VMEM((ENC_W, rows), BF),
            pltpu.VMEM((rows, 2 * HD), BF),
            pltpu.SemaphoreType.DMA((8,)),
        ],
        2 * rows * ENC_W * 2 * HD,
        4 * 1024 * 1024,
        "memory",
    )(order, picks, *ms, w_mixed, own_term, k_gain.reshape(HD, 1))
    arrived = lax.all_to_all(slots, "replica", split_axis=0, concat_axis=0, tiled=True)
    arrived_other = lax.ppermute(arrived, "pipe", [(0, 1), (1, 0)])

    cross_out = call(
        cross_kernel,
        shape_of(q_cross.shape, BF),
        [SMEM, SMEM] + [VMEM] * 4,
        scratch(128),
        4 * rows_here * 16 * 128 * 128,
        4 * 1024 * 1024,
        "cross_attend",
    )(slot_ids, pipe_at, per_head(counts_rows), heads_of(q_cross), arrived, arrived_other)
    return (cross_out, self_out)


def solution(mesh):
    in_specs = (
        P("replica", "pipe", None, "tensor"),
        P(),
        P(),
        P(None, None, "tensor"),
        P("tensor", None),
        P(None, "tensor"),
        P("tensor", None, None),
        P(),
        P(),
        P(("replica", "pipe")),
        P(None, ("replica", "pipe"), "tensor"),
        P(None, ("replica", "pipe"), "tensor"),
        P(("replica", "pipe"), None, None, "tensor"),
        P(None, ("replica", "pipe"), None, "tensor"),
        P(("replica", "pipe")),
    )
    out_specs = (P(None, ("replica", "pipe"), "tensor"), P(None, ("replica", "pipe"), "tensor"))
    return jax.shard_map(shards, mesh=mesh, in_specs=in_specs, out_specs=out_specs, check_vma=False)
```

time: 608 us -> 186 us (0.31)
  waiting for transfers between devices: 454 us -> 45 us
  starting transfers between devices: 7.3 us -> 71 us
  local copies, waits for them, and re-layouts: 81.4 us -> 28.8 us
  matrix products: 30.7 us -> 4.21 us
  Pallas kernels: 0 us -> 21.6 us
  between operations: 15.6 us -> 2.51 us
    all_gather x2 -> x0, waiting for transfers between devices: 227 us -> none  [the longest x1 168 us: shards(): gathered = lax.all_gather(patches, 'tensor', axis=3, tiled=True)]
    unnamed x5 -> x0, waiting for transfers between devices: 102 us -> none
    reduce_scatter x1 -> x0, waiting for transfers between devices: 85.1 us -> none  [shards(): lax.psum_scatter(partial_value.astype(jnp.bfloat16), 'tensor', scatter_di...]
    ppermute x0 -> x31, starting transfers between devices: none -> 66.2 us  [the longest x2 12.4 us: gather8(): z = lax.ppermute(s, 'tensor', ZX)]
    dot_general x14 -> x2, matrix products: 30.7 us -> 4.21 us  [the longest x1 3.61 us: fold_weights(): jnp.einsum('rk,kcn->crn', left, cross_kv_w, preferred_element_type=F32)]
    pallas_call x0 -> x7, Pallas kernels: none -> 21.6 us  [the longest x1 5.3 us: shards(): call(qkv_kernel, (shape_of((part, rows), BF), shape_of((2 * part, rows),...]
    ppermute x0 -> x31, waiting for transfers between devices: none -> 20.4 us  [the longest x6 4.69 us: gather8(): za, zb, zc = (lax.ppermute(z, 'tensor', p) for p in (p1, p3, p2))]
    unnamed x53 -> x47, local copies, waits for them, and re-layouts: 28.9 us -> 8.57 us
  transfers between devices with their start and end apart: 5 -> 32, of which waited for: 5 -> 15; matrix products, arithmetic and copies ran while one was open for 4% -> 20% of each run, Pallas kernels for 0% -> 5%
where the time goes in v1:
time: 186 us; the launch traced here: 184 us
  starting transfers between devices  71 us (38%)
  waiting for transfers between devices  45 us (24%)
  local copies, waits for them, and re-layouts  28.8 us (15%)
  Pallas kernels  21.6 us (12%)
  other arithmetic  11 us (6%)
  matrix products  4.21 us (2%)
  between operations  2.51 us (1%)
    all_to_all x1, waiting for transfers between devices, shards(): lax.all_to_all(slots, 'replica', split_axis=0, concat_axis=0, tiled=True)  24.6 us
    ppermute x2, starting transfers between devices, gather8(): z = lax.ppermute(s, 'tensor', ZX)  12.4 us
    ppermute x1, starting transfers between devices, shards(): kv_other = lax.ppermute(kv, 'pipe', [(0, 1), (1, 0)])  9.07 us
    unnamed x47, local copies, waits for them, and re-layouts  8.57 us
    ppermute x3, starting transfers between devices, spread_weights(): lax.ppermute(piece, 'replica', [(r, r // 4 * 4 + (r + d) % 4) for r in ra...  8.42 us
    ppermute x6, starting transfers between devices, gather8(): a, b, c = (lax.ppermute(s, 'tensor', p) for p in (p1, p3, p2))  8.23 us
    ppermute x6, starting transfers between devices, gather8(): za, zb, zc = (lax.ppermute(z, 'tensor', p) for p in (p1, p3, p2))  7.33 us
    pallas_call x1, Pallas kernels, shards(): call(qkv_kernel, (shape_of((part, rows), BF), shape_of((2 * part, rows),...  5.3 us
  transfers between devices with their start and end apart: 32, of which 15 were waited for; matrix products, arithmetic and copies ran while one was open for 20% of the time, Pallas kernels for 5%

profile of v1, /device:TPU:1, one launch (start us, length us, event | category | flops | bytes accessed | tf_op | source)
XLA Modules:
  0.0 184.1 jit_solution(1069798836664802848)
XLA Ops:
  2.1 7.8 %collective-permute-start = (bf16[160,768]{1,0:T(8,128)(2,1)S(1)}, bf16[160,768]{1,0:T(8,128)(2,1)}, u32[]{:S(2)}, u32[]{:S(2)}) collective-permute-start(bf16[160,768]{1,0:T(8,128)(2,1)S(1)} %turn.1.refs_0_), channel_id=1, source_target_pairs={{0,1},{1,0},{2,3},{3,2},{4,5},{5,4},{6,7},{7,6},{8,9},{9,8},{10,11... | collective-permute-start | bytes 737288 | tf_op jit(solution)/shard_map/ppermute | solution.py:197
  14.6 4.1 %collective-permute-done.15 = bf16[5,1280]{1,0:T(8,128)(2,1)S(1)} collective-permute-done((bf16[5,1280]{1,0:T(8,128)(2,1)S(1)}, bf16[5,1280]{1,0:T(8,128)(2,1)S(1)}, u32[]{:S(2)}, u32[]{:S(2)}) %collective-permute-start.15) | collective-permute-done | bytes 12832 | tf_op jit(solution)/shard_map/ppermute | solution.py:213
  26.2 3.6 %fusion.5 = bf16[2,80,1024]{2,1,0:T(8,128)(2,1)S(1)} fusion(bf16[1024,2,1024]{2,1,0:T(2,128)(2,1)} %param.21, bf16[40,1024]{1,0:T(8,128)(2,1)S(1)} %convolution_convert_fusion, bf16[40,1024]{1,0:T(8,128)(2,1)S(1)} %copy-done.14), kind=kOutput, calls=%fused_computation.7 | convolution fusion | flops 336035840 | bytes 4685824 | tf_op jit(solution)/shard_map/rk,kcn->crn/dot_general | solution.py:219
  30.6 4.6 %collective-permute-start.19 = (bf16[4,80,256]{2,1,0:T(8,128)(2,1)S(1)}, bf16[4,80,256]{2,1,0:T(8,128)(2,1)}, u32[]{:S(2)}, u32[]{:S(2)}) collective-permute-start(bf16[4,80,256]{2,1,0:T(8,128)(2,1)S(1)} %dynamic-slice_bitcast_fusion), channel_id=1, source_target_pairs={{0,1},{1,0},{2,3},{3,2},{4,5},{5,4},{6,7},{7,6},{8,9},{9,8},{10,11... | collective-permute-start | bytes 491528 | tf_op jit(solution)/shard_map/ppermute | solution.py:225
  40.8 3.3 %collective-permute-start.21 = (bf16[80,256]{1,0:T(8,128)(2,1)S(1)}, bf16[80,256]{1,0:T(8,128)(2,1)S(1)}, u32[]{:S(2)}, u32[]{:S(2)}) collective-permute-start(bf16[80,256]{1,0:T(8,128)(2,1)S(1)} %get-tuple-element.16), channel_id=1, source_target_pairs={{0,4},{1,5},{2,6},{3,7},{4,0},{5,1},{6,2},{7,3},{8,12},{9,13},{10,... | collective-permute-start | bytes 122888 | tf_op jit(solution)/shard_map/ppermute | solution.py:230
  47.0 6.2 %collective-permute-start.23 = (bf16[80,256]{1,0:T(8,128)(2,1)S(1)}, bf16[80,256]{1,0:T(8,128)(2,1)S(1)}, u32[]{:S(2)}, u32[]{:S(2)}) collective-permute-start(bf16[80,256]{1,0:T(8,128)(2,1)S(1)} %fusion.14), channel_id=1, source_target_pairs={{0,16},{16,32},{32,48},{48,0},{64,80},{80,96},{96,112},{112,64},{1... | collective-permute-start | bytes 122888 | tf_op jit(solution)/shard_map/ppermute | solution.py:237
  53.2 2.2 %collective-permute-start.25 = (bf16[80,256]{1,0:T(8,128)(2,1)S(1)}, bf16[80,256]{1,0:T(8,128)(2,1)S(1)}, u32[]{:S(2)}, u32[]{:S(2)}) collective-permute-start(bf16[80,256]{1,0:T(8,128)(2,1)S(1)} %fusion.14), channel_id=1, source_target_pairs={{0,48},{16,0},{32,16},{48,32},{64,112},{80,64},{96,80},{112,96},{1... | collective-permute-start | bytes 122888 | tf_op jit(solution)/shard_map/ppermute | solution.py:237
  59.8 2.5 %collective-permute-start.27 = (bf16[4,80,256]{2,1,0:T(8,128)(2,1)}, bf16[4,80,256]{2,1,0:T(8,128)(2,1)}, u32[]{:S(2)}, u32[]{:S(2)}) collective-permute-start(bf16[4,80,256]{2,1,0:T(8,128)(2,1)} %broadcast_select_fusion.1), channel_id=1, source_target_pairs={{0,128},{16,144},{32,160},{48,176},{64,192},{80,208},{96,224},{112... | collective-permute-start | bytes 491528 | tf_op jit(solution)/shard_map/ppermute | solution.py:242
  63.8 2.5 %collective-permute-start.2 = (bf16[160,768]{1,0:T(8,128)(2,1)S(1)}, bf16[160,768]{1,0:T(8,128)(2,1)}, u32[]{:S(2)}, u32[]{:S(2)}) collective-permute-start(bf16[160,768]{1,0:T(8,128)(2,1)S(1)} %turn.1.refs_0_), channel_id=1, source_target_pairs={{0,6},{1,7},{2,0},{3,1},{4,2},{5,3},{6,4},{7,5},{8,14},{9,15},{10,... | collective-permute-start | bytes 737288 | tf_op jit(solution)/shard_map/ppermute | solution.py:198
  67.0 2.4 %collective-permute-start.5 = (bf16[160,768]{1,0:T(8,128)(2,1)}, bf16[160,768]{1,0:T(8,128)(2,1)}, u32[]{:S(2)}, u32[]{:S(2)}) collective-permute-start(bf16[160,768]{1,0:T(8,128)(2,1)} %collective-permute-done.refs_1_), channel_id=1, source_target_pairs={{0,6},{1,7},{2,0},{3,1},{4,2},{5,3},{6,4},{7,5},{8,14},{9,15},{10,... | collective-permute-start | bytes 737288 | tf_op jit(solution)/shard_map/ppermute | solution.py:199
  73.7 2.5 %gather_fusion.2 = bf16[4,4,80,256]{3,2,1,0:T(8,128)(2,1)} fusion(bf16[4,4,80,256]{3,2,1,0:T(8,128)(2,1)} %pad_maximum_fusion, s32[1024]{0:T(1024)S(1)} %pad_clamp_fusion), kind=kCustom, calls=%fused_computation.2 | custom fusion | bytes 1310736 | tf_op jit(solution)/shard_map/jit(_take)/gather | solution.py:245
  80.6 5.3 %qkv.1 = (bf16[160,768]{1,0:T(8,128)(2,1)S(1)}, bf16[320,768]{1,0:T(8,128)(2,1)}) custom-call(s32[8]{0:T(128)S(1)} %stack.110.off_ref, bf16[160,768]{1,0:T(8,128)(2,1)S(1)} %turn.1.refs_0_, bf16[160,768]{1,0:T(8,128)(2,1)} %collective-permute-done.refs_1_, bf16[160,768]{1,0:T(8,128)(2,1)} %collective-permute-done.1.refs_2_, ...), custom_call_target="tpu_custom_call" | custom-call | flops 943718400 | bytes 6291456 | tf_op jit(solution)/shard_map/qkv/pallas_call | solution.py:327
  86.6 9.1 %collective-permute-start.7 = (bf16[320,768]{1,0:T(8,128)(2,1)}, bf16[320,768]{1,0:T(8,128)(2,1)S(1)}, u32[]{:S(2)}, u32[]{:S(2)}) collective-permute-start(bf16[320,768]{1,0:T(8,128)(2,1)} %get-tuple-element.5.own_ref), channel_id=1, source_target_pairs={{0,8},{8,0},{1,9},{9,1},{2,10},{10,2},{3,11},{11,3},{4,12},{12,4},... | collective-permute-start | bytes 1474568 | tf_op jit(solution)/shard_map/ppermute | solution.py:336
  98.8 5.0 %encoder_attend.1.refs_0_ = bf16[160,768]{1,0:T(8,128)(2,1)} custom-call(s32[12]{0:T(128)S(1)} %dynamic_slice.39.count_ref, s32[1]{0:T(128)} %bitcast.3.pipe_ref, bf16[160,768]{1,0:T(8,128)(2,1)S(1)} %copy-done.7, bf16[320,768]{1,0:T(8,128)(2,1)} %get-tuple-element.5.own_ref, bf16[320,768]{1,0:T(8,128)(2,1)S(1)} %collective-permute-done.7.other_ref), custom_call_target="tpu_custom_call" | custom-call | flops 125829120 | bytes 2097152 | tf_op jit(solution)/shard_map/encoder_attend/pallas_call | solution.py:338
  103.8 4.6 %collective-permute-start.8 = (bf16[160,768]{1,0:T(8,128)(2,1)}, bf16[160,768]{1,0:T(8,128)(2,1)}, u32[]{:S(2)}, u32[]{:S(2)}) collective-permute-start(bf16[160,768]{1,0:T(8,128)(2,1)} %encoder_attend.1.refs_0_), channel_id=1, source_target_pairs={{0,1},{1,0},{2,3},{3,2},{4,5},{5,4},{6,7},{7,6},{8,9},{9,8},{10,11... | collective-permute-start | bytes 737288 | tf_op jit(solution)/shard_map/ppermute | solution.py:197
  108.4 3.4 %collective-permute-start.10 = (bf16[160,768]{1,0:T(8,128)(2,1)}, bf16[160,768]{1,0:T(8,128)(2,1)S(1)}, u32[]{:S(2)}, u32[]{:S(2)}) collective-permute-start(bf16[160,768]{1,0:T(8,128)(2,1)} %encoder_attend.1.refs_0_), channel_id=1, source_target_pairs={{0,6},{1,7},{2,0},{3,1},{4,2},{5,3},{6,4},{7,5},{8,14},{9,15},{10,... | collective-permute-start | bytes 737288 | tf_op jit(solution)/shard_map/ppermute | solution.py:198
  114.0 2.6 %collective-permute-done.8.refs_1_ = bf16[160,768]{1,0:T(8,128)(2,1)} collective-permute-done((bf16[160,768]{1,0:T(8,128)(2,1)}, bf16[160,768]{1,0:T(8,128)(2,1)}, u32[]{:S(2)}, u32[]{:S(2)}) %collective-permute-start.8) | collective-permute-done | bytes 245792 | tf_op jit(solution)/shard_map/ppermute | solution.py:197
  131.3 3.1 %own_term.1.refs_9_ = f32[256,768]{1,0:T(8,128)S(1)} custom-call(s32[8]{0:T(128)S(1)} %stack.110.off_ref, bf16[160,768]{1,0:T(8,128)(2,1)S(1)} %turn.1.refs_0_, bf16[160,768]{1,0:T(8,128)(2,1)} %collective-permute-done.refs_1_, bf16[160,768]{1,0:T(8,128)(2,1)} %collective-permute-done.1.refs_2_, bf16[160,768]{1,0:T(8,128)(2,1)} %collective-permute-done.2.refs_3_, ...), custom_call_target="tpu_custom_call" | custom-call | flops 503316480 | bytes 4194304 | tf_op jit(solution)/shard_map/own_term/pallas_call | solution.py:348
  136.1 3.1 %memory.1 = bf16[2048,256]{1,0:T(8,128)(2,1)S(1)} custom-call(s32[8]{0:T(128)S(1)} %stack.110.off_ref, s32[32]{0:T(128)S(1)} %select_reduce_fusion.2.pick_ref, bf16[160,768]{1,0:T(8,128)(2,1)} %encoder_attend.1.refs_0_, bf16[160,768]{1,0:T(8,128)(2,1)} %collective-permute-done.8.refs_1_, bf16[160,768]{1,0:T(8,128)(2,1)} %collective-permute-done.9.refs_2_, ...), custom_call_target="tpu_custom_call" | custom-call | flops 503316480 | bytes 4194304 | tf_op jit(solution)/shard_map/memory/pallas_call | solution.py:386
  140.2 4.8 %all-to-all-start = ((bf16[16,128,256]{2,1,0:T(8,128)(2,1)}), bf16[16,128,256]{2,1,0:T(8,128)(2,1)}, u32[]{:S(2)}, u32[]{:S(2)}) async-start(bf16[16,128,256]{2,1,0:T(8,128)(2,1)} %bitcast.116), calls=%async_computation | async-start | bytes 2097152 | tf_op jit(solution)/shard_map/all_to_all | solution.py:399
  146.9 24.6 %all-to-all-done = bf16[16,128,256]{2,1,0:T(8,128)(2,1)} async-done(((bf16[16,128,256]{2,1,0:T(8,128)(2,1)}), bf16[16,128,256]{2,1,0:T(8,128)(2,1)}, u32[]{:S(2)}, u32[]{:S(2)}) %all-to-all-start) | async-done | bytes 1048608 | tf_op jit(solution)/shard_map/all_to_all | solution.py:399
  171.6 2.3 %collective-permute-start.30 = (bf16[2048,256]{1,0:T(8,128)(2,1)}, bf16[2048,256]{1,0:T(8,128)(2,1)}, u32[]{:S(2)}, u32[]{:S(2)}) collective-permute-start(bf16[2048,256]{1,0:T(8,128)(2,1)} %bitcast.56.own_ref), channel_id=1, source_target_pairs={{0,8},{8,0},{1,9},{9,1},{2,10},{10,2},{3,11},{11,3},{4,12},{12,4},... | collective-permute-start | bytes 3145736 | tf_op jit(solution)/shard_map/ppermute | solution.py:400
  174.5 2.2 %reshape.372 = bf16[32,32,256]{2,1,0:T(8,128)(2,1)} reshape(bf16[32,32,2,128]{3,2,1,0:T(2,128)(2,1)} %param.27) | data formatting | bytes 1048576 | tf_op jit(solution)/shard_map/reshape | solution.py:299
  180.9 3.2 %cross_attend.1 = bf16[2,32,1024]{2,1,0:T(8,128)(2,1)} custom-call(s32[32]{0:T(128)S(1)} %get-tuple-element.7.slot_ref, s32[1]{0:T(128)} %bitcast.3.pipe_ref, s32[512,1]{1,0:T(8,128)S(1)} %reshape_reshape.8.count_ref, bf16[32,16,128]{2,1,0:T(8,128)(2,1)S(1)} %copy_bitcast_fusion.2.q_ref, bf16[2048,256]{1,0:T(8,128)(2,1)} %bitcast.56.own_ref, ...), custom_call_target="tpu_custom_call" | custom-call | flops 33554432 | bytes 4194304 | tf_op jit(solution)/shard_map/cross_attend/pallas_call | solution.py:402
  (171 shorter events, 66.8 us)
Async XLA Ops:
  2.1 61.7 %collective-permute-start = (bf16[160,768]{1,0:T(8,128)(2,1)S(1)}, bf16[160,768]{1,0:T(8,128)(2,1)}, u32[]{:S(2)}, u32[]{:S(2)}) collective-permute-start(bf16[160,768]{1,0:T(8,128)(2,1)S(1)} %turn.1.refs_0_), channel_id=1, source_target_pairs={{0,1},{1,0},{2,3},{3,2},{4,5},{5,4},{6,7},{7,6},{8,9},{9,8},{10,11... | collective-permute-start | bytes 737288 | tf_op jit(solution)/shard_map/ppermute | solution.py:197
  9.9 56.3 %collective-permute-start.1 = (bf16[160,768]{1,0:T(8,128)(2,1)S(1)}, bf16[160,768]{1,0:T(8,128)(2,1)}, u32[]{:S(2)}, u32[]{:S(2)}) collective-permute-start(bf16[160,768]{1,0:T(8,128)(2,1)S(1)} %turn.1.refs_0_), channel_id=1, source_target_pairs={{0,2},{1,3},{2,4},{3,5},{4,6},{5,7},{6,0},{7,1},{8,10},{9,11},{10,... | collective-permute-start | bytes 737288 | tf_op jit(solution)/shard_map/ppermute | solution.py:198
  12.0 6.7 %collective-permute-start.15 = (bf16[5,1280]{1,0:T(8,128)(2,1)S(1)}, bf16[5,1280]{1,0:T(8,128)(2,1)S(1)}, u32[]{:S(2)}, u32[]{:S(2)}) collective-permute-start(bf16[5,1280]{1,0:T(8,128)(2,1)S(1)} %constant_dynamic-slice_fusion), channel_id=1, source_target_pairs={{0,1},{1,0},{2,3},{3,2},{4,5},{5,4},{6,7},{7,6},{8,9},{9,8},{10,11... | collective-permute-start | bytes 38408 | tf_op jit(solution)/shard_map/ppermute | solution.py:213
  30.6 8.3 %collective-permute-start.19 = (bf16[4,80,256]{2,1,0:T(8,128)(2,1)S(1)}, bf16[4,80,256]{2,1,0:T(8,128)(2,1)}, u32[]{:S(2)}, u32[]{:S(2)}) collective-permute-start(bf16[4,80,256]{2,1,0:T(8,128)(2,1)S(1)} %dynamic-slice_bitcast_fusion), channel_id=1, source_target_pairs={{0,1},{1,0},{2,3},{3,2},{4,5},{5,4},{6,7},{7,6},{8,9},{9,8},{10,11... | collective-permute-start | bytes 491528 | tf_op jit(solution)/shard_map/ppermute | solution.py:225
  47.0 8.4 %collective-permute-start.23 = (bf16[80,256]{1,0:T(8,128)(2,1)S(1)}, bf16[80,256]{1,0:T(8,128)(2,1)S(1)}, u32[]{:S(2)}, u32[]{:S(2)}) collective-permute-start(bf16[80,256]{1,0:T(8,128)(2,1)S(1)} %fusion.14), channel_id=1, source_target_pairs={{0,16},{16,32},{32,48},{48,0},{64,80},{80,96},{96,112},{112,64},{1... | collective-permute-start | bytes 122888 | tf_op jit(solution)/shard_map/ppermute | solution.py:237
  58.6 8.1 %collective-permute-start.26 = (bf16[4,80,256]{2,1,0:T(8,128)(2,1)}, bf16[4,80,256]{2,1,0:T(8,128)(2,1)}, u32[]{:S(2)}, u32[]{:S(2)}) collective-permute-start(bf16[4,80,256]{2,1,0:T(8,128)(2,1)} %broadcast_select_fusion.1), channel_id=1, source_target_pairs={{0,64},{16,80},{32,96},{48,112},{64,128},{80,144},{96,160},{112,17... | collective-permute-start | bytes 491528 | tf_op jit(solution)/shard_map/ppermute | solution.py:242
  59.8 7.2 %collective-permute-start.27 = (bf16[4,80,256]{2,1,0:T(8,128)(2,1)}, bf16[4,80,256]{2,1,0:T(8,128)(2,1)}, u32[]{:S(2)}, u32[]{:S(2)}) collective-permute-start(bf16[4,80,256]{2,1,0:T(8,128)(2,1)} %broadcast_select_fusion.1), channel_id=1, source_target_pairs={{0,128},{16,144},{32,160},{48,176},{64,192},{80,208},{96,224},{112... | collective-permute-start | bytes 491528 | tf_op jit(solution)/shard_map/ppermute | solution.py:242
  62.3 7.2 %collective-permute-start.28 = (bf16[4,80,256]{2,1,0:T(8,128)(2,1)}, bf16[4,80,256]{2,1,0:T(8,128)(2,1)}, u32[]{:S(2)}, u32[]{:S(2)}) collective-permute-start(bf16[4,80,256]{2,1,0:T(8,128)(2,1)} %broadcast_select_fusion.1), channel_id=1, source_target_pairs={{0,192},{16,208},{32,224},{48,240},{64,0},{80,16},{96,32},{112,48}... | collective-permute-start | bytes 491528 | tf_op jit(solution)/shard_map/ppermute | solution.py:242
  63.8 12.4 %collective-permute-start.2 = (bf16[160,768]{1,0:T(8,128)(2,1)S(1)}, bf16[160,768]{1,0:T(8,128)(2,1)}, u32[]{:S(2)}, u32[]{:S(2)}) collective-permute-start(bf16[160,768]{1,0:T(8,128)(2,1)S(1)} %turn.1.refs_0_), channel_id=1, source_target_pairs={{0,6},{1,7},{2,0},{3,1},{4,2},{5,3},{6,4},{7,5},{8,14},{9,15},{10,... | collective-permute-start | bytes 737288 | tf_op jit(solution)/shard_map/ppermute | solution.py:198
  66.3 10.0 %collective-permute-start.3 = (bf16[160,768]{1,0:T(8,128)(2,1)S(1)}, bf16[160,768]{1,0:T(8,128)(2,1)}, u32[]{:S(2)}, u32[]{:S(2)}) collective-permute-start(bf16[160,768]{1,0:T(8,128)(2,1)S(1)} %turn.1.refs_0_), channel_id=1, source_target_pairs={{0,4},{1,5},{2,6},{3,7},{4,0},{5,1},{6,2},{7,3},{8,12},{9,13},{10,... | collective-permute-start | bytes 737288 | tf_op jit(solution)/shard_map/ppermute | solution.py:198
  66.7 9.5 %collective-permute-start.4 = (bf16[160,768]{1,0:T(8,128)(2,1)}, bf16[160,768]{1,0:T(8,128)(2,1)}, u32[]{:S(2)}, u32[]{:S(2)}) collective-permute-start(bf16[160,768]{1,0:T(8,128)(2,1)} %collective-permute-done.refs_1_), channel_id=1, source_target_pairs={{0,2},{1,3},{2,4},{3,5},{4,6},{5,7},{6,0},{7,1},{8,10},{9,11},{10,... | collective-permute-start | bytes 737288 | tf_op jit(solution)/shard_map/ppermute | solution.py:199
  67.0 10.7 %collective-permute-start.5 = (bf16[160,768]{1,0:T(8,128)(2,1)}, bf16[160,768]{1,0:T(8,128)(2,1)}, u32[]{:S(2)}, u32[]{:S(2)}) collective-permute-start(bf16[160,768]{1,0:T(8,128)(2,1)} %collective-permute-done.refs_1_), channel_id=1, source_target_pairs={{0,6},{1,7},{2,0},{3,1},{4,2},{5,3},{6,4},{7,5},{8,14},{9,15},{10,... | collective-permute-start | bytes 737288 | tf_op jit(solution)/shard_map/ppermute | solution.py:199
  69.4 9.9 %collective-permute-start.6 = (bf16[160,768]{1,0:T(8,128)(2,1)}, bf16[160,768]{1,0:T(8,128)(2,1)}, u32[]{:S(2)}, u32[]{:S(2)}) collective-permute-start(bf16[160,768]{1,0:T(8,128)(2,1)} %collective-permute-done.refs_1_), channel_id=1, source_target_pairs={{0,4},{1,5},{2,6},{3,7},{4,0},{5,1},{6,2},{7,3},{8,12},{9,13},{10,... | collective-permute-start | bytes 737288 | tf_op jit(solution)/shard_map/ppermute | solution.py:199
  86.6 11.3 %collective-permute-start.7 = (bf16[320,768]{1,0:T(8,128)(2,1)}, bf16[320,768]{1,0:T(8,128)(2,1)S(1)}, u32[]{:S(2)}, u32[]{:S(2)}) collective-permute-start(bf16[320,768]{1,0:T(8,128)(2,1)} %get-tuple-element.5.own_ref), channel_id=1, source_target_pairs={{0,8},{8,0},{1,9},{9,1},{2,10},{10,2},{3,11},{11,3},{4,12},{12,4},... | collective-permute-start | bytes 1474568 | tf_op jit(solution)/shard_map/ppermute | solution.py:336
  96.6 16.0 %collective-permute-start.29 = (bf16[4,4,80,256]{3,2,1,0:T(8,128)(2,1)}, bf16[4,4,80,256]{3,2,1,0:T(8,128)(2,1)}, u32[]{:S(2)}, u32[]{:S(2)}) collective-permute-start(bf16[4,4,80,256]{3,2,1,0:T(8,128)(2,1)} %broadcast_select_fusion), channel_id=1, source_target_pairs={{0,8},{8,0},{1,9},{9,1},{2,10},{10,2},{3,11},{11,3},{4,12},{12,4},... | collective-permute-start | bytes 1966088 | tf_op jit(solution)/shard_map/ppermute | solution.py:246
  103.8 12.8 %collective-permute-start.8 = (bf16[160,768]{1,0:T(8,128)(2,1)}, bf16[160,768]{1,0:T(8,128)(2,1)}, u32[]{:S(2)}, u32[]{:S(2)}) collective-permute-start(bf16[160,768]{1,0:T(8,128)(2,1)} %encoder_attend.1.refs_0_), channel_id=1, source_target_pairs={{0,1},{1,0},{2,3},{3,2},{4,5},{5,4},{6,7},{7,6},{8,9},{9,8},{10,11... | collective-permute-start | bytes 737288 | tf_op jit(solution)/shard_map/ppermute | solution.py:197
  108.4 12.9 %collective-permute-start.10 = (bf16[160,768]{1,0:T(8,128)(2,1)}, bf16[160,768]{1,0:T(8,128)(2,1)S(1)}, u32[]{:S(2)}, u32[]{:S(2)}) collective-permute-start(bf16[160,768]{1,0:T(8,128)(2,1)} %encoder_attend.1.refs_0_), channel_id=1, source_target_pairs={{0,6},{1,7},{2,0},{3,1},{4,2},{5,3},{6,4},{7,5},{8,14},{9,15},{10,... | collective-permute-start | bytes 737288 | tf_op jit(solution)/shard_map/ppermute | solution.py:198
  111.9 22.5 %collective-permute-start.11 = (bf16[160,768]{1,0:T(8,128)(2,1)}, bf16[160,768]{1,0:T(8,128)(2,1)}, u32[]{:S(2)}, u32[]{:S(2)}) collective-permute-start(bf16[160,768]{1,0:T(8,128)(2,1)} %encoder_attend.1.refs_0_), channel_id=1, source_target_pairs={{0,4},{1,5},{2,6},{3,7},{4,0},{5,1},{6,2},{7,3},{8,12},{9,13},{10,... | collective-permute-start | bytes 737288 | tf_op jit(solution)/shard_map/ppermute | solution.py:198
  112.0 22.4 %collective-permute-start.9 = (bf16[160,768]{1,0:T(8,128)(2,1)}, bf16[160,768]{1,0:T(8,128)(2,1)}, u32[]{:S(2)}, u32[]{:S(2)}) collective-permute-start(bf16[160,768]{1,0:T(8,128)(2,1)} %encoder_attend.1.refs_0_), channel_id=1, source_target_pairs={{0,2},{1,3},{2,4},{3,5},{4,6},{5,7},{6,0},{7,1},{8,10},{9,11},{10,... | collective-permute-start | bytes 737288 | tf_op jit(solution)/shard_map/ppermute | solution.py:198
  116.7 17.8 %collective-permute-start.12 = (bf16[160,768]{1,0:T(8,128)(2,1)}, bf16[160,768]{1,0:T(8,128)(2,1)}, u32[]{:S(2)}, u32[]{:S(2)}) collective-permute-start(bf16[160,768]{1,0:T(8,128)(2,1)} %collective-permute-done.8.refs_1_), channel_id=1, source_target_pairs={{0,2},{1,3},{2,4},{3,5},{4,6},{5,7},{6,0},{7,1},{8,10},{9,11},{10,... | collective-permute-start | bytes 737288 | tf_op jit(solution)/shard_map/ppermute | solution.py:199
  118.0 16.4 %collective-permute-start.13 = (bf16[160,768]{1,0:T(8,128)(2,1)}, bf16[160,768]{1,0:T(8,128)(2,1)}, u32[]{:S(2)}, u32[]{:S(2)}) collective-permute-start(bf16[160,768]{1,0:T(8,128)(2,1)} %collective-permute-done.8.refs_1_), channel_id=1, source_target_pairs={{0,6},{1,7},{2,0},{3,1},{4,2},{5,3},{6,4},{7,5},{8,14},{9,15},{10,... | collective-permute-start | bytes 737288 | tf_op jit(solution)/shard_map/ppermute | solution.py:199
  122.0 14.1 %collective-permute-start.14 = (bf16[160,768]{1,0:T(8,128)(2,1)}, bf16[160,768]{1,0:T(8,128)(2,1)}, u32[]{:S(2)}, u32[]{:S(2)}) collective-permute-start(bf16[160,768]{1,0:T(8,128)(2,1)} %collective-permute-done.8.refs_1_), channel_id=1, source_target_pairs={{0,4},{1,5},{2,6},{3,7},{4,0},{5,1},{6,2},{7,3},{8,12},{9,13},{10,... | collective-permute-start | bytes 737288 | tf_op jit(solution)/shard_map/ppermute | solution.py:199
  140.2 31.4 %all-to-all-start = ((bf16[16,128,256]{2,1,0:T(8,128)(2,1)}), bf16[16,128,256]{2,1,0:T(8,128)(2,1)}, u32[]{:S(2)}, u32[]{:S(2)}) async-start(bf16[16,128,256]{2,1,0:T(8,128)(2,1)} %bitcast.116), calls=%async_computation | async-start | bytes 2097152 | tf_op jit(solution)/shard_map/all_to_all | solution.py:399
  171.6 9.4 %collective-permute-start.30 = (bf16[2048,256]{1,0:T(8,128)(2,1)}, bf16[2048,256]{1,0:T(8,128)(2,1)}, u32[]{:S(2)}, u32[]{:S(2)}) collective-permute-start(bf16[2048,256]{1,0:T(8,128)(2,1)} %bitcast.56.own_ref), channel_id=1, source_target_pairs={{0,8},{8,0},{1,9},{9,1},{2,10},{10,2},{3,11},{11,3},{4,12},{12,4},... | collective-permute-start | bytes 3145736 | tf_op jit(solution)/shard_map/ppermute | solution.py:400
  (30 other events, 310.2 us)

commit v2 on v1

--- a/solution.py
+++ b/solution.py
@@ -16,7 +16,7 @@
 STEPS = 2
 LMAX = 32
 TT = 32
-LIMIT = 48 * 1024 * 1024
+LIMIT = 62 * 1024 * 1024
 BF = jnp.bfloat16
 F32 = jnp.float32
 
@@ -56,25 +56,29 @@
 
 def qkv_kernel(off_ref, *refs):
     shards = refs[:8]
-    w_ref, gain_ref, q_ref, kv_ref, normed = refs[8:]
-    part = shards[0].shape[0]
+    w_ref, gain_ref, q_ref, kv_ref, full, sems = refs[8:]
+    part, rows = shards[0].shape
     width = part * 8
-    total = jnp.zeros((1, shards[0].shape[1]), F32)
-    for s in shards:
-        total += jnp.sum(s[...].astype(F32), 0, keepdims=True)
-    mean = total / width
-    total = jnp.zeros_like(mean)
-    for s in shards:
-        c = s[...].astype(F32) - mean
-        total += jnp.sum(c * c, 0, keepdims=True)
-    scale = lax.rsqrt(total / width + 1e-06)
-    for i, s in enumerate(shards):
-        at = pl.ds(pl.multiple_of(off_ref[i] * part, 16), part)
-        c = s[...].astype(F32) - mean
-        normed[at, :] = (c * scale * gain_ref[at, :]).astype(BF)
-    out = jnp.dot(w_ref[...], normed[...], preferred_element_type=F32).astype(BF)
-    q_ref[...] = out[:part]
-    kv_ref[...] = out[part:]
+    fill(off_ref, shards, (full,), (sems,))
+    cut = 256
+    for j in range(rows // cut):
+        lanes = slice(j * cut, (j + 1) * cut)
+        base = full[0:1, lanes].astype(F32)
+        total, squares = jnp.zeros((1, cut), F32), jnp.zeros((1, cut), F32)
+        for i in range(8):
+            c = full[i * part : (i + 1) * part, lanes].astype(F32) - base
+            total += jnp.sum(c, 0, keepdims=True)
+            squares += jnp.sum(c * c, 0, keepdims=True)
+        shift = total / width
+        mean = base + shift
+        scale = lax.rsqrt(jnp.maximum(squares / width - shift * shift, 0.0) + 1e-06)
+        for i in range(8):
+            at = slice(i * part, (i + 1) * part)
+            c = full[at, lanes].astype(F32) - mean
+            full[at, lanes] = (c * scale * gain_ref[at, :]).astype(BF)
+        out = jnp.dot(w_ref[...], full[:, lanes], preferred_element_type=F32).astype(BF)
+        q_ref[:, lanes] = out[:part]
+        kv_ref[:, lanes] = out[part:]
 
 
 def attend_kernel(count_ref, pipe_ref, q_ref, own_ref, other_ref, out_ref):
@@ -103,30 +107,28 @@
             out_ref[k_at, lanes] = jnp.dot(values, probs, preferred_element_type=F32).astype(BF)
 
 
-def fill(off_ref, shards, full, sems):
+def fill(off_ref, shards, fulls, sems):
     part = shards[0].shape[0]
     copies = []
     for i, s in enumerate(shards):
-        at = pl.ds(pl.multiple_of(off_ref[i] * part, 16), part)
-        copies.append(pltpu.make_async_copy(s, full.at[at, :], sems.at[i]))
+        at = pl.ds(pl.multiple_of(off_ref[i % 8] * part, 16), part)
+        copies.append(pltpu.make_async_copy(s, fulls[i // 8].at[at, :], sems[i // 8].at[i % 8]))
     for c in copies:
         c.start()
     for c in copies:
         c.wait()
 
 
-def own_term_kernel(off_ref, *refs):
-    shards = refs[:8]
-    w_ref, out_ref, full, sems = refs[8:]
-    fill(off_ref, shards, full, sems)
-    out_ref[...] = jnp.dot(w_ref[...], full[...], preferred_element_type=F32)
-
-
-def memory_kernel(off_ref, pick_ref, *refs):
-    shards = refs[:8]
-    w_ref, own_ref, gain_ref, out_ref, full, rows_ref, sems = refs[8:]
-    fill(off_ref, shards, full, sems)
-    kv = jnp.dot(w_ref[...], full[...], preferred_element_type=F32) + own_ref[...]
+def memory_kernel(off_ref, pick_ref, pipe_ref, *refs):
+    xs, ms = refs[:8], refs[8:16]
+    own_ref, other_ref, gain_ref, out_ref, x_ref, m_ref, rows_ref, x_sems, m_sems = refs[16:]
+    fill(off_ref, xs + ms, (x_ref, m_ref), (x_sems, m_sems))
+    half = own_ref.shape[0] // 2
+    mine = pl.ds(pl.multiple_of(pipe_ref[0] * half, 128), half)
+    rest = pl.ds(pl.multiple_of((1 - pipe_ref[0]) * half, 128), half)
+    first = ((0,), (0,))
+    kv = dot(own_ref[:half], x_ref[mine, :], first) + dot(other_ref[:half], x_ref[rest, :], first)
+    kv += dot(own_ref[half:], m_ref[mine, :], first) + dot(other_ref[half:], m_ref[rest, :], first)
     keys = kv[:HD]
     keys = keys * lax.rsqrt(jnp.mean(keys * keys, 0, keepdims=True) + 1e-05) * gain_ref[...]
     rows_ref[:, :HD] = jnp.transpose(keys).astype(BF)
@@ -192,10 +194,12 @@
     return [(t, (t + 2 * d) % 8) for t in range(8)]
 
 
-def gather8(s):
+def gather8(s, near=None):
     p1, p2, p3 = y_perm(1), y_perm(2), y_perm(3)
     z = lax.ppermute(s, "tensor", ZX)
+    s = s if near is None else near
     a, b, c = (lax.ppermute(s, "tensor", p) for p in (p1, p3, p2))
+    z = after(z, *((a, b, c) if near is None else ()))
     za, zb, zc = (lax.ppermute(z, "tensor", p) for p in (p1, p3, p2))
     return (s, z, a, b, c, za, zb, zc)
 
@@ -205,51 +209,68 @@
     return jnp.stack([t, t ^ 1, a, b, c, a ^ 1, b ^ 1, c ^ 1]).astype(jnp.int32)
 
 
-def fold_weights(enc_out_w, proj_w, cross_kv_w, u, tensor):
-    y, zh = tensor // 2, tensor % 2
+def after(value, *others):
+    return lax.optimization_barrier((value,) + others)[0]
+
+
+def swap(values, axis, bit, size):
+    return lax.ppermute(values, axis, [(i, i ^ bit) for i in range(size)])
+
+
+def choose(flag, a, b):
+    return jnp.where(flag, a, b)
+
+
+def out_rows(enc_out_w, replica, pipe):
     per = ENC_W // 32
-    few = per // 8
-    mine = lax.dynamic_slice_in_dim(enc_out_w, u * few, few)
-    other = lax.ppermute(mine, "tensor", ZX)
-    pair = jnp.where(zh == 0, jnp.stack([mine, other]), jnp.stack([other, mine]))
-    rel = jnp.stack([pair] + [lax.ppermute(pair, "tensor", y_perm(d)) for d in (1, 2, 3)])
-    whole = jnp.take(rel, (y - jnp.arange(4)) % 4, axis=0).reshape(per, ENC_W)
-    folded = jnp.dot(whole, proj_w, preferred_element_type=F32).astype(BF)
-    left = jnp.concatenate([lax.dynamic_slice_in_dim(proj_w, u * per, per), folded], 0)
-    part = jnp.einsum(
-        "rk,kcn->crn", left, cross_kv_w, preferred_element_type=F32
-    ).astype(BF)
-    part = part.reshape(2, 2 * per, 4, 2, HD).transpose(3, 2, 1, 0, 4).reshape(2, 4, 2 * per, 2 * HD)
-    keep = lax.dynamic_index_in_dim(part, zh, 0, keepdims=False)
-    send = lax.dynamic_index_in_dim(part, 1 - zh, 0, keepdims=False)
-    half = keep.astype(F32) + lax.ppermute(send, "tensor", ZX).astype(F32)
-    total = lax.dynamic_index_in_dim(half, y, 0, keepdims=False)
-    half = half.astype(BF)
-    for d in (1, 2, 3):
-        block = lax.dynamic_index_in_dim(half, (y + d) % 4, 0, keepdims=False)
-        total = total + lax.ppermute(block, "tensor", y_perm(d)).astype(F32)
-    return total.astype(BF)
-
-
-def spread_weights(piece, replica, pipe):
-    x, zl = replica // 4, replica % 4
-    zs = [piece] + [
-        lax.ppermute(piece, "replica", [(r, r // 4 * 4 + (r + d) % 4) for r in range(16)])
-        for d in (1, 2, 3)
-    ]
-    line = jnp.take(jnp.stack(zs), (zl - jnp.arange(4)) % 4, axis=0)
-    xs = [line] + [
-        lax.ppermute(line, "replica", [(r, (r + 4 * d) % 16) for r in range(16)])
-        for d in (1, 2, 3)
-    ]
-    plane = jnp.take(jnp.stack(xs), (x - jnp.arange(4)) % 4, axis=0)
-    other = lax.ppermute(plane, "pipe", [(0, 1), (1, 0)])
-    both = jnp.where(pipe == 0, jnp.stack([plane, other], 2), jnp.stack([other, plane], 2))
-    per = piece.shape[0] // 2
-    both = both.reshape(32, 2, per, 2 * HD)
-    first = both[:, 0].reshape(ENC_W, 2 * HD)
-    second = both[:, 1].reshape(32, 8, per // 8, 2 * HD).transpose(1, 0, 2, 3).reshape(ENC_W, 2 * HD)
-    return first.T, second.T
+    pairs = []
+    for r in range(16):
+        for p in range(2):
+            for t in range(8):
+                part = p * 4 + r // 4
+                near = t % 2 == part % 2
+                source = t // 2 * 4 + (r % 4 if near else 3 - r % 4)
+                core = 0 if near else 1
+                pairs.append(((source * 2 + core) * 8 + part, (r * 2 + p) * 8 + t))
+    block = jnp.where(pipe == 0, replica % 4, 3 - replica % 4)
+    mine = lax.dynamic_slice_in_dim(enc_out_w, block * per, per)
+    return lax.ppermute(mine, ("replica", "pipe", "tensor"), pairs)
+
+
+def heads_kernel(part_ref, out_ref):
+    for h in range(KV_HEADS):
+        out_ref[h, :, :HD] = part_ref[0, :, h * HD : (h + 1) * HD]
+        out_ref[h, :, HD:] = part_ref[1, :, h * HD : (h + 1) * HD]
+
+
+def fold_weights(few, proj_w, cross_kv_w, replica, pipe, hold, late):
+    per = ENC_W // 32
+    folded = jnp.dot(few, proj_w, preferred_element_type=F32).astype(BF)
+    left = lax.dynamic_slice_in_dim(proj_w, (pipe * 16 + replica) * per, per)
+    left = after(jnp.concatenate([left, folded], 0), *hold)
+    part = jnp.einsum("rk,kcn->crn", left, cross_kv_w, preferred_element_type=F32).astype(BF)
+    blocks = call(
+        heads_kernel,
+        shape_of((KV_HEADS, 2 * per, 2 * HD), BF),
+        [VMEM],
+        [],
+        0,
+        2 * part.size * 2,
+        "heads",
+    )(part)
+    return lax.all_to_all(after(blocks, *late), "tensor", split_axis=0, concat_axis=0, tiled=True)
+
+
+def line_shift(d):
+    return [(r, r // 4 * 4 + (r + d) % 4) for r in range(16)]
+
+
+def plane_shift(d):
+    return [(r, (r + 4 * d) % 16) for r in range(16)]
+
+
+def ring_of(piece, shift):
+    return jnp.stack([piece] + [lax.ppermute(piece, "replica", shift(d)) for d in (1, 2, 3)])
 
 
 def shards(
@@ -281,54 +302,15 @@
     turned = call(
         turn_kernel, shape_of((part, rows), BF), [VMEM], [], 2 * rows * part * part, 4 * rows * part, "turn"
     )(patches.reshape(rows, part))
-    xs = gather8(turned)
-
-    u = group * 2 + pipe
-    piece = fold_weights(enc_out_w, proj_w, cross_kv_w, u, tensor)
-    w_own, w_mixed = spread_weights(piece, group, pipe)
-
-    rows_here = row_pick.shape[0]
-    steps_heads = q_self.shape[0] * q_self.shape[2] // HD
-
-    def heads_of(q):
-        return q.reshape(STEPS, rows_here, -1, HD).transpose(1, 0, 2, 3).reshape(rows_here, steps_heads, HD)
-
-    spots = 48
-    joined = jnp.concatenate(
-        [
-            cache_kv.reshape(rows_here, LMAX, 2 * HD),
-            jnp.moveaxis(new_kv, 0, 1).reshape(rows_here, STEPS, 2 * HD),
-            jnp.zeros((rows_here, spots - LMAX - STEPS, 2 * HD), BF),
-        ],
-        1,
-    )
-
-    def per_head(values):
-        return jnp.repeat(values.astype(jnp.int32), steps_heads).reshape(rows_here * steps_heads, 1)
-
-    def scratch(n):
-        return [
-            pltpu.VMEM((rows_here * steps_heads, n), F32),
-            pltpu.VMEM((rows_here * steps_heads, n), BF),
-            pltpu.VMEM((rows_here, steps_heads, HD), F32),
-        ]
-
-    self_out = call(
-        self_kernel,
-        shape_of(q_self.shape, BF),
-        [VMEM] * 3,
-        scratch(spots),
-        4 * rows_here * 16 * 128 * 128,
-        4 * 1024 * 1024,
-        "self_attend",
-    )(per_head(kv_len), heads_of(q_self), joined)
+    few = out_rows(enc_out_w, group, pipe)
+    xs = gather8(turned, after(turned, few))
 
     turned_w = enc_qkv.transpose(1, 2, 0).reshape(3 * part, ENC_W)
     q, kv = call(
         qkv_kernel,
         (shape_of((part, rows), BF), shape_of((2 * part, rows), BF)),
-        [SMEM] + [VMEM] * 10,
-        [pltpu.VMEM((ENC_W, rows), BF)],
+        [SMEM] + [ANY] * 8 + [VMEM] * 2,
+        [pltpu.VMEM((ENC_W, rows), BF), pltpu.SemaphoreType.DMA((8,))],
         2 * rows * ENC_W * 3 * part,
         6 * 1024 * 1024,
         "qkv",
@@ -345,17 +327,16 @@
         "encoder_attend",
     )(counts_local, pipe_at, q, kv, kv_other)
 
-    own_term = call(
-        own_term_kernel,
-        shape_of((2 * HD, rows), F32),
-        [SMEM] + [ANY] * 8 + [VMEM],
-        [pltpu.VMEM((ENC_W, rows), BF), pltpu.SemaphoreType.DMA((8,))],
-        2 * rows * ENC_W * 2 * HD,
-        4 * 1024 * 1024,
-        "own_term",
-    )(order, *xs, w_own)
-
+    parts = fold_weights(few, proj_w, cross_kv_w, group, pipe, (), ())
+    piece = jnp.sum(after(parts, kv).astype(F32), 0).astype(BF)
+    line = ring_of(piece, line_shift)
     ms = gather8(mixed)
+    plane = ring_of(after(line, mixed), plane_shift)
+    spot = jnp.arange(16)
+    spot = (group // 4 - spot // 4) % 4 * 4 + (group - spot) % 4
+    pieces = jnp.take(after(plane, *ms[5:]).reshape(16, 2, -1, 2 * HD), spot, axis=0)
+    pieces = jnp.moveaxis(pieces, 1, 0).reshape(ENC_W, 2 * HD)
+    pieces_other = lax.ppermute(pieces, "pipe", [(0, 1), (1, 0)])
 
     destination = plan[:, 0]
     grouped = destination.reshape(replicas, images)
@@ -386,17 +367,57 @@
     slots = call(
         memory_kernel,
         shape_of((replicas * CAP * held * tile_rows, 2 * HD), BF),
-        [SMEM, SMEM] + [ANY] * 8 + [VMEM] * 3,
+        [SMEM] * 3 + [ANY] * 16 + [VMEM] * 3,
         [
+            pltpu.VMEM((ENC_W, rows), BF),
             pltpu.VMEM((ENC_W, rows), BF),
             pltpu.VMEM((rows, 2 * HD), BF),
             pltpu.SemaphoreType.DMA((8,)),
+            pltpu.SemaphoreType.DMA((8,)),
         ],
-        2 * rows * ENC_W * 2 * HD,
+        4 * rows * ENC_W * 2 * HD,
+        6 * 1024 * 1024,
+        "memory",
+    )(order, picks, pipe_at, *xs, *ms, pieces, pieces_other, k_gain.reshape(HD, 1))
+    arrived = lax.all_to_all(slots, "replica", split_axis=0, concat_axis=0, tiled=True)
+    q_self, q_cross, cache_kv, new_kv, kv_len = (after(v, slots) for v in (q_self, q_cross, cache_kv, new_kv, kv_len))
+    rows_here = row_pick.shape[0]
+    steps_heads = q_self.shape[0] * q_self.shape[2] // HD
+
+    def heads_of(q):
+        return q.reshape(STEPS, rows_here, -1, HD).transpose(1, 0, 2, 3).reshape(rows_here, steps_heads, HD)
+
+    spots = 48
+    joined = jnp.concatenate(
+        [
+            cache_kv.reshape(rows_here, LMAX, 2 * HD),
+            jnp.moveaxis(new_kv, 0, 1).reshape(rows_here, STEPS, 2 * HD),
+            jnp.zeros((rows_here, spots - LMAX - STEPS, 2 * HD), BF),
+        ],
+        1,
+    )
+
+    def per_head(values):
+        return jnp.repeat(values.astype(jnp.int32), steps_heads).reshape(rows_here * steps_heads, 1)
+
+    def scratch(n):
+        return [
+            pltpu.VMEM((rows_here * steps_heads, n), F32),
+            pltpu.VMEM((rows_here * steps_heads, n), BF),
+            pltpu.VMEM((rows_here, steps_heads, HD), F32),
+        ]
+
+    self_out = call(
+        self_kernel,
+        shape_of(q_self.shape, BF),
+        [VMEM] * 3,
+        scratch(spots),
+        4 * rows_here * 16 * 128 * 128,
         4 * 1024 * 1024,
-        "memory",
-    )(order, picks, *ms, w_mixed, own_term, k_gain.reshape(HD, 1))
-    arrived = lax.all_to_all(slots, "replica", split_axis=0, concat_axis=0, tiled=True)
+        "self_attend",
+    )(per_head(kv_len), heads_of(q_self), joined)
+    cross_heads, cross_counts = heads_of(q_cross), per_head(counts_rows)
+    arrived = after(arrived, self_out, cross_heads, cross_counts, slot_ids)
     arrived_other = lax.ppermute(arrived, "pipe", [(0, 1), (1, 0)])
 
     cross_out = call(
@@ -407,7 +428,7 @@
         4 * rows_here * 16 * 128 * 128,
         4 * 1024 * 1024,
         "cross_attend",
-    )(slot_ids, pipe_at, per_head(counts_rows), heads_of(q_cross), arrived, arrived_other)
+    )(slot_ids, pipe_at, cross_counts, cross_heads, arrived, arrived_other)
     return (cross_out, self_out)
 
 

time: 186 us -> 156 us (0.84)
  local copies, waits for them, and re-layouts: 28.8 us -> 13.9 us
  waiting for transfers between devices: 45 us -> 31.6 us
  other arithmetic: 11 us -> 4.74 us
  Pallas kernels: 21.6 us -> 27.4 us
  starting transfers between devices: 71 us -> 68.1 us
  matrix products: 4.21 us -> 6.65 us
    ppermute x15 -> x8, waiting for transfers between devices: 11.8 us -> 0.02 us  [the longest x6 0.02 us: ring_of(): lax.ppermute(piece, 'replica', shift(d))]
    all_to_all x1, waiting for transfers between devices: 24.6 us -> 16.3 us  [shards(): lax.all_to_all(slots, 'replica', split_axis=0, concat_axis=0, tiled=True)]
    ppermute x1, starting transfers between devices: 9.07 us -> 1.75 us  [shards(): kv_other = lax.ppermute(kv, 'pipe', [(0, 1), (1, 0)])]
    all_to_all x0 -> x1, starting transfers between devices: none -> 6.56 us  [fold_weights(): lax.all_to_all(after(blocks, *late), 'tensor', split_axis=0, concat_axis=...]
    ppermute x2, starting transfers between devices: 12.4 us -> 7.17 us  [gather8(): z = lax.ppermute(s, 'tensor', ZX)]
    ppermute x2, waiting for transfers between devices: 2.61 us -> 7.2 us  [gather8(): z = lax.ppermute(s, 'tensor', ZX)]
    unnamed x47 -> x53, local copies, waits for them, and re-layouts: 8.57 us -> 4.08 us
    select_n x10 -> x2, other arithmetic: 4.37 us -> 0.14 us  [shards(): jnp.take(after(plane, *ms[5:]).reshape(16, 2, -1, 2 * HD), spot, axis=0)]
  transfers between devices with their start and end apart: 32 -> 26, of which waited for: 15 -> 8; matrix products, arithmetic and copies ran while one was open for 20% -> 14% of each run, Pallas kernels for 5% -> 11%
where the time goes in v2:
time: 156 us; the launch traced here: 155 us
  starting transfers between devices  68.1 us (44%)
  waiting for transfers between devices  31.6 us (20%)
  Pallas kernels  27.4 us (18%)
  local copies, waits for them, and re-layouts  13.9 us (9%)
  matrix products  6.65 us (4%)
  other arithmetic  4.74 us (3%)
  between operations  2.44 us (2%)
    all_to_all x1, waiting for transfers between devices, shards(): lax.all_to_all(slots, 'replica', split_axis=0, concat_axis=0, tiled=True)  16.3 us
    ppermute x6, starting transfers between devices, ring_of(): lax.ppermute(piece, 'replica', shift(d))  11.3 us
    ppermute x6, starting transfers between devices, gather8(): a, b, c = (lax.ppermute(s, 'tensor', p) for p in (p1, p3, p2))  9.07 us
    ppermute x1, starting transfers between devices, out_rows(): return lax.ppermute(mine, ('replica', 'pipe', 'tensor'), pairs)  8.87 us
    all_to_all x1, starting transfers between devices, shards(): lax.all_to_all(slots, 'replica', split_axis=0, concat_axis=0, tiled=True)  8.38 us
    ppermute x2, waiting for transfers between devices, gather8(): z = lax.ppermute(s, 'tensor', ZX)  7.2 us
    ppermute x2, starting transfers between devices, gather8(): z = lax.ppermute(s, 'tensor', ZX)  7.17 us
    ppermute x1, starting transfers between devices, shards(): pieces_other = lax.ppermute(pieces, 'pipe', [(0, 1), (1, 0)])  7.16 us
  transfers between devices with their start and end apart: 26, of which 8 were waited for; matrix products, arithmetic and copies ran while one was open for 14% of the time, Pallas kernels for 11%

profile of v2, /device:TPU:1, one launch (start us, length us, event | category | flops | bytes accessed | tf_op | source)
XLA Modules:
  0.0 154.9 jit_solution(12681461329341761185)
XLA Ops:
  1.6 8.9 %collective-permute-start = (bf16[40,1280]{1,0:T(8,128)(2,1)S(1)}, bf16[40,1280]{1,0:T(8,128)(2,1)S(1)}, u32[]{:S(2)}, u32[]{:S(2)}) collective-permute-start(bf16[40,1280]{1,0:T(8,128)(2,1)S(1)} %constant_dynamic-slice_fusion.1), channel_id=1, source_target_pairs={{0,0},{56,1},{64,2},{120,3},{128,4},{184,5},{192,6},{248,7},{4,8},... | collective-permute-start | bytes 307208 | tf_op jit(solution)/shard_map/ppermute | solution.py:237
  10.5 2.0 %turn.1.refs_0_ = bf16[160,768]{1,0:T(8,128)(2,1)} custom-call(bf16[768,160]{1,0:T(8,128)(2,1)} %bitcast.82), custom_call_target="tpu_custom_call" | custom-call | flops 39321600 | bytes 491520 | tf_op jit(solution)/shard_map/turn/pallas_call | solution.py:302
  12.5 2.1 %collective-permute-start.1 = (bf16[160,768]{1,0:T(8,128)(2,1)}, bf16[160,768]{1,0:T(8,128)(2,1)S(1)}, u32[]{:S(2)}, u32[]{:S(2)}) collective-permute-start(bf16[160,768]{1,0:T(8,128)(2,1)} %turn.1.refs_0_), channel_id=1, source_target_pairs={{0,1},{1,0},{2,3},{3,2},{4,5},{5,4},{6,7},{7,6},{8,9},{9,8},{10,11... | collective-permute-start | bytes 737288 | tf_op jit(solution)/shard_map/ppermute | solution.py:199
  15.5 2.5 %collective-permute-start.2 = (bf16[160,768]{1,0:T(8,128)(2,1)}, bf16[160,768]{1,0:T(8,128)(2,1)S(1)}, u32[]{:S(2)}, u32[]{:S(2)}) collective-permute-start(bf16[160,768]{1,0:T(8,128)(2,1)} %turn.1.refs_0_), channel_id=1, source_target_pairs={{0,2},{1,3},{2,4},{3,5},{4,6},{5,7},{6,0},{7,1},{8,10},{9,11},{10,... | collective-permute-start | bytes 737288 | tf_op jit(solution)/shard_map/ppermute | solution.py:201
  19.9 2.3 %convolution_convert_fusion = bf16[40,1024]{1,0:T(8,128)(2,1)S(1)} fusion(bf16[40,1280]{1,0:T(8,128)(2,1)S(1)} %collective-permute-done, bf16[1280,1024]{1,0:T(8,128)(2,1)} %param.20), kind=kOutput, calls=%fused_computation.5 | convolution fusion | flops 104898560 | bytes 2805760 | tf_op jit(solution)/shard_map/dot_general | solution.py:248
  22.3 6.0 %collective-permute-done.1.refs_1_ = bf16[160,768]{1,0:T(8,128)(2,1)S(1)} collective-permute-done((bf16[160,768]{1,0:T(8,128)(2,1)}, bf16[160,768]{1,0:T(8,128)(2,1)S(1)}, u32[]{:S(2)}, u32[]{:S(2)}) %collective-permute-start.1) | collective-permute-done | bytes 245792 | tf_op jit(solution)/shard_map/ppermute | solution.py:199
  31.8 4.3 %fusion.5.part_ref = bf16[2,80,1024]{2,1,0:T(8,128)(2,1)} fusion(bf16[1024,2,1024]{2,1,0:T(2,128)(2,1)} %param.21, bf16[80,1024]{1,0:T(8,128)(2,1)S(1)} %pad_maximum_fusion.1), kind=kOutput, calls=%fused_computation.4 | convolution fusion | flops 335708160 | bytes 4685824 | tf_op jit(solution)/shard_map/rk,kcn->crn/dot_general | solution.py:251
  37.9 6.6 %all-to-all-start = ((bf16[8,80,256]{2,1,0:T(8,128)(2,1)}), bf16[8,80,256]{2,1,0:T(8,128)(2,1)S(1)}, u32[]{:S(2)}, u32[]{:S(2)}) async-start(bf16[8,80,256]{2,1,0:T(8,128)(2,1)} %heads.1), calls=%async_computation | async-start | bytes 655360 | tf_op jit(solution)/shard_map/all_to_all | solution.py:261
  47.1 5.9 %qkv.1 = (bf16[160,768]{1,0:T(8,128)(2,1)}, bf16[320,768]{1,0:T(8,128)(2,1)}) custom-call(s32[8]{0:T(128)} %stack.65.off_ref, bf16[160,768]{1,0:T(8,128)(2,1)} %turn.1.refs_0_, bf16[160,768]{1,0:T(8,128)(2,1)} %copy-done.3, bf16[160,768]{1,0:T(8,128)(2,1)} %copy-done.4, bf16[160,768]{1,0:T(8,128)(2,1)} %copy-done.5, bf16[160,768]{1,0:T(8,128)(2,1)} %copy-done.6, ...), custom_call_target="tpu_custom_call" | custom-call | flops 943718400 | bytes 6291456 | tf_op jit(solution)/shard_map/qkv/pallas_call | solution.py:309
  55.0 2.4 %collective-permute-start.16 = (bf16[80,256]{1,0:T(8,128)(2,1)S(1)}, bf16[80,256]{1,0:T(8,128)(2,1)S(1)}, u32[]{:S(2)}, u32[]{:S(2)}) collective-permute-start(bf16[80,256]{1,0:T(8,128)(2,1)S(1)} %reduce_sum.62), channel_id=1, source_target_pairs={{0,16},{16,32},{32,48},{48,0},{64,80},{80,96},{96,112},{112,64},{1... | collective-permute-start | bytes 122888 | tf_op jit(solution)/shard_map/ppermute | solution.py:273
  58.0 2.3 %collective-permute-start.18 = (bf16[80,256]{1,0:T(8,128)(2,1)S(1)}, bf16[80,256]{1,0:T(8,128)(2,1)S(1)}, u32[]{:S(2)}, u32[]{:S(2)}) collective-permute-start(bf16[80,256]{1,0:T(8,128)(2,1)S(1)} %reduce_sum.62), channel_id=1, source_target_pairs={{0,48},{16,0},{32,16},{48,32},{64,112},{80,64},{96,80},{112,96},{1... | collective-permute-start | bytes 122888 | tf_op jit(solution)/shard_map/ppermute | solution.py:273
  61.7 5.2 %encoder_attend.1.refs_8_ = bf16[160,768]{1,0:T(8,128)(2,1)} custom-call(s32[12]{0:T(128)} %dynamic_slice.19.count_ref, s32[1]{0:T(128)} %bitcast.3.pipe_ref, bf16[160,768]{1,0:T(8,128)(2,1)} %get-tuple-element.16.q_ref, bf16[320,768]{1,0:T(8,128)(2,1)} %get-tuple-element.17.own_ref, bf16[320,768]{1,0:T(8,128)(2,1)} %copy-done.8), custom_call_target="tpu_custom_call" | custom-call | flops 125829120 | bytes 2097152 | tf_op jit(solution)/shard_map/encoder_attend/pallas_call | solution.py:320
  71.6 5.1 %collective-permute-start.9 = (bf16[160,768]{1,0:T(8,128)(2,1)}, bf16[160,768]{1,0:T(8,128)(2,1)S(1)}, u32[]{:S(2)}, u32[]{:S(2)}) collective-permute-start(bf16[160,768]{1,0:T(8,128)(2,1)} %encoder_attend.1.refs_8_), channel_id=1, source_target_pairs={{0,1},{1,0},{2,3},{3,2},{4,5},{5,4},{6,7},{7,6},{8,9},{9,8},{10,11... | collective-permute-start | bytes 737288 | tf_op jit(solution)/shard_map/ppermute | solution.py:199
  76.8 4.0 %collective-permute-start.20 = (bf16[4,80,256]{2,1,0:T(8,128)(2,1)S(1)}, bf16[4,80,256]{2,1,0:T(8,128)(2,1)S(1)}, u32[]{:S(2)}, u32[]{:S(2)}) collective-permute-start(bf16[4,80,256]{2,1,0:T(8,128)(2,1)S(1)} %pad_maximum_fusion.2), channel_id=1, source_target_pairs={{0,128},{16,144},{32,160},{48,176},{64,192},{80,208},{96,224},{112... | collective-permute-start | bytes 491528 | tf_op jit(solution)/shard_map/ppermute | solution.py:273
  80.8 1.9 %collective-permute-start.21 = (bf16[4,80,256]{2,1,0:T(8,128)(2,1)S(1)}, bf16[4,80,256]{2,1,0:T(8,128)(2,1)S(1)}, u32[]{:S(2)}, u32[]{:S(2)}) collective-permute-start(bf16[4,80,256]{2,1,0:T(8,128)(2,1)S(1)} %pad_maximum_fusion.2), channel_id=1, source_target_pairs={{0,192},{16,208},{32,224},{48,240},{64,0},{80,16},{96,32},{112,48}... | collective-permute-start | bytes 491528 | tf_op jit(solution)/shard_map/ppermute | solution.py:273
  84.2 2.4 %collective-permute-start.14 = (bf16[160,768]{1,0:T(8,128)(2,1)S(1)}, bf16[160,768]{1,0:T(8,128)(2,1)S(1)}, u32[]{:S(2)}, u32[]{:S(2)}) collective-permute-start(bf16[160,768]{1,0:T(8,128)(2,1)S(1)} %collective-permute-done.9.refs_9_), channel_id=1, source_target_pairs={{0,6},{1,7},{2,0},{3,1},{4,2},{5,3},{6,4},{7,5},{8,14},{9,15},{10,... | collective-permute-start | bytes 737288 | tf_op jit(solution)/shard_map/ppermute | solution.py:203
  86.8 3.7 %collective-permute-done.13.refs_13_ = bf16[160,768]{1,0:T(8,128)(2,1)S(1)} collective-permute-done((bf16[160,768]{1,0:T(8,128)(2,1)S(1)}, bf16[160,768]{1,0:T(8,128)(2,1)S(1)}, u32[]{:S(2)}, u32[]{:S(2)}) %collective-permute-start.13) | collective-permute-done | bytes 245792 | tf_op jit(solution)/shard_map/ppermute | solution.py:203
  90.5 1.9 %collective-permute-done.14.refs_14_ = bf16[160,768]{1,0:T(8,128)(2,1)S(1)} collective-permute-done((bf16[160,768]{1,0:T(8,128)(2,1)S(1)}, bf16[160,768]{1,0:T(8,128)(2,1)S(1)}, u32[]{:S(2)}, u32[]{:S(2)}) %collective-permute-start.14) | collective-permute-done | bytes 245792 | tf_op jit(solution)/shard_map/ppermute | solution.py:203
  94.1 7.2 %collective-permute-start.22 = (bf16[1280,256]{1,0:T(8,128)(2,1)S(1)}, bf16[1280,256]{1,0:T(8,128)(2,1)S(1)}, u32[]{:S(2)}, u32[]{:S(2)}) collective-permute-start(bf16[1280,256]{1,0:T(8,128)(2,1)S(1)} %bitcast.76), channel_id=1, source_target_pairs={{0,8},{8,0},{1,9},{9,1},{2,10},{10,2},{3,11},{11,3},{4,12},{12,4},... | collective-permute-start | bytes 1966088 | tf_op jit(solution)/shard_map/ppermute | solution.py:339
  105.6 6.3 %memory.1 = bf16[2048,256]{1,0:T(8,128)(2,1)} custom-call(s32[8]{0:T(128)} %stack.65.off_ref, s32[32]{0:T(128)} %select_reduce_fusion.2.pick_ref, s32[1]{0:T(128)} %bitcast.3.pipe_ref, bf16[160,768]{1,0:T(8,128)(2,1)} %turn.1.refs_0_, bf16[160,768]{1,0:T(8,128)(2,1)} %copy-done.3, bf16[160,768]{1,0:T(8,128)(2,1)} %copy-done.4, bf16[160,768]{1,0:T(8,128)(2,1)} %copy-done.5, ...), custom_call_target="tpu_custom_call" | custom-call | flops 1006632960 | bytes 6291456 | tf_op jit(solution)/shard_map/memory/pallas_call | solution.py:367
  111.9 8.4 %all-to-all-start.1 = ((bf16[16,128,256]{2,1,0:T(8,128)(2,1)}), bf16[16,128,256]{2,1,0:T(8,128)(2,1)S(1)}, u32[]{:S(2)}, u32[]{:S(2)}) async-start(bf16[16,128,256]{2,1,0:T(8,128)(2,1)} %bitcast.74), calls=%async_computation.1 | async-start | bytes 2097152 | tf_op jit(solution)/shard_map/all_to_all | solution.py:382
  127.7 2.8 %self_attend.1 = bf16[2,32,1024]{2,1,0:T(8,128)(2,1)} custom-call(s32[512,1]{1,0:T(8,128)} %reshape_reshape.8.len_ref, bf16[32,16,128]{2,1,0:T(8,128)(2,1)} %copy_bitcast_fusion.q_ref, bf16[32,48,256]{2,1,0:T(8,128)(2,1)} %maximum_maximum_fusion.kv_ref), custom_call_target="tpu_custom_call" | custom-call | flops 33554432 | bytes 4194304 | tf_op jit(solution)/shard_map/self_attend/pallas_call | solution.py:410
  131.2 16.3 %all-to-all-done.1 = bf16[16,128,256]{2,1,0:T(8,128)(2,1)S(1)} async-done(((bf16[16,128,256]{2,1,0:T(8,128)(2,1)}), bf16[16,128,256]{2,1,0:T(8,128)(2,1)S(1)}, u32[]{:S(2)}, u32[]{:S(2)}) %all-to-all-start.1) | async-done | bytes 1048608 | tf_op jit(solution)/shard_map/all_to_all | solution.py:382
  151.5 3.4 %cross_attend.1 = bf16[2,32,1024]{2,1,0:T(8,128)(2,1)} custom-call(s32[32]{0:T(128)} %get-tuple-element.29.slot_ref, s32[1]{0:T(128)} %bitcast.3.pipe_ref, s32[512,1]{1,0:T(8,128)} %copy.40.count_ref, bf16[32,16,128]{2,1,0:T(8,128)(2,1)} %copy_bitcast_fusion.1.q_ref, bf16[2048,256]{1,0:T(8,128)(2,1)} %bitcast.73, ...), custom_call_target="tpu_custom_call" | custom-call | flops 33554432 | bytes 4194304 | tf_op jit(solution)/shard_map/cross_attend/pallas_call | solution.py:423
  (137 shorter events, 38.7 us)
Async XLA Ops:
  1.6 13.9 %collective-permute-start = (bf16[40,1280]{1,0:T(8,128)(2,1)S(1)}, bf16[40,1280]{1,0:T(8,128)(2,1)S(1)}, u32[]{:S(2)}, u32[]{:S(2)}) collective-permute-start(bf16[40,1280]{1,0:T(8,128)(2,1)S(1)} %constant_dynamic-slice_fusion.1), channel_id=1, source_target_pairs={{0,0},{56,1},{64,2},{120,3},{128,4},{184,5},{192,6},{248,7},{4,8},... | collective-permute-start | bytes 307208 | tf_op jit(solution)/shard_map/ppermute | solution.py:237
  12.5 15.7 %collective-permute-start.1 = (bf16[160,768]{1,0:T(8,128)(2,1)}, bf16[160,768]{1,0:T(8,128)(2,1)S(1)}, u32[]{:S(2)}, u32[]{:S(2)}) collective-permute-start(bf16[160,768]{1,0:T(8,128)(2,1)} %turn.1.refs_0_), channel_id=1, source_target_pairs={{0,1},{1,0},{2,3},{3,2},{4,5},{5,4},{6,7},{7,6},{8,9},{9,8},{10,11... | collective-permute-start | bytes 737288 | tf_op jit(solution)/shard_map/ppermute | solution.py:199
  15.5 15.4 %collective-permute-start.2 = (bf16[160,768]{1,0:T(8,128)(2,1)}, bf16[160,768]{1,0:T(8,128)(2,1)S(1)}, u32[]{:S(2)}, u32[]{:S(2)}) collective-permute-start(bf16[160,768]{1,0:T(8,128)(2,1)} %turn.1.refs_0_), channel_id=1, source_target_pairs={{0,2},{1,3},{2,4},{3,5},{4,6},{5,7},{6,0},{7,1},{8,10},{9,11},{10,... | collective-permute-start | bytes 737288 | tf_op jit(solution)/shard_map/ppermute | solution.py:201
  18.0 28.2 %collective-permute-start.3 = (bf16[160,768]{1,0:T(8,128)(2,1)}, bf16[160,768]{1,0:T(8,128)(2,1)S(1)}, u32[]{:S(2)}, u32[]{:S(2)}) collective-permute-start(bf16[160,768]{1,0:T(8,128)(2,1)} %turn.1.refs_0_), channel_id=1, source_target_pairs={{0,6},{1,7},{2,0},{3,1},{4,2},{5,3},{6,4},{7,5},{8,14},{9,15},{10,... | collective-permute-start | bytes 737288 | tf_op jit(solution)/shard_map/ppermute | solution.py:201
  18.8 27.5 %collective-permute-start.4 = (bf16[160,768]{1,0:T(8,128)(2,1)}, bf16[160,768]{1,0:T(8,128)(2,1)S(1)}, u32[]{:S(2)}, u32[]{:S(2)}) collective-permute-start(bf16[160,768]{1,0:T(8,128)(2,1)} %turn.1.refs_0_), channel_id=1, source_target_pairs={{0,4},{1,5},{2,6},{3,7},{4,0},{5,1},{6,2},{7,3},{8,12},{9,13},{10,... | collective-permute-start | bytes 737288 | tf_op jit(solution)/shard_map/ppermute | solution.py:201
  28.2 18.1 %collective-permute-start.5 = (bf16[160,768]{1,0:T(8,128)(2,1)S(1)}, bf16[160,768]{1,0:T(8,128)(2,1)}, u32[]{:S(2)}, u32[]{:S(2)}) collective-permute-start(bf16[160,768]{1,0:T(8,128)(2,1)S(1)} %collective-permute-done.1.refs_1_), channel_id=1, source_target_pairs={{0,2},{1,3},{2,4},{3,5},{4,6},{5,7},{6,0},{7,1},{8,10},{9,11},{10,... | collective-permute-start | bytes 737288 | tf_op jit(solution)/shard_map/ppermute | solution.py:203
  29.1 17.2 %collective-permute-start.6 = (bf16[160,768]{1,0:T(8,128)(2,1)S(1)}, bf16[160,768]{1,0:T(8,128)(2,1)}, u32[]{:S(2)}, u32[]{:S(2)}) collective-permute-start(bf16[160,768]{1,0:T(8,128)(2,1)S(1)} %collective-permute-done.1.refs_1_), channel_id=1, source_target_pairs={{0,6},{1,7},{2,0},{3,1},{4,2},{5,3},{6,4},{7,5},{8,14},{9,15},{10,... | collective-permute-start | bytes 737288 | tf_op jit(solution)/shard_map/ppermute | solution.py:203
  30.9 15.4 %collective-permute-start.7 = (bf16[160,768]{1,0:T(8,128)(2,1)S(1)}, bf16[160,768]{1,0:T(8,128)(2,1)}, u32[]{:S(2)}, u32[]{:S(2)}) collective-permute-start(bf16[160,768]{1,0:T(8,128)(2,1)S(1)} %collective-permute-done.1.refs_1_), channel_id=1, source_target_pairs={{0,4},{1,5},{2,6},{3,7},{4,0},{5,1},{6,2},{7,3},{8,12},{9,13},{10,... | collective-permute-start | bytes 737288 | tf_op jit(solution)/shard_map/ppermute | solution.py:203
  37.9 17.0 %all-to-all-start = ((bf16[8,80,256]{2,1,0:T(8,128)(2,1)}), bf16[8,80,256]{2,1,0:T(8,128)(2,1)S(1)}, u32[]{:S(2)}, u32[]{:S(2)}) async-start(bf16[8,80,256]{2,1,0:T(8,128)(2,1)} %heads.1), calls=%async_computation | async-start | bytes 655360 | tf_op jit(solution)/shard_map/all_to_all | solution.py:261
  53.0 7.9 %collective-permute-start.8 = (bf16[320,768]{1,0:T(8,128)(2,1)}, bf16[320,768]{1,0:T(8,128)(2,1)S(1)}, u32[]{:S(2)}, u32[]{:S(2)}) collective-permute-start(bf16[320,768]{1,0:T(8,128)(2,1)} %get-tuple-element.17.own_ref), channel_id=1, source_target_pairs={{0,8},{8,0},{1,9},{9,1},{2,10},{10,2},{3,11},{11,3},{4,12},{12,4},... | collective-permute-start | bytes 1474568 | tf_op jit(solution)/shard_map/ppermute | solution.py:318
  55.0 14.8 %collective-permute-start.16 = (bf16[80,256]{1,0:T(8,128)(2,1)S(1)}, bf16[80,256]{1,0:T(8,128)(2,1)S(1)}, u32[]{:S(2)}, u32[]{:S(2)}) collective-permute-start(bf16[80,256]{1,0:T(8,128)(2,1)S(1)} %reduce_sum.62), channel_id=1, source_target_pairs={{0,16},{16,32},{32,48},{48,0},{64,80},{80,96},{96,112},{112,64},{1... | collective-permute-start | bytes 122888 | tf_op jit(solution)/shard_map/ppermute | solution.py:273
  57.4 14.1 %collective-permute-start.17 = (bf16[80,256]{1,0:T(8,128)(2,1)S(1)}, bf16[80,256]{1,0:T(8,128)(2,1)S(1)}, u32[]{:S(2)}, u32[]{:S(2)}) collective-permute-start(bf16[80,256]{1,0:T(8,128)(2,1)S(1)} %reduce_sum.62), channel_id=1, source_target_pairs={{0,32},{16,48},{32,0},{48,16},{64,96},{80,112},{96,64},{112,80},{1... | collective-permute-start | bytes 122888 | tf_op jit(solution)/shard_map/ppermute | solution.py:273
  58.0 18.6 %collective-permute-start.18 = (bf16[80,256]{1,0:T(8,128)(2,1)S(1)}, bf16[80,256]{1,0:T(8,128)(2,1)S(1)}, u32[]{:S(2)}, u32[]{:S(2)}) collective-permute-start(bf16[80,256]{1,0:T(8,128)(2,1)S(1)} %reduce_sum.62), channel_id=1, source_target_pairs={{0,48},{16,0},{32,16},{48,32},{64,112},{80,64},{96,80},{112,96},{1... | collective-permute-start | bytes 122888 | tf_op jit(solution)/shard_map/ppermute | solution.py:273
  66.9 9.9 %collective-permute-start.10 = (bf16[160,768]{1,0:T(8,128)(2,1)}, bf16[160,768]{1,0:T(8,128)(2,1)S(1)}, u32[]{:S(2)}, u32[]{:S(2)}) collective-permute-start(bf16[160,768]{1,0:T(8,128)(2,1)} %encoder_attend.1.refs_8_), channel_id=1, source_target_pairs={{0,2},{1,3},{2,4},{3,5},{4,6},{5,7},{6,0},{7,1},{8,10},{9,11},{10,... | collective-permute-start | bytes 737288 | tf_op jit(solution)/shard_map/ppermute | solution.py:201
  68.6 12.2 %collective-permute-start.11 = (bf16[160,768]{1,0:T(8,128)(2,1)}, bf16[160,768]{1,0:T(8,128)(2,1)S(1)}, u32[]{:S(2)}, u32[]{:S(2)}) collective-permute-start(bf16[160,768]{1,0:T(8,128)(2,1)} %encoder_attend.1.refs_8_), channel_id=1, source_target_pairs={{0,6},{1,7},{2,0},{3,1},{4,2},{5,3},{6,4},{7,5},{8,14},{9,15},{10,... | collective-permute-start | bytes 737288 | tf_op jit(solution)/shard_map/ppermute | solution.py:201
  69.8 12.9 %collective-permute-start.12 = (bf16[160,768]{1,0:T(8,128)(2,1)}, bf16[160,768]{1,0:T(8,128)(2,1)S(1)}, u32[]{:S(2)}, u32[]{:S(2)}) collective-permute-start(bf16[160,768]{1,0:T(8,128)(2,1)} %encoder_attend.1.refs_8_), channel_id=1, source_target_pairs={{0,4},{1,5},{2,6},{3,7},{4,0},{5,1},{6,2},{7,3},{8,12},{9,13},{10,... | collective-permute-start | bytes 737288 | tf_op jit(solution)/shard_map/ppermute | solution.py:201
  71.6 12.4 %collective-permute-start.9 = (bf16[160,768]{1,0:T(8,128)(2,1)}, bf16[160,768]{1,0:T(8,128)(2,1)S(1)}, u32[]{:S(2)}, u32[]{:S(2)}) collective-permute-start(bf16[160,768]{1,0:T(8,128)(2,1)} %encoder_attend.1.refs_8_), channel_id=1, source_target_pairs={{0,1},{1,0},{2,3},{3,2},{4,5},{5,4},{6,7},{7,6},{8,9},{9,8},{10,11... | collective-permute-start | bytes 737288 | tf_op jit(solution)/shard_map/ppermute | solution.py:199
  76.7 10.0 %collective-permute-start.19 = (bf16[4,80,256]{2,1,0:T(8,128)(2,1)S(1)}, bf16[4,80,256]{2,1,0:T(8,128)(2,1)S(1)}, u32[]{:S(2)}, u32[]{:S(2)}) collective-permute-start(bf16[4,80,256]{2,1,0:T(8,128)(2,1)S(1)} %pad_maximum_fusion.2), channel_id=1, source_target_pairs={{0,64},{16,80},{32,96},{48,112},{64,128},{80,144},{96,160},{112,17... | collective-permute-start | bytes 491528 | tf_op jit(solution)/shard_map/ppermute | solution.py:273
  76.8 9.9 %collective-permute-start.20 = (bf16[4,80,256]{2,1,0:T(8,128)(2,1)S(1)}, bf16[4,80,256]{2,1,0:T(8,128)(2,1)S(1)}, u32[]{:S(2)}, u32[]{:S(2)}) collective-permute-start(bf16[4,80,256]{2,1,0:T(8,128)(2,1)S(1)} %pad_maximum_fusion.2), channel_id=1, source_target_pairs={{0,128},{16,144},{32,160},{48,176},{64,192},{80,208},{96,224},{112... | collective-permute-start | bytes 491528 | tf_op jit(solution)/shard_map/ppermute | solution.py:273
  84.0 6.6 %collective-permute-start.13 = (bf16[160,768]{1,0:T(8,128)(2,1)S(1)}, bf16[160,768]{1,0:T(8,128)(2,1)S(1)}, u32[]{:S(2)}, u32[]{:S(2)}) collective-permute-start(bf16[160,768]{1,0:T(8,128)(2,1)S(1)} %collective-permute-done.9.refs_9_), channel_id=1, source_target_pairs={{0,2},{1,3},{2,4},{3,5},{4,6},{5,7},{6,0},{7,1},{8,10},{9,11},{10,... | collective-permute-start | bytes 737288 | tf_op jit(solution)/shard_map/ppermute | solution.py:203
  84.2 8.2 %collective-permute-start.14 = (bf16[160,768]{1,0:T(8,128)(2,1)S(1)}, bf16[160,768]{1,0:T(8,128)(2,1)S(1)}, u32[]{:S(2)}, u32[]{:S(2)}) collective-permute-start(bf16[160,768]{1,0:T(8,128)(2,1)S(1)} %collective-permute-done.9.refs_9_), channel_id=1, source_target_pairs={{0,6},{1,7},{2,0},{3,1},{4,2},{5,3},{6,4},{7,5},{8,14},{9,15},{10,... | collective-permute-start | bytes 737288 | tf_op jit(solution)/shard_map/ppermute | solution.py:203
  86.6 6.6 %collective-permute-start.15 = (bf16[160,768]{1,0:T(8,128)(2,1)S(1)}, bf16[160,768]{1,0:T(8,128)(2,1)S(1)}, u32[]{:S(2)}, u32[]{:S(2)}) collective-permute-start(bf16[160,768]{1,0:T(8,128)(2,1)S(1)} %collective-permute-done.9.refs_9_), channel_id=1, source_target_pairs={{0,4},{1,5},{2,6},{3,7},{4,0},{5,1},{6,2},{7,3},{8,12},{9,13},{10,... | collective-permute-start | bytes 737288 | tf_op jit(solution)/shard_map/ppermute | solution.py:203
  94.1 10.6 %collective-permute-start.22 = (bf16[1280,256]{1,0:T(8,128)(2,1)S(1)}, bf16[1280,256]{1,0:T(8,128)(2,1)S(1)}, u32[]{:S(2)}, u32[]{:S(2)}) collective-permute-start(bf16[1280,256]{1,0:T(8,128)(2,1)S(1)} %bitcast.76), channel_id=1, source_target_pairs={{0,8},{8,0},{1,9},{9,1},{2,10},{10,2},{3,11},{11,3},{4,12},{12,4},... | collective-permute-start | bytes 1966088 | tf_op jit(solution)/shard_map/ppermute | solution.py:339
  111.9 35.6 %all-to-all-start.1 = ((bf16[16,128,256]{2,1,0:T(8,128)(2,1)}), bf16[16,128,256]{2,1,0:T(8,128)(2,1)S(1)}, u32[]{:S(2)}, u32[]{:S(2)}) async-start(bf16[16,128,256]{2,1,0:T(8,128)(2,1)} %bitcast.74), calls=%async_computation.1 | async-start | bytes 2097152 | tf_op jit(solution)/shard_map/all_to_all | solution.py:382
  (27 other events, 224.0 us)

commit v3 on v2

--- a/solution.py
+++ b/solution.py
@@ -54,12 +54,12 @@
     out_ref[...] = dot(eye, x_ref[...], ((1,), (1,))).astype(BF)
 
 
-def qkv_kernel(off_ref, *refs):
+def qkv_kernel(at_ref, *refs):
     shards = refs[:8]
     w_ref, gain_ref, q_ref, kv_ref, full, sems = refs[8:]
     part, rows = shards[0].shape
     width = part * 8
-    fill(off_ref, shards, (full,), (sems,))
+    fill(at_ref, shards, (full,), (sems,))
     cut = 256
     for j in range(rows // cut):
         lanes = slice(j * cut, (j + 1) * cut)
@@ -85,7 +85,7 @@
     part, rows = q_ref.shape
     heads = 2
     hd = part // heads
-    pipe = pipe_ref[0]
+    pipe, first = pipe_ref[0], pipe_ref[1] * (rows // 64)
     key = lax.broadcasted_iota(jnp.int32, (256, 1), 0)
     from_other = key // 128
     key_image = (key % 128) // 64
@@ -93,7 +93,7 @@
     lane_image = lax.broadcasted_iota(jnp.int32, (1, 128), 1) // 64
     for j in range(rows // 128):
         lanes = slice(j * 128, (j + 1) * 128)
-        count = jnp.where(lane_image == 0, count_ref[2 * j], count_ref[2 * j + 1])
+        count = jnp.where(lane_image == 0, count_ref[first + 2 * j], count_ref[first + 2 * j + 1])
         valid = (key_image == lane_image) & (tile < count)
         for h in range(heads):
             k_at = slice(h * hd, (h + 1) * hd)
@@ -107,11 +107,17 @@
             out_ref[k_at, lanes] = jnp.dot(values, probs, preferred_element_type=F32).astype(BF)
 
 
-def fill(off_ref, shards, fulls, sems):
+def gather_order(t):
+    a, b, c = (t + 6) % 8, (t + 2) % 8, (t + 4) % 8
+    return [t, t ^ 1, a, b, c, a ^ 1, b ^ 1, c ^ 1]
+
+
+def fill(at_ref, shards, fulls, sems):
     part = shards[0].shape[0]
     copies = []
+    order = gather_order(at_ref[2])
     for i, s in enumerate(shards):
-        at = pl.ds(pl.multiple_of(off_ref[i % 8] * part, 16), part)
+        at = pl.ds(pl.multiple_of(order[i % 8] * part, 16), part)
         copies.append(pltpu.make_async_copy(s, fulls[i // 8].at[at, :], sems[i // 8].at[i % 8]))
     for c in copies:
         c.start()
@@ -119,16 +125,16 @@
         c.wait()
 
 
-def memory_kernel(off_ref, pick_ref, pipe_ref, *refs):
+def memory_kernel(at_ref, pick_ref, *refs):
     xs, ms = refs[:8], refs[8:16]
-    own_ref, other_ref, gain_ref, out_ref, x_ref, m_ref, rows_ref, x_sems, m_sems = refs[16:]
-    fill(off_ref, xs + ms, (x_ref, m_ref), (x_sems, m_sems))
-    half = own_ref.shape[0] // 2
-    mine = pl.ds(pl.multiple_of(pipe_ref[0] * half, 128), half)
-    rest = pl.ds(pl.multiple_of((1 - pipe_ref[0]) * half, 128), half)
-    first = ((0,), (0,))
-    kv = dot(own_ref[:half], x_ref[mine, :], first) + dot(other_ref[:half], x_ref[rest, :], first)
-    kv += dot(own_ref[half:], m_ref[mine, :], first) + dot(other_ref[half:], m_ref[rest, :], first)
+    w_ref, gain_ref, out_ref, x_ref, m_ref, rows_ref, x_sems, m_sems = refs[16:]
+    fill(at_ref, xs + ms, (x_ref, m_ref), (x_sems, m_sems))
+    half = w_ref.shape[0] // 4
+    mine = pl.ds(pl.multiple_of(at_ref[0] * half, 128), half)
+    rest = pl.ds(pl.multiple_of((1 - at_ref[0]) * half, 128), half)
+    kv = jnp.zeros((2 * HD, rows_ref.shape[0]), F32)
+    for i, rows in enumerate((x_ref[mine, :], m_ref[mine, :], x_ref[rest, :], m_ref[rest, :])):
+        kv += dot(w_ref[i * half : (i + 1) * half], rows, ((0,), (0,)))
     keys = kv[:HD]
     keys = keys * lax.rsqrt(jnp.mean(keys * keys, 0, keepdims=True) + 1e-05) * gain_ref[...]
     rows_ref[:, :HD] = jnp.transpose(keys).astype(BF)
@@ -194,19 +200,13 @@
     return [(t, (t + 2 * d) % 8) for t in range(8)]
 
 
-def gather8(s, near=None):
+def gather8(s, near, hold):
     p1, p2, p3 = y_perm(1), y_perm(2), y_perm(3)
     z = lax.ppermute(s, "tensor", ZX)
-    s = s if near is None else near
-    a, b, c = (lax.ppermute(s, "tensor", p) for p in (p1, p3, p2))
-    z = after(z, *((a, b, c) if near is None else ()))
+    a, b, c = (lax.ppermute(near, "tensor", p) for p in (p1, p3, p2))
+    z = after(z, *hold(a, b, c))
     za, zb, zc = (lax.ppermute(z, "tensor", p) for p in (p1, p3, p2))
     return (s, z, a, b, c, za, zb, zc)
-
-
-def gather_order(t):
-    a, b, c = (t + 6) % 8, (t + 2) % 8, (t + 4) % 8
-    return jnp.stack([t, t ^ 1, a, b, c, a ^ 1, b ^ 1, c ^ 1]).astype(jnp.int32)
 
 
 def after(value, *others):
@@ -243,13 +243,13 @@
         out_ref[h, :, HD:] = part_ref[1, :, h * HD : (h + 1) * HD]
 
 
-def fold_weights(few, proj_w, cross_kv_w, replica, pipe, hold, late):
+def fold_weights(few, proj_w, cross_kv_w, replica, pipe):
     per = ENC_W // 32
     folded = jnp.dot(few, proj_w, preferred_element_type=F32).astype(BF)
     left = lax.dynamic_slice_in_dim(proj_w, (pipe * 16 + replica) * per, per)
-    left = after(jnp.concatenate([left, folded], 0), *hold)
+    left = jnp.concatenate([left, folded], 0)
     part = jnp.einsum("rk,kcn->crn", left, cross_kv_w, preferred_element_type=F32).astype(BF)
-    blocks = call(
+    return call(
         heads_kernel,
         shape_of((KV_HEADS, 2 * per, 2 * HD), BF),
         [VMEM],
@@ -258,7 +258,6 @@
         2 * part.size * 2,
         "heads",
     )(part)
-    return lax.all_to_all(after(blocks, *late), "tensor", split_axis=0, concat_axis=0, tiled=True)
 
 
 def line_shift(d):
@@ -296,14 +295,15 @@
     tensor = lax.axis_index("tensor")
     images, held, tile_rows, part = patches.shape
     rows = images * held * tile_rows
-    order = gather_order(tensor)
-    pipe_at = pipe.reshape(1).astype(jnp.int32)
+    pipe_at = jnp.stack([pipe, group, tensor]).astype(jnp.int32)
 
     turned = call(
         turn_kernel, shape_of((part, rows), BF), [VMEM], [], 2 * rows * part * part, 4 * rows * part, "turn"
     )(patches.reshape(rows, part))
     few = out_rows(enc_out_w, group, pipe)
-    xs = gather8(turned, after(turned, few))
+    blocks = fold_weights(few, proj_w, cross_kv_w, group, pipe)
+    norm_gain = ln_gain.reshape(ENC_W, 1)
+    xs = gather8(turned, after(turned, few, norm_gain), lambda *_: (blocks,))
 
     turned_w = enc_qkv.transpose(1, 2, 0).reshape(3 * part, ENC_W)
     q, kv = call(
@@ -314,9 +314,8 @@
         2 * rows * ENC_W * 3 * part,
         6 * 1024 * 1024,
         "qkv",
-    )(order, *xs, turned_w, ln_gain.reshape(ENC_W, 1))
+    )(pipe_at, *xs, turned_w, norm_gain)
     kv_other = lax.ppermute(kv, "pipe", [(0, 1), (1, 0)])
-    counts_local = lax.dynamic_slice_in_dim(tile_counts, group * images, images)
     mixed = call(
         attend_kernel,
         shape_of((part, rows), BF),
@@ -325,20 +324,20 @@
         4 * rows * 256 * part,
         2 * 1024 * 1024,
         "encoder_attend",
-    )(counts_local, pipe_at, q, kv, kv_other)
-
-    parts = fold_weights(few, proj_w, cross_kv_w, group, pipe, (), ())
+    )(tile_counts, pipe_at, q, kv, kv_other)
+
+    parts = lax.all_to_all(blocks, "tensor", split_axis=0, concat_axis=0, tiled=True)
     piece = jnp.sum(after(parts, kv).astype(F32), 0).astype(BF)
     line = ring_of(piece, line_shift)
-    ms = gather8(mixed)
-    plane = ring_of(after(line, mixed), plane_shift)
+    ms = gather8(mixed, mixed, lambda *abc: abc)
+    line_other = lax.ppermute(line, "pipe", [(0, 1), (1, 0)])
+    plane = ring_of(after(jnp.stack([line, line_other]), mixed), plane_shift)
     spot = jnp.arange(16)
     spot = (group // 4 - spot // 4) % 4 * 4 + (group - spot) % 4
-    pieces = jnp.take(after(plane, *ms[5:]).reshape(16, 2, -1, 2 * HD), spot, axis=0)
-    pieces = jnp.moveaxis(pieces, 1, 0).reshape(ENC_W, 2 * HD)
-    pieces_other = lax.ppermute(pieces, "pipe", [(0, 1), (1, 0)])
-
-    destination = plan[:, 0]
+    plane = jnp.moveaxis(plane, 1, 0).reshape(2, 16, 2, -1, 2 * HD)
+    pieces = jnp.moveaxis(jnp.take(plane, spot, axis=1), 2, 1).reshape(2 * ENC_W, 2 * HD)
+
+    destination = after(plan, ms[1])[:, 0]
     grouped = destination.reshape(replicas, images)
     earlier = jnp.arange(images)[:, None] < jnp.arange(images)[None, :]
     same_dest = grouped[:, :, None] == grouped[:, None, :]
@@ -363,11 +362,11 @@
     slot_of = (every // images) * CAP + ranks.reshape(-1)
     slot_ids = jnp.sum(jnp.where(hit, slot_of[None, :], 0), 1).astype(jnp.int32)
     counts_rows = jnp.sum(jnp.where(hit, tile_counts[None, :], 0), 1).astype(jnp.int32)
-
+    gain = k_gain.reshape(HD, 1)
     slots = call(
         memory_kernel,
         shape_of((replicas * CAP * held * tile_rows, 2 * HD), BF),
-        [SMEM] * 3 + [ANY] * 16 + [VMEM] * 3,
+        [SMEM] * 2 + [ANY] * 16 + [VMEM] * 2,
         [
             pltpu.VMEM((ENC_W, rows), BF),
             pltpu.VMEM((ENC_W, rows), BF),
@@ -378,7 +377,7 @@
         4 * rows * ENC_W * 2 * HD,
         6 * 1024 * 1024,
         "memory",
-    )(order, picks, pipe_at, *xs, *ms, pieces, pieces_other, k_gain.reshape(HD, 1))
+    )(pipe_at, picks, *xs, *ms, pieces, gain)
     arrived = lax.all_to_all(slots, "replica", split_axis=0, concat_axis=0, tiled=True)
     q_self, q_cross, cache_kv, new_kv, kv_len = (after(v, slots) for v in (q_self, q_cross, cache_kv, new_kv, kv_len))
     rows_here = row_pick.shape[0]

time: 156 us -> 154 us (0.987)
  starting transfers between devices: 68.1 us -> 66.5 us
    ppermute x2, waiting for transfers between devices: 7.2 us -> 0.01 us  [gather8(): z = lax.ppermute(s, 'tensor', ZX)]
    ppermute x6, waiting for transfers between devices: 0.02 us -> 6.43 us  [ring_of(): lax.ppermute(piece, 'replica', shift(d))]
    ppermute x6, waiting for transfers between devices: 6.36 us -> 0.02 us  [gather8(): za, zb, zc = (lax.ppermute(z, 'tensor', p) for p in (p1, p3, p2))]
    ppermute x7, waiting for transfers between devices: 0.02 us -> 5.76 us  [the longest x6 5.75 us: gather8(): a, b, c = (lax.ppermute(near, 'tensor', p) for p in (p1, p3, p2))]
    ppermute x7, starting transfers between devices: 16.2 us -> 11.8 us  [the longest x6 7.08 us: gather8(): a, b, c = (lax.ppermute(near, 'tensor', p) for p in (p1, p3, p2))]
    ppermute x6, starting transfers between devices: 11.3 us -> 7.68 us  [ring_of(): lax.ppermute(piece, 'replica', shift(d))]
    all_to_all x1, starting transfers between devices: 8.38 us -> 10.8 us  [shards(): lax.all_to_all(slots, 'replica', split_axis=0, concat_axis=0, tiled=True)]
    ppermute x1, starting transfers between devices: 1.75 us -> 4.02 us  [shards(): kv_other = lax.ppermute(kv, 'pipe', [(0, 1), (1, 0)])]
  transfers between devices with their start and end apart: 26 -> 26, of which waited for: 8 -> 7; matrix products, arithmetic and copies ran while one was open for 14% -> 15% of each run, Pallas kernels for 11% -> 12%
where the time goes in v3:
time: 154 us; the launch traced here: 153 us
  starting transfers between devices  66.5 us (43%)
  waiting for transfers between devices  30.7 us (20%)
  Pallas kernels  27.4 us (18%)
  local copies, waits for them, and re-layouts  13.4 us (9%)
  matrix products  6.64 us (4%)
  other arithmetic  5.71 us (4%)
  between operations  2.46 us (2%)
    all_to_all x1, waiting for transfers between devices, shards(): lax.all_to_all(slots, 'replica', split_axis=0, concat_axis=0, tiled=True)  16.9 us
    all_to_all x1, starting transfers between devices, shards(): lax.all_to_all(slots, 'replica', split_axis=0, concat_axis=0, tiled=True)  10.8 us
    ppermute x1, starting transfers between devices, out_rows(): return lax.ppermute(mine, ('replica', 'pipe', 'tensor'), pairs)  8.87 us
    all_to_all x1, starting transfers between devices, shards(): lax.all_to_all(blocks, 'tensor', split_axis=0, concat_axis=0, tiled=True)  7.82 us
    ppermute x6, starting transfers between devices, ring_of(): lax.ppermute(piece, 'replica', shift(d))  7.68 us
    ppermute x2, starting transfers between devices, gather8(): z = lax.ppermute(s, 'tensor', ZX)  7.11 us
    ppermute x6, starting transfers between devices, gather8(): a, b, c = (lax.ppermute(near, 'tensor', p) for p in (p1, p3, p2))  7.08 us
    ppermute x6, starting transfers between devices, gather8(): za, zb, zc = (lax.ppermute(z, 'tensor', p) for p in (p1, p3, p2))  6.72 us
  transfers between devices with their start and end apart: 26, of which 7 were waited for; matrix products, arithmetic and copies ran while one was open for 15% of the time, Pallas kernels for 12%

profile of v3, /device:TPU:1, one launch (start us, length us, event | category | flops | bytes accessed | tf_op | source)
XLA Modules:
  0.0 152.9 jit_solution(7122283754831166622)
XLA Ops:
  1.6 8.9 %collective-permute-start.1 = (bf16[40,1280]{1,0:T(8,128)(2,1)S(1)}, bf16[40,1280]{1,0:T(8,128)(2,1)S(1)}, u32[]{:S(2)}, u32[]{:S(2)}) collective-permute-start(bf16[40,1280]{1,0:T(8,128)(2,1)S(1)} %constant_dynamic-slice_fusion.2), channel_id=1, source_target_pairs={{0,0},{56,1},{64,2},{120,3},{128,4},{184,5},{192,6},{248,7},{4,8},... | collective-permute-start | bytes 307208 | tf_op jit(solution)/shard_map/ppermute | solution.py:237
  10.5 2.0 %turn.1.refs_0_ = bf16[160,768]{1,0:T(8,128)(2,1)} custom-call(bf16[768,160]{1,0:T(8,128)(2,1)} %bitcast.86), custom_call_target="tpu_custom_call" | custom-call | flops 39321600 | bytes 491520 | tf_op jit(solution)/shard_map/turn/pallas_call | solution.py:300
  12.5 2.1 %collective-permute-start = (bf16[160,768]{1,0:T(8,128)(2,1)}, bf16[160,768]{1,0:T(8,128)(2,1)S(1)}, u32[]{:S(2)}, u32[]{:S(2)}) collective-permute-start(bf16[160,768]{1,0:T(8,128)(2,1)} %turn.1.refs_0_), channel_id=1, source_target_pairs={{0,1},{1,0},{2,3},{3,2},{4,5},{5,4},{6,7},{7,6},{8,9},{9,8},{10,11... | collective-permute-start | bytes 737288 | tf_op jit(solution)/shard_map/ppermute | solution.py:205
  16.2 2.5 %collective-permute-start.2 = (bf16[160,768]{1,0:T(8,128)(2,1)}, bf16[160,768]{1,0:T(8,128)(2,1)S(1)}, u32[]{:S(2)}, u32[]{:S(2)}) collective-permute-start(bf16[160,768]{1,0:T(8,128)(2,1)} %turn.1.refs_0_), channel_id=1, source_target_pairs={{0,2},{1,3},{2,4},{3,5},{4,6},{5,7},{6,0},{7,1},{8,10},{9,11},{10,... | collective-permute-start | bytes 737288 | tf_op jit(solution)/shard_map/ppermute | solution.py:206
  20.6 2.3 %convolution_convert_fusion = bf16[40,1024]{1,0:T(8,128)(2,1)S(1)} fusion(bf16[40,1280]{1,0:T(8,128)(2,1)S(1)} %collective-permute-done.1, bf16[1280,1024]{1,0:T(8,128)(2,1)} %param.20), kind=kOutput, calls=%fused_computation.7 | convolution fusion | flops 104898560 | bytes 2805760 | tf_op jit(solution)/shard_map/dot_general | solution.py:248
  22.9 4.3 %fusion.5.part_ref = bf16[2,80,1024]{2,1,0:T(8,128)(2,1)} fusion(bf16[1024,2,1024]{2,1,0:T(2,128)(2,1)} %param.21, bf16[40,1024]{1,0:T(8,128)(2,1)S(1)} %convolution_convert_fusion, bf16[40,1024]{1,0:T(8,128)(2,1)S(1)} %constant_dynamic-slice_fusion.3), kind=kOutput, calls=%fused_computation.6 | convolution fusion | flops 336035840 | bytes 4685824 | tf_op jit(solution)/shard_map/rk,kcn->crn/dot_general | solution.py:251
  29.8 1.9 %collective-permute-start.6 = (bf16[160,768]{1,0:T(8,128)(2,1)S(1)}, bf16[160,768]{1,0:T(8,128)(2,1)S(1)}, u32[]{:S(2)}, u32[]{:S(2)}) collective-permute-start(bf16[160,768]{1,0:T(8,128)(2,1)S(1)} %collective-permute-done.refs_1_), channel_id=1, source_target_pairs={{0,6},{1,7},{2,0},{3,1},{4,2},{5,3},{6,4},{7,5},{8,14},{9,15},{10,... | collective-permute-start | bytes 737288 | tf_op jit(solution)/shard_map/ppermute | solution.py:208
  32.3 7.8 %all-to-all-start = ((bf16[8,80,256]{2,1,0:T(8,128)(2,1)}), bf16[8,80,256]{2,1,0:T(8,128)(2,1)S(1)}, u32[]{:S(2)}, u32[]{:S(2)}) async-start(bf16[8,80,256]{2,1,0:T(8,128)(2,1)} %heads.1), calls=%async_computation | async-start | bytes 655360 | tf_op jit(solution)/shard_map/all_to_all | solution.py:329
  43.5 6.0 %qkv.1 = (bf16[160,768]{1,0:T(8,128)(2,1)}, bf16[320,768]{1,0:T(8,128)(2,1)}) custom-call(s32[3]{0:T(128)} %pad_add_fusion.at_ref.pipe_ref, bf16[160,768]{1,0:T(8,128)(2,1)} %turn.1.refs_0_, bf16[160,768]{1,0:T(8,128)(2,1)} %copy-done.2, bf16[160,768]{1,0:T(8,128)(2,1)} %copy-done.3, bf16[160,768]{1,0:T(8,128)(2,1)} %copy-done.4, ...), custom_call_target="tpu_custom_call" | custom-call | flops 943718400 | bytes 6291456 | tf_op jit(solution)/shard_map/qkv/pallas_call | solution.py:309
  49.4 4.0 %collective-permute-start.8 = (bf16[320,768]{1,0:T(8,128)(2,1)}, bf16[320,768]{1,0:T(8,128)(2,1)S(1)}, u32[]{:S(2)}, u32[]{:S(2)}) collective-permute-start(bf16[320,768]{1,0:T(8,128)(2,1)} %get-tuple-element.19.own_ref), channel_id=1, source_target_pairs={{0,8},{8,0},{1,9},{9,1},{2,10},{10,2},{3,11},{11,3},{4,12},{12,4},... | collective-permute-start | bytes 1474568 | tf_op jit(solution)/shard_map/ppermute | solution.py:318
  53.5 2.6 %collective-permute-start.16 = (bf16[80,256]{1,0:T(8,128)(2,1)S(1)}, bf16[80,256]{1,0:T(8,128)(2,1)S(1)}, u32[]{:S(2)}, u32[]{:S(2)}) collective-permute-start(bf16[80,256]{1,0:T(8,128)(2,1)S(1)} %reduce_sum.62), channel_id=1, source_target_pairs={{0,16},{16,32},{32,48},{48,0},{64,80},{80,96},{96,112},{112,64},{1... | collective-permute-start | bytes 122888 | tf_op jit(solution)/shard_map/ppermute | solution.py:272
  56.7 2.3 %collective-permute-start.18 = (bf16[80,256]{1,0:T(8,128)(2,1)S(1)}, bf16[80,256]{1,0:T(8,128)(2,1)S(1)}, u32[]{:S(2)}, u32[]{:S(2)}) collective-permute-start(bf16[80,256]{1,0:T(8,128)(2,1)S(1)} %reduce_sum.62), channel_id=1, source_target_pairs={{0,48},{16,0},{32,16},{48,32},{64,112},{80,64},{96,80},{112,96},{1... | collective-permute-start | bytes 122888 | tf_op jit(solution)/shard_map/ppermute | solution.py:272
  60.1 4.7 %collective-permute-start.19 = (bf16[4,80,256]{2,1,0:T(8,128)(2,1)S(1)}, bf16[4,80,256]{2,1,0:T(8,128)(2,1)S(1)}, u32[]{:S(2)}, u32[]{:S(2)}) collective-permute-start(bf16[4,80,256]{2,1,0:T(8,128)(2,1)S(1)} %get-tuple-element.35), channel_id=1, source_target_pairs={{0,8},{8,0},{1,9},{9,1},{2,10},{10,2},{3,11},{11,3},{4,12},{12,4},... | collective-permute-start | bytes 491528 | tf_op jit(solution)/shard_map/ppermute | solution.py:333
  65.6 5.2 %encoder_attend.1.refs_8_ = bf16[160,768]{1,0:T(8,128)(2,1)} custom-call(s32[192]{0:T(256)} %count_ref.1, s32[3]{0:T(128)} %pad_add_fusion.at_ref.pipe_ref, bf16[160,768]{1,0:T(8,128)(2,1)} %get-tuple-element.18.q_ref, bf16[320,768]{1,0:T(8,128)(2,1)} %get-tuple-element.19.own_ref, bf16[320,768]{1,0:T(8,128)(2,1)} %copy-done.10), custom_call_target="tpu_custom_call" | custom-call | flops 125829120 | bytes 2097152 | tf_op jit(solution)/shard_map/encoder_attend/pallas_call | solution.py:319
  70.8 2.7 %collective-permute-start.11 = (bf16[160,768]{1,0:T(8,128)(2,1)}, bf16[160,768]{1,0:T(8,128)(2,1)S(1)}, u32[]{:S(2)}, u32[]{:S(2)}) collective-permute-start(bf16[160,768]{1,0:T(8,128)(2,1)} %encoder_attend.1.refs_8_), channel_id=1, source_target_pairs={{0,6},{1,7},{2,0},{3,1},{4,2},{5,3},{6,4},{7,5},{8,14},{9,15},{10,... | collective-permute-start | bytes 737288 | tf_op jit(solution)/shard_map/ppermute | solution.py:206
  73.5 5.0 %collective-permute-start.9 = (bf16[160,768]{1,0:T(8,128)(2,1)}, bf16[160,768]{1,0:T(8,128)(2,1)}, u32[]{:S(2)}, u32[]{:S(2)}) collective-permute-start(bf16[160,768]{1,0:T(8,128)(2,1)} %encoder_attend.1.refs_8_), channel_id=1, source_target_pairs={{0,1},{1,0},{2,3},{3,2},{4,5},{5,4},{6,7},{7,6},{8,9},{9,8},{10,11... | collective-permute-start | bytes 737288 | tf_op jit(solution)/shard_map/ppermute | solution.py:205
  79.4 5.7 %collective-permute-done.10.refs_10_ = bf16[160,768]{1,0:T(8,128)(2,1)S(1)} collective-permute-done((bf16[160,768]{1,0:T(8,128)(2,1)}, bf16[160,768]{1,0:T(8,128)(2,1)S(1)}, u32[]{:S(2)}, u32[]{:S(2)}) %collective-permute-start.10) | collective-permute-done | bytes 245792 | tf_op jit(solution)/shard_map/ppermute | solution.py:206
  87.4 2.7 %collective-permute-start.14 = (bf16[160,768]{1,0:T(8,128)(2,1)}, bf16[160,768]{1,0:T(8,128)(2,1)}, u32[]{:S(2)}, u32[]{:S(2)}) collective-permute-start(bf16[160,768]{1,0:T(8,128)(2,1)} %collective-permute-done.9.refs_9_), channel_id=1, source_target_pairs={{0,6},{1,7},{2,0},{3,1},{4,2},{5,3},{6,4},{7,5},{8,14},{9,15},{10,... | collective-permute-start | bytes 737288 | tf_op jit(solution)/shard_map/ppermute | solution.py:208
  95.3 3.7 %collective-permute-done.22 = bf16[2,4,80,256]{3,2,1,0:T(8,128)(2,1)S(1)} collective-permute-done((bf16[2,4,80,256]{3,2,1,0:T(8,128)(2,1)S(1)}, bf16[2,4,80,256]{3,2,1,0:T(8,128)(2,1)S(1)}, u32[]{:S(2)}, u32[]{:S(2)}) %collective-permute-start.22) | collective-permute-done | bytes 327712 | tf_op jit(solution)/shard_map/ppermute | solution.py:272
  101.2 6.3 %memory.1 = bf16[2048,256]{1,0:T(8,128)(2,1)} custom-call(s32[3]{0:T(128)} %pad_add_fusion.at_ref.pipe_ref, s32[32]{0:T(128)} %select_reduce_fusion.2.pick_ref, bf16[160,768]{1,0:T(8,128)(2,1)} %turn.1.refs_0_, bf16[160,768]{1,0:T(8,128)(2,1)} %copy-done.2, bf16[160,768]{1,0:T(8,128)(2,1)} %copy-done.3, bf16[160,768]{1,0:T(8,128)(2,1)} %copy-done.4, ...), custom_call_target="tpu_custom_call" | custom-call | flops 1006632960 | bytes 6291456 | tf_op jit(solution)/shard_map/memory/pallas_call | solution.py:366
  107.6 10.8 %all-to-all-start.1 = ((bf16[16,128,256]{2,1,0:T(8,128)(2,1)}), bf16[16,128,256]{2,1,0:T(8,128)(2,1)S(1)}, u32[]{:S(2)}, u32[]{:S(2)}) async-start(bf16[16,128,256]{2,1,0:T(8,128)(2,1)} %bitcast.81), calls=%async_computation.1 | async-start | bytes 2097152 | tf_op jit(solution)/shard_map/all_to_all | solution.py:381
  124.9 2.8 %self_attend.1 = bf16[2,32,1024]{2,1,0:T(8,128)(2,1)} custom-call(s32[512,1]{1,0:T(8,128)} %reshape_reshape.8.len_ref, bf16[32,16,128]{2,1,0:T(8,128)(2,1)} %copy_bitcast_fusion.q_ref, bf16[32,48,256]{2,1,0:T(8,128)(2,1)} %maximum_maximum_fusion.kv_ref), custom_call_target="tpu_custom_call" | custom-call | flops 33554432 | bytes 4194304 | tf_op jit(solution)/shard_map/self_attend/pallas_call | solution.py:409
  128.4 16.9 %all-to-all-done.1 = bf16[16,128,256]{2,1,0:T(8,128)(2,1)S(1)} async-done(((bf16[16,128,256]{2,1,0:T(8,128)(2,1)}), bf16[16,128,256]{2,1,0:T(8,128)(2,1)S(1)}, u32[]{:S(2)}, u32[]{:S(2)}) %all-to-all-start.1) | async-done | bytes 1048608 | tf_op jit(solution)/shard_map/all_to_all | solution.py:381
  149.5 3.4 %cross_attend.1 = bf16[2,32,1024]{2,1,0:T(8,128)(2,1)} custom-call(s32[32]{0:T(128)} %get-tuple-element.31.slot_ref, s32[3]{0:T(128)} %pad_add_fusion.at_ref.pipe_ref, s32[512,1]{1,0:T(8,128)} %copy.46.count_ref, bf16[32,16,128]{2,1,0:T(8,128)(2,1)} %copy_bitcast_fusion.1.q_ref, bf16[2048,256]{1,0:T(8,128)(2,1)} %bitcast.80, ...), custom_call_target="tpu_custom_call" | custom-call | flops 33554432 | bytes 4194304 | tf_op jit(solution)/shard_map/cross_attend/pallas_call | solution.py:422
  (131 shorter events, 33.8 us)
Async XLA Ops:
  1.6 14.6 %collective-permute-start.1 = (bf16[40,1280]{1,0:T(8,128)(2,1)S(1)}, bf16[40,1280]{1,0:T(8,128)(2,1)S(1)}, u32[]{:S(2)}, u32[]{:S(2)}) collective-permute-start(bf16[40,1280]{1,0:T(8,128)(2,1)S(1)} %constant_dynamic-slice_fusion.2), channel_id=1, source_target_pairs={{0,0},{56,1},{64,2},{120,3},{128,4},{184,5},{192,6},{248,7},{4,8},... | collective-permute-start | bytes 307208 | tf_op jit(solution)/shard_map/ppermute | solution.py:237
  12.5 16.5 %collective-permute-start = (bf16[160,768]{1,0:T(8,128)(2,1)}, bf16[160,768]{1,0:T(8,128)(2,1)S(1)}, u32[]{:S(2)}, u32[]{:S(2)}) collective-permute-start(bf16[160,768]{1,0:T(8,128)(2,1)} %turn.1.refs_0_), channel_id=1, source_target_pairs={{0,1},{1,0},{2,3},{3,2},{4,5},{5,4},{6,7},{7,6},{8,9},{9,8},{10,11... | collective-permute-start | bytes 737288 | tf_op jit(solution)/shard_map/ppermute | solution.py:205
  16.2 15.5 %collective-permute-start.2 = (bf16[160,768]{1,0:T(8,128)(2,1)}, bf16[160,768]{1,0:T(8,128)(2,1)S(1)}, u32[]{:S(2)}, u32[]{:S(2)}) collective-permute-start(bf16[160,768]{1,0:T(8,128)(2,1)} %turn.1.refs_0_), channel_id=1, source_target_pairs={{0,2},{1,3},{2,4},{3,5},{4,6},{5,7},{6,0},{7,1},{8,10},{9,11},{10,... | collective-permute-start | bytes 737288 | tf_op jit(solution)/shard_map/ppermute | solution.py:206
  18.7 23.2 %collective-permute-start.3 = (bf16[160,768]{1,0:T(8,128)(2,1)}, bf16[160,768]{1,0:T(8,128)(2,1)S(1)}, u32[]{:S(2)}, u32[]{:S(2)}) collective-permute-start(bf16[160,768]{1,0:T(8,128)(2,1)} %turn.1.refs_0_), channel_id=1, source_target_pairs={{0,6},{1,7},{2,0},{3,1},{4,2},{5,3},{6,4},{7,5},{8,14},{9,15},{10,... | collective-permute-start | bytes 737288 | tf_op jit(solution)/shard_map/ppermute | solution.py:206
  19.5 22.4 %collective-permute-start.4 = (bf16[160,768]{1,0:T(8,128)(2,1)}, bf16[160,768]{1,0:T(8,128)(2,1)S(1)}, u32[]{:S(2)}, u32[]{:S(2)}) collective-permute-start(bf16[160,768]{1,0:T(8,128)(2,1)} %turn.1.refs_0_), channel_id=1, source_target_pairs={{0,4},{1,5},{2,6},{3,7},{4,0},{5,1},{6,2},{7,3},{8,12},{9,13},{10,... | collective-permute-start | bytes 737288 | tf_op jit(solution)/shard_map/ppermute | solution.py:206
  29.0 12.9 %collective-permute-start.5 = (bf16[160,768]{1,0:T(8,128)(2,1)S(1)}, bf16[160,768]{1,0:T(8,128)(2,1)S(1)}, u32[]{:S(2)}, u32[]{:S(2)}) collective-permute-start(bf16[160,768]{1,0:T(8,128)(2,1)S(1)} %collective-permute-done.refs_1_), channel_id=1, source_target_pairs={{0,2},{1,3},{2,4},{3,5},{4,6},{5,7},{6,0},{7,1},{8,10},{9,11},{10,... | collective-permute-start | bytes 737288 | tf_op jit(solution)/shard_map/ppermute | solution.py:208
  29.8 12.1 %collective-permute-start.6 = (bf16[160,768]{1,0:T(8,128)(2,1)S(1)}, bf16[160,768]{1,0:T(8,128)(2,1)S(1)}, u32[]{:S(2)}, u32[]{:S(2)}) collective-permute-start(bf16[160,768]{1,0:T(8,128)(2,1)S(1)} %collective-permute-done.refs_1_), channel_id=1, source_target_pairs={{0,6},{1,7},{2,0},{3,1},{4,2},{5,3},{6,4},{7,5},{8,14},{9,15},{10,... | collective-permute-start | bytes 737288 | tf_op jit(solution)/shard_map/ppermute | solution.py:208
  31.7 10.3 %collective-permute-start.7 = (bf16[160,768]{1,0:T(8,128)(2,1)S(1)}, bf16[160,768]{1,0:T(8,128)(2,1)S(1)}, u32[]{:S(2)}, u32[]{:S(2)}) collective-permute-start(bf16[160,768]{1,0:T(8,128)(2,1)S(1)} %collective-permute-done.refs_1_), channel_id=1, source_target_pairs={{0,4},{1,5},{2,6},{3,7},{4,0},{5,1},{6,2},{7,3},{8,12},{9,13},{10,... | collective-permute-start | bytes 737288 | tf_op jit(solution)/shard_map/ppermute | solution.py:208
  32.3 21.1 %all-to-all-start = ((bf16[8,80,256]{2,1,0:T(8,128)(2,1)}), bf16[8,80,256]{2,1,0:T(8,128)(2,1)S(1)}, u32[]{:S(2)}, u32[]{:S(2)}) async-start(bf16[8,80,256]{2,1,0:T(8,128)(2,1)} %heads.1), calls=%async_computation | async-start | bytes 655360 | tf_op jit(solution)/shard_map/all_to_all | solution.py:329
  49.4 15.3 %collective-permute-start.8 = (bf16[320,768]{1,0:T(8,128)(2,1)}, bf16[320,768]{1,0:T(8,128)(2,1)S(1)}, u32[]{:S(2)}, u32[]{:S(2)}) collective-permute-start(bf16[320,768]{1,0:T(8,128)(2,1)} %get-tuple-element.19.own_ref), channel_id=1, source_target_pairs={{0,8},{8,0},{1,9},{9,1},{2,10},{10,2},{3,11},{11,3},{4,12},{12,4},... | collective-permute-start | bytes 1474568 | tf_op jit(solution)/shard_map/ppermute | solution.py:318
  53.5 5.5 %collective-permute-start.16 = (bf16[80,256]{1,0:T(8,128)(2,1)S(1)}, bf16[80,256]{1,0:T(8,128)(2,1)S(1)}, u32[]{:S(2)}, u32[]{:S(2)}) collective-permute-start(bf16[80,256]{1,0:T(8,128)(2,1)S(1)} %reduce_sum.62), channel_id=1, source_target_pairs={{0,16},{16,32},{32,48},{48,0},{64,80},{80,96},{96,112},{112,64},{1... | collective-permute-start | bytes 122888 | tf_op jit(solution)/shard_map/ppermute | solution.py:272
  60.1 19.2 %collective-permute-start.19 = (bf16[4,80,256]{2,1,0:T(8,128)(2,1)S(1)}, bf16[4,80,256]{2,1,0:T(8,128)(2,1)S(1)}, u32[]{:S(2)}, u32[]{:S(2)}) collective-permute-start(bf16[4,80,256]{2,1,0:T(8,128)(2,1)S(1)} %get-tuple-element.35), channel_id=1, source_target_pairs={{0,8},{8,0},{1,9},{9,1},{2,10},{10,2},{3,11},{11,3},{4,12},{12,4},... | collective-permute-start | bytes 491528 | tf_op jit(solution)/shard_map/ppermute | solution.py:333
  70.8 14.4 %collective-permute-start.10 = (bf16[160,768]{1,0:T(8,128)(2,1)}, bf16[160,768]{1,0:T(8,128)(2,1)S(1)}, u32[]{:S(2)}, u32[]{:S(2)}) collective-permute-start(bf16[160,768]{1,0:T(8,128)(2,1)} %encoder_attend.1.refs_8_), channel_id=1, source_target_pairs={{0,2},{1,3},{2,4},{3,5},{4,6},{5,7},{6,0},{7,1},{8,10},{9,11},{10,... | collective-permute-start | bytes 737288 | tf_op jit(solution)/shard_map/ppermute | solution.py:206
  70.8 16.2 %collective-permute-start.11 = (bf16[160,768]{1,0:T(8,128)(2,1)}, bf16[160,768]{1,0:T(8,128)(2,1)S(1)}, u32[]{:S(2)}, u32[]{:S(2)}) collective-permute-start(bf16[160,768]{1,0:T(8,128)(2,1)} %encoder_attend.1.refs_8_), channel_id=1, source_target_pairs={{0,6},{1,7},{2,0},{3,1},{4,2},{5,3},{6,4},{7,5},{8,14},{9,15},{10,... | collective-permute-start | bytes 737288 | tf_op jit(solution)/shard_map/ppermute | solution.py:206
  73.5 13.9 %collective-permute-start.12 = (bf16[160,768]{1,0:T(8,128)(2,1)}, bf16[160,768]{1,0:T(8,128)(2,1)S(1)}, u32[]{:S(2)}, u32[]{:S(2)}) collective-permute-start(bf16[160,768]{1,0:T(8,128)(2,1)} %encoder_attend.1.refs_8_), channel_id=1, source_target_pairs={{0,4},{1,5},{2,6},{3,7},{4,0},{5,1},{6,2},{7,3},{8,12},{9,13},{10,... | collective-permute-start | bytes 737288 | tf_op jit(solution)/shard_map/ppermute | solution.py:206
  73.5 13.9 %collective-permute-start.9 = (bf16[160,768]{1,0:T(8,128)(2,1)}, bf16[160,768]{1,0:T(8,128)(2,1)}, u32[]{:S(2)}, u32[]{:S(2)}) collective-permute-start(bf16[160,768]{1,0:T(8,128)(2,1)} %encoder_attend.1.refs_8_), channel_id=1, source_target_pairs={{0,1},{1,0},{2,3},{3,2},{4,5},{5,4},{6,7},{7,6},{8,9},{9,8},{10,11... | collective-permute-start | bytes 737288 | tf_op jit(solution)/shard_map/ppermute | solution.py:205
  79.3 13.7 %collective-permute-start.20 = (bf16[2,4,80,256]{3,2,1,0:T(8,128)(2,1)S(1)}, bf16[2,4,80,256]{3,2,1,0:T(8,128)(2,1)S(1)}, u32[]{:S(2)}, u32[]{:S(2)}) collective-permute-start(bf16[2,4,80,256]{3,2,1,0:T(8,128)(2,1)S(1)} %pad_maximum_fusion.1), channel_id=1, source_target_pairs={{0,64},{16,80},{32,96},{48,112},{64,128},{80,144},{96,160},{112,17... | collective-permute-start | bytes 983048 | tf_op jit(solution)/shard_map/ppermute | solution.py:272
  85.1 10.1 %collective-permute-start.21 = (bf16[2,4,80,256]{3,2,1,0:T(8,128)(2,1)S(1)}, bf16[2,4,80,256]{3,2,1,0:T(8,128)(2,1)S(1)}, u32[]{:S(2)}, u32[]{:S(2)}) collective-permute-start(bf16[2,4,80,256]{3,2,1,0:T(8,128)(2,1)S(1)} %pad_maximum_fusion.1), channel_id=1, source_target_pairs={{0,128},{16,144},{32,160},{48,176},{64,192},{80,208},{96,224},{112... | collective-permute-start | bytes 983048 | tf_op jit(solution)/shard_map/ppermute | solution.py:272
  87.0 12.0 %collective-permute-start.22 = (bf16[2,4,80,256]{3,2,1,0:T(8,128)(2,1)S(1)}, bf16[2,4,80,256]{3,2,1,0:T(8,128)(2,1)S(1)}, u32[]{:S(2)}, u32[]{:S(2)}) collective-permute-start(bf16[2,4,80,256]{3,2,1,0:T(8,128)(2,1)S(1)} %pad_maximum_fusion.1), channel_id=1, source_target_pairs={{0,192},{16,208},{32,224},{48,240},{64,0},{80,16},{96,32},{112,48}... | collective-permute-start | bytes 983048 | tf_op jit(solution)/shard_map/ppermute | solution.py:272
  87.3 13.8 %collective-permute-start.13 = (bf16[160,768]{1,0:T(8,128)(2,1)}, bf16[160,768]{1,0:T(8,128)(2,1)}, u32[]{:S(2)}, u32[]{:S(2)}) collective-permute-start(bf16[160,768]{1,0:T(8,128)(2,1)} %collective-permute-done.9.refs_9_), channel_id=1, source_target_pairs={{0,2},{1,3},{2,4},{3,5},{4,6},{5,7},{6,0},{7,1},{8,10},{9,11},{10,... | collective-permute-start | bytes 737288 | tf_op jit(solution)/shard_map/ppermute | solution.py:208
  87.4 13.8 %collective-permute-start.14 = (bf16[160,768]{1,0:T(8,128)(2,1)}, bf16[160,768]{1,0:T(8,128)(2,1)}, u32[]{:S(2)}, u32[]{:S(2)}) collective-permute-start(bf16[160,768]{1,0:T(8,128)(2,1)} %collective-permute-done.9.refs_9_), channel_id=1, source_target_pairs={{0,6},{1,7},{2,0},{3,1},{4,2},{5,3},{6,4},{7,5},{8,14},{9,15},{10,... | collective-permute-start | bytes 737288 | tf_op jit(solution)/shard_map/ppermute | solution.py:208
  93.0 8.2 %collective-permute-start.15 = (bf16[160,768]{1,0:T(8,128)(2,1)}, bf16[160,768]{1,0:T(8,128)(2,1)}, u32[]{:S(2)}, u32[]{:S(2)}) collective-permute-start(bf16[160,768]{1,0:T(8,128)(2,1)} %collective-permute-done.9.refs_9_), channel_id=1, source_target_pairs={{0,4},{1,5},{2,6},{3,7},{4,0},{5,1},{6,2},{7,3},{8,12},{9,13},{10,... | collective-permute-start | bytes 737288 | tf_op jit(solution)/shard_map/ppermute | solution.py:208
  107.6 37.7 %all-to-all-start.1 = ((bf16[16,128,256]{2,1,0:T(8,128)(2,1)}), bf16[16,128,256]{2,1,0:T(8,128)(2,1)S(1)}, u32[]{:S(2)}, u32[]{:S(2)}) async-start(bf16[16,128,256]{2,1,0:T(8,128)(2,1)} %bitcast.81), calls=%async_computation.1 | async-start | bytes 2097152 | tf_op jit(solution)/shard_map/all_to_all | solution.py:381
  145.3 4.2 %collective-permute-start.23 = (bf16[2048,256]{1,0:T(8,128)(2,1)S(1)}, bf16[2048,256]{1,0:T(8,128)(2,1)}, u32[]{:S(2)}, u32[]{:S(2)}) collective-permute-start(bf16[2048,256]{1,0:T(8,128)(2,1)S(1)} %bitcast.79), channel_id=1, source_target_pairs={{0,8},{8,0},{1,9},{9,1},{2,10},{10,2},{3,11},{11,3},{4,12},{12,4},... | collective-permute-start | bytes 3145736 | tf_op jit(solution)/shard_map/ppermute | solution.py:420
  (24 other events, 221.2 us)

commit v4 on v3

--- a/solution.py
+++ b/solution.py
@@ -330,6 +330,7 @@
     piece = jnp.sum(after(parts, kv).astype(F32), 0).astype(BF)
     line = ring_of(piece, line_shift)
     ms = gather8(mixed, mixed, lambda *abc: abc)
+    line = after(line, mixed)
     line_other = lax.ppermute(line, "pipe", [(0, 1), (1, 0)])
     plane = ring_of(after(jnp.stack([line, line_other]), mixed), plane_shift)
     spot = jnp.arange(16)

time: 154 us -> 152 us (0.987)
  starting transfers between devices: 66.5 us -> 62.5 us
  waiting for transfers between devices: 30.7 us -> 33.2 us
    all_to_all x1, starting transfers between devices: 10.8 us -> 4.53 us  [shards(): lax.all_to_all(slots, 'replica', split_axis=0, concat_axis=0, tiled=True)]
    ppermute x6, waiting for transfers between devices: 5.75 us -> 0.02 us  [gather8(): a, b, c = (lax.ppermute(near, 'tensor', p) for p in (p1, p3, p2))]
    ppermute x6, waiting for transfers between devices: 0.02 us -> 4.4 us  [gather8(): za, zb, zc = (lax.ppermute(z, 'tensor', p) for p in (p1, p3, p2))]
    ppermute x6, waiting for transfers between devices: 6.43 us -> 9.92 us  [ring_of(): lax.ppermute(piece, 'replica', shift(d))]
    ppermute x6, starting transfers between devices: 7.08 us -> 9.12 us  [gather8(): a, b, c = (lax.ppermute(near, 'tensor', p) for p in (p1, p3, p2))]
  transfers between devices with their start and end apart: 26 -> 26, of which waited for: 7 -> 7; matrix products, arithmetic and copies ran while one was open for 15% -> 15% of each run, Pallas kernels for 12% -> 8%
where the time goes in v4:
time: 152 us; the launch traced here: 151 us
  starting transfers between devices  62.5 us (41%)
  waiting for transfers between devices  33.2 us (22%)
  Pallas kernels  27.4 us (18%)
  local copies, waits for them, and re-layouts  13.4 us (9%)
  matrix products  6.65 us (4%)
  other arithmetic  5.53 us (4%)
  between operations  2.38 us (2%)
    all_to_all x1, waiting for transfers between devices, shards(): lax.all_to_all(slots, 'replica', split_axis=0, concat_axis=0, tiled=True)  17.1 us
    ppermute x6, waiting for transfers between devices, ring_of(): lax.ppermute(piece, 'replica', shift(d))  9.92 us
    ppermute x6, starting transfers between devices, gather8(): a, b, c = (lax.ppermute(near, 'tensor', p) for p in (p1, p3, p2))  9.12 us
    ppermute x1, starting transfers between devices, out_rows(): return lax.ppermute(mine, ('replica', 'pipe', 'tensor'), pairs)  8.87 us
    ppermute x6, starting transfers between devices, ring_of(): lax.ppermute(piece, 'replica', shift(d))  8.26 us
    all_to_all x1, starting transfers between devices, shards(): lax.all_to_all(blocks, 'tensor', split_axis=0, concat_axis=0, tiled=True)  7.83 us
    ppermute x6, starting transfers between devices, gather8(): za, zb, zc = (lax.ppermute(z, 'tensor', p) for p in (p1, p3, p2))  7.54 us
    ppermute x2, starting transfers between devices, gather8(): z = lax.ppermute(s, 'tensor', ZX)  7.17 us
  transfers between devices with their start and end apart: 26, of which 7 were waited for; matrix products, arithmetic and copies ran while one was open for 15% of the time, Pallas kernels for 8%

profile of v4, /device:TPU:1, one launch (start us, length us, event | category | flops | bytes accessed | tf_op | source)
XLA Modules:
  0.0 151.1 jit_solution(16547552827082559581)
XLA Ops:
  1.6 8.9 %collective-permute-start.1 = (bf16[40,1280]{1,0:T(8,128)(2,1)S(1)}, bf16[40,1280]{1,0:T(8,128)(2,1)S(1)}, u32[]{:S(2)}, u32[]{:S(2)}) collective-permute-start(bf16[40,1280]{1,0:T(8,128)(2,1)S(1)} %constant_dynamic-slice_fusion.2), channel_id=1, source_target_pairs={{0,0},{56,1},{64,2},{120,3},{128,4},{184,5},{192,6},{248,7},{4,8},... | collective-permute-start | bytes 307208 | tf_op jit(solution)/shard_map/ppermute | solution.py:237
  10.5 2.0 %turn.1.refs_0_ = bf16[160,768]{1,0:T(8,128)(2,1)} custom-call(bf16[768,160]{1,0:T(8,128)(2,1)} %bitcast.86), custom_call_target="tpu_custom_call" | custom-call | flops 39321600 | bytes 491520 | tf_op jit(solution)/shard_map/turn/pallas_call | solution.py:300
  12.5 2.1 %collective-permute-start = (bf16[160,768]{1,0:T(8,128)(2,1)}, bf16[160,768]{1,0:T(8,128)(2,1)S(1)}, u32[]{:S(2)}, u32[]{:S(2)}) collective-permute-start(bf16[160,768]{1,0:T(8,128)(2,1)} %turn.1.refs_0_), channel_id=1, source_target_pairs={{0,1},{1,0},{2,3},{3,2},{4,5},{5,4},{6,7},{7,6},{8,9},{9,8},{10,11... | collective-permute-start | bytes 737288 | tf_op jit(solution)/shard_map/ppermute | solution.py:205
  16.2 2.5 %collective-permute-start.2 = (bf16[160,768]{1,0:T(8,128)(2,1)}, bf16[160,768]{1,0:T(8,128)(2,1)S(1)}, u32[]{:S(2)}, u32[]{:S(2)}) collective-permute-start(bf16[160,768]{1,0:T(8,128)(2,1)} %turn.1.refs_0_), channel_id=1, source_target_pairs={{0,2},{1,3},{2,4},{3,5},{4,6},{5,7},{6,0},{7,1},{8,10},{9,11},{10,... | collective-permute-start | bytes 737288 | tf_op jit(solution)/shard_map/ppermute | solution.py:206
  20.6 2.3 %convolution_convert_fusion = bf16[40,1024]{1,0:T(8,128)(2,1)S(1)} fusion(bf16[40,1280]{1,0:T(8,128)(2,1)S(1)} %collective-permute-done.1, bf16[1280,1024]{1,0:T(8,128)(2,1)} %param.20), kind=kOutput, calls=%fused_computation.7 | convolution fusion | flops 104898560 | bytes 2805760 | tf_op jit(solution)/shard_map/dot_general | solution.py:248
  22.9 4.3 %fusion.5.part_ref = bf16[2,80,1024]{2,1,0:T(8,128)(2,1)} fusion(bf16[1024,2,1024]{2,1,0:T(2,128)(2,1)} %param.21, bf16[40,1024]{1,0:T(8,128)(2,1)S(1)} %convolution_convert_fusion, bf16[40,1024]{1,0:T(8,128)(2,1)S(1)} %constant_dynamic-slice_fusion.3), kind=kOutput, calls=%fused_computation.6 | convolution fusion | flops 336035840 | bytes 4685824 | tf_op jit(solution)/shard_map/rk,kcn->crn/dot_general | solution.py:251
  32.3 7.8 %all-to-all-start = ((bf16[8,80,256]{2,1,0:T(8,128)(2,1)}), bf16[8,80,256]{2,1,0:T(8,128)(2,1)S(1)}, u32[]{:S(2)}, u32[]{:S(2)}) async-start(bf16[8,80,256]{2,1,0:T(8,128)(2,1)} %heads.1), calls=%async_computation | async-start | bytes 655360 | tf_op jit(solution)/shard_map/all_to_all | solution.py:329
  43.5 6.0 %qkv.1 = (bf16[160,768]{1,0:T(8,128)(2,1)}, bf16[320,768]{1,0:T(8,128)(2,1)}) custom-call(s32[3]{0:T(128)} %pad_add_fusion.at_ref.pipe_ref, bf16[160,768]{1,0:T(8,128)(2,1)} %turn.1.refs_0_, bf16[160,768]{1,0:T(8,128)(2,1)} %copy-done.2, bf16[160,768]{1,0:T(8,128)(2,1)} %copy-done.3, bf16[160,768]{1,0:T(8,128)(2,1)} %copy-done.4, ...), custom_call_target="tpu_custom_call" | custom-call | flops 943718400 | bytes 6291456 | tf_op jit(solution)/shard_map/qkv/pallas_call | solution.py:309
  49.4 4.0 %collective-permute-start.8 = (bf16[320,768]{1,0:T(8,128)(2,1)}, bf16[320,768]{1,0:T(8,128)(2,1)S(1)}, u32[]{:S(2)}, u32[]{:S(2)}) collective-permute-start(bf16[320,768]{1,0:T(8,128)(2,1)} %get-tuple-element.20.own_ref), channel_id=1, source_target_pairs={{0,8},{8,0},{1,9},{9,1},{2,10},{10,2},{3,11},{11,3},{4,12},{12,4},... | collective-permute-start | bytes 1474568 | tf_op jit(solution)/shard_map/ppermute | solution.py:318
  53.5 2.6 %collective-permute-start.16 = (bf16[80,256]{1,0:T(8,128)(2,1)S(1)}, bf16[80,256]{1,0:T(8,128)(2,1)S(1)}, u32[]{:S(2)}, u32[]{:S(2)}) collective-permute-start(bf16[80,256]{1,0:T(8,128)(2,1)S(1)} %reduce_sum.62), channel_id=1, source_target_pairs={{0,16},{16,32},{32,48},{48,0},{64,80},{80,96},{96,112},{112,64},{1... | collective-permute-start | bytes 122888 | tf_op jit(solution)/shard_map/ppermute | solution.py:272
  56.7 2.3 %collective-permute-start.18 = (bf16[80,256]{1,0:T(8,128)(2,1)S(1)}, bf16[80,256]{1,0:T(8,128)(2,1)S(1)}, u32[]{:S(2)}, u32[]{:S(2)}) collective-permute-start(bf16[80,256]{1,0:T(8,128)(2,1)S(1)} %reduce_sum.62), channel_id=1, source_target_pairs={{0,48},{16,0},{32,16},{48,32},{64,112},{80,64},{96,80},{112,96},{1... | collective-permute-start | bytes 122888 | tf_op jit(solution)/shard_map/ppermute | solution.py:272
  60.9 5.2 %encoder_attend.1.refs_8_ = bf16[160,768]{1,0:T(8,128)(2,1)} custom-call(s32[192]{0:T(256)} %count_ref.1, s32[3]{0:T(128)} %pad_add_fusion.at_ref.pipe_ref, bf16[160,768]{1,0:T(8,128)(2,1)} %get-tuple-element.19.q_ref, bf16[320,768]{1,0:T(8,128)(2,1)} %get-tuple-element.20.own_ref, bf16[320,768]{1,0:T(8,128)(2,1)} %copy-done.10), custom_call_target="tpu_custom_call" | custom-call | flops 125829120 | bytes 2097152 | tf_op jit(solution)/shard_map/encoder_attend/pallas_call | solution.py:319
  66.1 2.5 %collective-permute-start.10 = (bf16[160,768]{1,0:T(8,128)(2,1)}, bf16[160,768]{1,0:T(8,128)(2,1)S(1)}, u32[]{:S(2)}, u32[]{:S(2)}) collective-permute-start(bf16[160,768]{1,0:T(8,128)(2,1)} %encoder_attend.1.refs_8_), channel_id=1, source_target_pairs={{0,2},{1,3},{2,4},{3,5},{4,6},{5,7},{6,0},{7,1},{8,10},{9,11},{10,... | collective-permute-start | bytes 737288 | tf_op jit(solution)/shard_map/ppermute | solution.py:206
  70.8 5.1 %collective-permute-start.9 = (bf16[160,768]{1,0:T(8,128)(2,1)}, bf16[160,768]{1,0:T(8,128)(2,1)}, u32[]{:S(2)}, u32[]{:S(2)}) collective-permute-start(bf16[160,768]{1,0:T(8,128)(2,1)} %encoder_attend.1.refs_8_), channel_id=1, source_target_pairs={{0,1},{1,0},{2,3},{3,2},{4,5},{5,4},{6,7},{7,6},{8,9},{9,8},{10,11... | collective-permute-start | bytes 737288 | tf_op jit(solution)/shard_map/ppermute | solution.py:205
  75.9 3.4 %collective-permute-start.19 = (bf16[4,80,256]{2,1,0:T(8,128)(2,1)S(1)}, bf16[4,80,256]{2,1,0:T(8,128)(2,1)S(1)}, u32[]{:S(2)}, u32[]{:S(2)}) collective-permute-start(bf16[4,80,256]{2,1,0:T(8,128)(2,1)S(1)} %pad_maximum_fusion.2), channel_id=1, source_target_pairs={{0,8},{8,0},{1,9},{9,1},{2,10},{10,2},{3,11},{11,3},{4,12},{12,4},... | collective-permute-start | bytes 491528 | tf_op jit(solution)/shard_map/ppermute | solution.py:334
  81.3 2.0 %collective-permute-start.22 = (bf16[2,4,80,256]{3,2,1,0:T(8,128)(2,1)S(1)}, bf16[2,4,80,256]{3,2,1,0:T(8,128)(2,1)S(1)}, u32[]{:S(2)}, u32[]{:S(2)}) collective-permute-start(bf16[2,4,80,256]{3,2,1,0:T(8,128)(2,1)S(1)} %pad_maximum_fusion.1), channel_id=1, source_target_pairs={{0,192},{16,208},{32,224},{48,240},{64,0},{80,16},{96,32},{112,48}... | collective-permute-start | bytes 983048 | tf_op jit(solution)/shard_map/ppermute | solution.py:272
  83.6 2.4 %collective-permute-start.14 = (bf16[160,768]{1,0:T(8,128)(2,1)}, bf16[160,768]{1,0:T(8,128)(2,1)}, u32[]{:S(2)}, u32[]{:S(2)}) collective-permute-start(bf16[160,768]{1,0:T(8,128)(2,1)} %collective-permute-done.9.refs_9_), channel_id=1, source_target_pairs={{0,6},{1,7},{2,0},{3,1},{4,2},{5,3},{6,4},{7,5},{8,14},{9,15},{10,... | collective-permute-start | bytes 737288 | tf_op jit(solution)/shard_map/ppermute | solution.py:208
  88.8 8.8 %collective-permute-done.20 = bf16[2,4,80,256]{3,2,1,0:T(8,128)(2,1)S(1)} collective-permute-done((bf16[2,4,80,256]{3,2,1,0:T(8,128)(2,1)S(1)}, bf16[2,4,80,256]{3,2,1,0:T(8,128)(2,1)S(1)}, u32[]{:S(2)}, u32[]{:S(2)}) %collective-permute-start.20) | collective-permute-done | bytes 327712 | tf_op jit(solution)/shard_map/ppermute | solution.py:272
  101.3 4.4 %collective-permute-done.15.refs_15_ = bf16[160,768]{1,0:T(8,128)(2,1)} collective-permute-done((bf16[160,768]{1,0:T(8,128)(2,1)}, bf16[160,768]{1,0:T(8,128)(2,1)}, u32[]{:S(2)}, u32[]{:S(2)}) %collective-permute-start.15) | collective-permute-done | bytes 245792 | tf_op jit(solution)/shard_map/ppermute | solution.py:208
  105.7 6.3 %memory.1 = bf16[2048,256]{1,0:T(8,128)(2,1)} custom-call(s32[3]{0:T(128)} %pad_add_fusion.at_ref.pipe_ref, s32[32]{0:T(128)} %select_reduce_fusion.2.pick_ref, bf16[160,768]{1,0:T(8,128)(2,1)} %turn.1.refs_0_, bf16[160,768]{1,0:T(8,128)(2,1)} %copy-done.2, bf16[160,768]{1,0:T(8,128)(2,1)} %copy-done.3, bf16[160,768]{1,0:T(8,128)(2,1)} %copy-done.4, ...), custom_call_target="tpu_custom_call" | custom-call | flops 1006632960 | bytes 6291456 | tf_op jit(solution)/shard_map/memory/pallas_call | solution.py:367
  112.1 4.5 %all-to-all-start.1 = ((bf16[16,128,256]{2,1,0:T(8,128)(2,1)}), bf16[16,128,256]{2,1,0:T(8,128)(2,1)S(1)}, u32[]{:S(2)}, u32[]{:S(2)}) async-start(bf16[16,128,256]{2,1,0:T(8,128)(2,1)} %bitcast.80), calls=%async_computation.1 | async-start | bytes 2097152 | tf_op jit(solution)/shard_map/all_to_all | solution.py:382
  123.0 2.8 %self_attend.1 = bf16[2,32,1024]{2,1,0:T(8,128)(2,1)} custom-call(s32[512,1]{1,0:T(8,128)} %reshape_reshape.8.len_ref, bf16[32,16,128]{2,1,0:T(8,128)(2,1)} %copy_bitcast_fusion.q_ref, bf16[32,48,256]{2,1,0:T(8,128)(2,1)} %maximum_maximum_fusion.kv_ref), custom_call_target="tpu_custom_call" | custom-call | flops 33554432 | bytes 4194304 | tf_op jit(solution)/shard_map/self_attend/pallas_call | solution.py:410
  126.5 17.1 %all-to-all-done.1 = bf16[16,128,256]{2,1,0:T(8,128)(2,1)S(1)} async-done(((bf16[16,128,256]{2,1,0:T(8,128)(2,1)}), bf16[16,128,256]{2,1,0:T(8,128)(2,1)S(1)}, u32[]{:S(2)}, u32[]{:S(2)}) %all-to-all-start.1) | async-done | bytes 1048608 | tf_op jit(solution)/shard_map/all_to_all | solution.py:382
  147.7 3.4 %cross_attend.1 = bf16[2,32,1024]{2,1,0:T(8,128)(2,1)} custom-call(s32[32]{0:T(128)} %get-tuple-element.33.slot_ref, s32[3]{0:T(128)} %pad_add_fusion.at_ref.pipe_ref, s32[512,1]{1,0:T(8,128)} %copy.46.count_ref, bf16[32,16,128]{2,1,0:T(8,128)(2,1)} %copy_bitcast_fusion.1.q_ref, bf16[2048,256]{1,0:T(8,128)(2,1)} %bitcast.79, ...), custom_call_target="tpu_custom_call" | custom-call | flops 33554432 | bytes 4194304 | tf_op jit(solution)/shard_map/cross_attend/pallas_call | solution.py:423
  (131 shorter events, 36.0 us)
Async XLA Ops:
  1.6 14.6 %collective-permute-start.1 = (bf16[40,1280]{1,0:T(8,128)(2,1)S(1)}, bf16[40,1280]{1,0:T(8,128)(2,1)S(1)}, u32[]{:S(2)}, u32[]{:S(2)}) collective-permute-start(bf16[40,1280]{1,0:T(8,128)(2,1)S(1)} %constant_dynamic-slice_fusion.2), channel_id=1, source_target_pairs={{0,0},{56,1},{64,2},{120,3},{128,4},{184,5},{192,6},{248,7},{4,8},... | collective-permute-start | bytes 307208 | tf_op jit(solution)/shard_map/ppermute | solution.py:237
  12.5 16.5 %collective-permute-start = (bf16[160,768]{1,0:T(8,128)(2,1)}, bf16[160,768]{1,0:T(8,128)(2,1)S(1)}, u32[]{:S(2)}, u32[]{:S(2)}) collective-permute-start(bf16[160,768]{1,0:T(8,128)(2,1)} %turn.1.refs_0_), channel_id=1, source_target_pairs={{0,1},{1,0},{2,3},{3,2},{4,5},{5,4},{6,7},{7,6},{8,9},{9,8},{10,11... | collective-permute-start | bytes 737288 | tf_op jit(solution)/shard_map/ppermute | solution.py:205
  16.2 15.5 %collective-permute-start.2 = (bf16[160,768]{1,0:T(8,128)(2,1)}, bf16[160,768]{1,0:T(8,128)(2,1)S(1)}, u32[]{:S(2)}, u32[]{:S(2)}) collective-permute-start(bf16[160,768]{1,0:T(8,128)(2,1)} %turn.1.refs_0_), channel_id=1, source_target_pairs={{0,2},{1,3},{2,4},{3,5},{4,6},{5,7},{6,0},{7,1},{8,10},{9,11},{10,... | collective-permute-start | bytes 737288 | tf_op jit(solution)/shard_map/ppermute | solution.py:206
  18.7 23.2 %collective-permute-start.3 = (bf16[160,768]{1,0:T(8,128)(2,1)}, bf16[160,768]{1,0:T(8,128)(2,1)S(1)}, u32[]{:S(2)}, u32[]{:S(2)}) collective-permute-start(bf16[160,768]{1,0:T(8,128)(2,1)} %turn.1.refs_0_), channel_id=1, source_target_pairs={{0,6},{1,7},{2,0},{3,1},{4,2},{5,3},{6,4},{7,5},{8,14},{9,15},{10,... | collective-permute-start | bytes 737288 | tf_op jit(solution)/shard_map/ppermute | solution.py:206
  19.5 22.4 %collective-permute-start.4 = (bf16[160,768]{1,0:T(8,128)(2,1)}, bf16[160,768]{1,0:T(8,128)(2,1)S(1)}, u32[]{:S(2)}, u32[]{:S(2)}) collective-permute-start(bf16[160,768]{1,0:T(8,128)(2,1)} %turn.1.refs_0_), channel_id=1, source_target_pairs={{0,4},{1,5},{2,6},{3,7},{4,0},{5,1},{6,2},{7,3},{8,12},{9,13},{10,... | collective-permute-start | bytes 737288 | tf_op jit(solution)/shard_map/ppermute | solution.py:206
  29.0 12.9 %collective-permute-start.5 = (bf16[160,768]{1,0:T(8,128)(2,1)S(1)}, bf16[160,768]{1,0:T(8,128)(2,1)S(1)}, u32[]{:S(2)}, u32[]{:S(2)}) collective-permute-start(bf16[160,768]{1,0:T(8,128)(2,1)S(1)} %collective-permute-done.refs_1_), channel_id=1, source_target_pairs={{0,2},{1,3},{2,4},{3,5},{4,6},{5,7},{6,0},{7,1},{8,10},{9,11},{10,... | collective-permute-start | bytes 737288 | tf_op jit(solution)/shard_map/ppermute | solution.py:208
  29.9 12.1 %collective-permute-start.6 = (bf16[160,768]{1,0:T(8,128)(2,1)S(1)}, bf16[160,768]{1,0:T(8,128)(2,1)S(1)}, u32[]{:S(2)}, u32[]{:S(2)}) collective-permute-start(bf16[160,768]{1,0:T(8,128)(2,1)S(1)} %collective-permute-done.refs_1_), channel_id=1, source_target_pairs={{0,6},{1,7},{2,0},{3,1},{4,2},{5,3},{6,4},{7,5},{8,14},{9,15},{10,... | collective-permute-start | bytes 737288 | tf_op jit(solution)/shard_map/ppermute | solution.py:208
  31.7 10.3 %collective-permute-start.7 = (bf16[160,768]{1,0:T(8,128)(2,1)S(1)}, bf16[160,768]{1,0:T(8,128)(2,1)S(1)}, u32[]{:S(2)}, u32[]{:S(2)}) collective-permute-start(bf16[160,768]{1,0:T(8,128)(2,1)S(1)} %collective-permute-done.refs_1_), channel_id=1, source_target_pairs={{0,4},{1,5},{2,6},{3,7},{4,0},{5,1},{6,2},{7,3},{8,12},{9,13},{10,... | collective-permute-start | bytes 737288 | tf_op jit(solution)/shard_map/ppermute | solution.py:208
  32.3 21.1 %all-to-all-start = ((bf16[8,80,256]{2,1,0:T(8,128)(2,1)}), bf16[8,80,256]{2,1,0:T(8,128)(2,1)S(1)}, u32[]{:S(2)}, u32[]{:S(2)}) async-start(bf16[8,80,256]{2,1,0:T(8,128)(2,1)} %heads.1), calls=%async_computation | async-start | bytes 655360 | tf_op jit(solution)/shard_map/all_to_all | solution.py:329
  49.4 10.7 %collective-permute-start.8 = (bf16[320,768]{1,0:T(8,128)(2,1)}, bf16[320,768]{1,0:T(8,128)(2,1)S(1)}, u32[]{:S(2)}, u32[]{:S(2)}) collective-permute-start(bf16[320,768]{1,0:T(8,128)(2,1)} %get-tuple-element.20.own_ref), channel_id=1, source_target_pairs={{0,8},{8,0},{1,9},{9,1},{2,10},{10,2},{3,11},{11,3},{4,12},{12,4},... | collective-permute-start | bytes 1474568 | tf_op jit(solution)/shard_map/ppermute | solution.py:318
  53.5 5.5 %collective-permute-start.16 = (bf16[80,256]{1,0:T(8,128)(2,1)S(1)}, bf16[80,256]{1,0:T(8,128)(2,1)S(1)}, u32[]{:S(2)}, u32[]{:S(2)}) collective-permute-start(bf16[80,256]{1,0:T(8,128)(2,1)S(1)} %reduce_sum.62), channel_id=1, source_target_pairs={{0,16},{16,32},{32,48},{48,0},{64,80},{80,96},{96,112},{112,64},{1... | collective-permute-start | bytes 122888 | tf_op jit(solution)/shard_map/ppermute | solution.py:272
  66.1 14.4 %collective-permute-start.10 = (bf16[160,768]{1,0:T(8,128)(2,1)}, bf16[160,768]{1,0:T(8,128)(2,1)S(1)}, u32[]{:S(2)}, u32[]{:S(2)}) collective-permute-start(bf16[160,768]{1,0:T(8,128)(2,1)} %encoder_attend.1.refs_8_), channel_id=1, source_target_pairs={{0,2},{1,3},{2,4},{3,5},{4,6},{5,7},{6,0},{7,1},{8,10},{9,11},{10,... | collective-permute-start | bytes 737288 | tf_op jit(solution)/shard_map/ppermute | solution.py:206
  68.6 12.7 %collective-permute-start.11 = (bf16[160,768]{1,0:T(8,128)(2,1)}, bf16[160,768]{1,0:T(8,128)(2,1)S(1)}, u32[]{:S(2)}, u32[]{:S(2)}) collective-permute-start(bf16[160,768]{1,0:T(8,128)(2,1)} %encoder_attend.1.refs_8_), channel_id=1, source_target_pairs={{0,6},{1,7},{2,0},{3,1},{4,2},{5,3},{6,4},{7,5},{8,14},{9,15},{10,... | collective-permute-start | bytes 737288 | tf_op jit(solution)/shard_map/ppermute | solution.py:206
  69.5 13.8 %collective-permute-start.12 = (bf16[160,768]{1,0:T(8,128)(2,1)}, bf16[160,768]{1,0:T(8,128)(2,1)S(1)}, u32[]{:S(2)}, u32[]{:S(2)}) collective-permute-start(bf16[160,768]{1,0:T(8,128)(2,1)} %encoder_attend.1.refs_8_), channel_id=1, source_target_pairs={{0,4},{1,5},{2,6},{3,7},{4,0},{5,1},{6,2},{7,3},{8,12},{9,13},{10,... | collective-permute-start | bytes 737288 | tf_op jit(solution)/shard_map/ppermute | solution.py:206
  70.8 12.4 %collective-permute-start.9 = (bf16[160,768]{1,0:T(8,128)(2,1)}, bf16[160,768]{1,0:T(8,128)(2,1)}, u32[]{:S(2)}, u32[]{:S(2)}) collective-permute-start(bf16[160,768]{1,0:T(8,128)(2,1)} %encoder_attend.1.refs_8_), channel_id=1, source_target_pairs={{0,1},{1,0},{2,3},{3,2},{4,5},{5,4},{6,7},{7,6},{8,9},{9,8},{10,11... | collective-permute-start | bytes 737288 | tf_op jit(solution)/shard_map/ppermute | solution.py:205
  75.9 4.4 %collective-permute-start.19 = (bf16[4,80,256]{2,1,0:T(8,128)(2,1)S(1)}, bf16[4,80,256]{2,1,0:T(8,128)(2,1)S(1)}, u32[]{:S(2)}, u32[]{:S(2)}) collective-permute-start(bf16[4,80,256]{2,1,0:T(8,128)(2,1)S(1)} %pad_maximum_fusion.2), channel_id=1, source_target_pairs={{0,8},{8,0},{1,9},{9,1},{2,10},{10,2},{3,11},{11,3},{4,12},{12,4},... | collective-permute-start | bytes 491528 | tf_op jit(solution)/shard_map/ppermute | solution.py:334
  80.4 17.2 %collective-permute-start.20 = (bf16[2,4,80,256]{3,2,1,0:T(8,128)(2,1)S(1)}, bf16[2,4,80,256]{3,2,1,0:T(8,128)(2,1)S(1)}, u32[]{:S(2)}, u32[]{:S(2)}) collective-permute-start(bf16[2,4,80,256]{3,2,1,0:T(8,128)(2,1)S(1)} %pad_maximum_fusion.1), channel_id=1, source_target_pairs={{0,64},{16,80},{32,96},{48,112},{64,128},{80,144},{96,160},{112,17... | collective-permute-start | bytes 983048 | tf_op jit(solution)/shard_map/ppermute | solution.py:272
  80.5 18.6 %collective-permute-start.21 = (bf16[2,4,80,256]{3,2,1,0:T(8,128)(2,1)S(1)}, bf16[2,4,80,256]{3,2,1,0:T(8,128)(2,1)S(1)}, u32[]{:S(2)}, u32[]{:S(2)}) collective-permute-start(bf16[2,4,80,256]{3,2,1,0:T(8,128)(2,1)S(1)} %pad_maximum_fusion.1), channel_id=1, source_target_pairs={{0,128},{16,144},{32,160},{48,176},{64,192},{80,208},{96,224},{112... | collective-permute-start | bytes 983048 | tf_op jit(solution)/shard_map/ppermute | solution.py:272
  81.3 17.8 %collective-permute-start.22 = (bf16[2,4,80,256]{3,2,1,0:T(8,128)(2,1)S(1)}, bf16[2,4,80,256]{3,2,1,0:T(8,128)(2,1)S(1)}, u32[]{:S(2)}, u32[]{:S(2)}) collective-permute-start(bf16[2,4,80,256]{3,2,1,0:T(8,128)(2,1)S(1)} %pad_maximum_fusion.1), channel_id=1, source_target_pairs={{0,192},{16,208},{32,224},{48,240},{64,0},{80,16},{96,32},{112,48}... | collective-permute-start | bytes 983048 | tf_op jit(solution)/shard_map/ppermute | solution.py:272
  83.3 18.0 %collective-permute-start.13 = (bf16[160,768]{1,0:T(8,128)(2,1)}, bf16[160,768]{1,0:T(8,128)(2,1)}, u32[]{:S(2)}, u32[]{:S(2)}) collective-permute-start(bf16[160,768]{1,0:T(8,128)(2,1)} %collective-permute-done.9.refs_9_), channel_id=1, source_target_pairs={{0,2},{1,3},{2,4},{3,5},{4,6},{5,7},{6,0},{7,1},{8,10},{9,11},{10,... | collective-permute-start | bytes 737288 | tf_op jit(solution)/shard_map/ppermute | solution.py:208
  83.6 17.7 %collective-permute-start.14 = (bf16[160,768]{1,0:T(8,128)(2,1)}, bf16[160,768]{1,0:T(8,128)(2,1)}, u32[]{:S(2)}, u32[]{:S(2)}) collective-permute-start(bf16[160,768]{1,0:T(8,128)(2,1)} %collective-permute-done.9.refs_9_), channel_id=1, source_target_pairs={{0,6},{1,7},{2,0},{3,1},{4,2},{5,3},{6,4},{7,5},{8,14},{9,15},{10,... | collective-permute-start | bytes 737288 | tf_op jit(solution)/shard_map/ppermute | solution.py:208
  97.6 8.1 %collective-permute-start.15 = (bf16[160,768]{1,0:T(8,128)(2,1)}, bf16[160,768]{1,0:T(8,128)(2,1)}, u32[]{:S(2)}, u32[]{:S(2)}) collective-permute-start(bf16[160,768]{1,0:T(8,128)(2,1)} %collective-permute-done.9.refs_9_), channel_id=1, source_target_pairs={{0,4},{1,5},{2,6},{3,7},{4,0},{5,1},{6,2},{7,3},{8,12},{9,13},{10,... | collective-permute-start | bytes 737288 | tf_op jit(solution)/shard_map/ppermute | solution.py:208
  112.1 31.5 %all-to-all-start.1 = ((bf16[16,128,256]{2,1,0:T(8,128)(2,1)}), bf16[16,128,256]{2,1,0:T(8,128)(2,1)S(1)}, u32[]{:S(2)}, u32[]{:S(2)}) async-start(bf16[16,128,256]{2,1,0:T(8,128)(2,1)} %bitcast.80), calls=%async_computation.1 | async-start | bytes 2097152 | tf_op jit(solution)/shard_map/all_to_all | solution.py:382
  143.6 4.2 %collective-permute-start.23 = (bf16[2048,256]{1,0:T(8,128)(2,1)S(1)}, bf16[2048,256]{1,0:T(8,128)(2,1)}, u32[]{:S(2)}, u32[]{:S(2)}) collective-permute-start(bf16[2048,256]{1,0:T(8,128)(2,1)S(1)} %bitcast.78), channel_id=1, source_target_pairs={{0,8},{8,0},{1,9},{9,1},{2,10},{10,2},{3,11},{11,3},{4,12},{12,4},... | collective-permute-start | bytes 3145736 | tf_op jit(solution)/shard_map/ppermute | solution.py:421
  (24 other events, 207.0 us)

commit v5 on v4

--- a/solution.py
+++ b/solution.py
@@ -56,10 +56,18 @@
 
 def qkv_kernel(at_ref, *refs):
     shards = refs[:8]
-    w_ref, gain_ref, q_ref, kv_ref, full, sems = refs[8:]
+    w_in, gain_in, q_ref, kv_ref, full, w_ref, gain_ref, sems, more = refs[8:]
     part, rows = shards[0].shape
     width = part * 8
+    extra = [
+        pltpu.make_async_copy(gain_in, gain_ref, more.at[0]),
+        pltpu.make_async_copy(w_in, w_ref, more.at[1]),
+    ]
+    for c in extra:
+        c.start()
     fill(at_ref, shards, (full,), (sems,))
+    for c in extra:
+        c.wait()
     cut = 256
     for j in range(rows // cut):
         lanes = slice(j * cut, (j + 1) * cut)
@@ -309,8 +317,14 @@
     q, kv = call(
         qkv_kernel,
         (shape_of((part, rows), BF), shape_of((2 * part, rows), BF)),
-        [SMEM] + [ANY] * 8 + [VMEM] * 2,
-        [pltpu.VMEM((ENC_W, rows), BF), pltpu.SemaphoreType.DMA((8,))],
+        [SMEM] + [ANY] * 10,
+        [
+            pltpu.VMEM((ENC_W, rows), BF),
+            pltpu.VMEM((3 * part, ENC_W), BF),
+            pltpu.VMEM((ENC_W, 1), F32),
+            pltpu.SemaphoreType.DMA((8,)),
+            pltpu.SemaphoreType.DMA((2,)),
+        ],
         2 * rows * ENC_W * 3 * part,
         6 * 1024 * 1024,
         "qkv",

time: 152 us -> 151 us (level)
  no operation moved by 1% of the time
where the time goes in v5:
time: 151 us
  starting transfers between devices  62.5 us (41%)
  waiting for transfers between devices  33.2 us (22%)
  Pallas kernels  27 us (18%)
  local copies, waits for them, and re-layouts  13.4 us (9%)
  matrix products  6.65 us (4%)
  other arithmetic  5.53 us (4%)
  between operations  2.38 us (2%)
    all_to_all x1, waiting for transfers between devices, shards(): lax.all_to_all(slots, 'replica', split_axis=0, concat_axis=0, tiled=True)  17.1 us
    ppermute x6, waiting for transfers between devices, ring_of(): lax.ppermute(piece, 'replica', shift(d))  9.92 us
    ppermute x6, starting transfers between devices, gather8(): a, b, c = (lax.ppermute(near, 'tensor', p) for p in (p1, p3, p2))  9.28 us
    ppermute x1, starting transfers between devices, out_rows(): return lax.ppermute(mine, ('replica', 'pipe', 'tensor'), pairs)  8.87 us
    ppermute x6, starting transfers between devices, ring_of(): lax.ppermute(piece, 'replica', shift(d))  8.27 us
    all_to_all x1, starting transfers between devices, shards(): lax.all_to_all(blocks, 'tensor', split_axis=0, concat_axis=0, tiled=True)  7.83 us
    ppermute x6, starting transfers between devices, gather8(): za, zb, zc = (lax.ppermute(z, 'tensor', p) for p in (p1, p3, p2))  7.54 us
    ppermute x2, starting transfers between devices, gather8(): z = lax.ppermute(s, 'tensor', ZX)  7.02 us
  transfers between devices with their start and end apart: 26, of which 7 were waited for; matrix products, arithmetic and copies ran while one was open for 15% of the time, Pallas kernels for 8%

profile of v5, /device:TPU:1, one launch (start us, length us, event | category | flops | bytes accessed | tf_op | source)
XLA Modules:
  0.0 150.7 jit_solution(1260312986081317731)
XLA Ops:
  1.6 8.9 %collective-permute-start.1 = (bf16[40,1280]{1,0:T(8,128)(2,1)S(1)}, bf16[40,1280]{1,0:T(8,128)(2,1)S(1)}, u32[]{:S(2)}, u32[]{:S(2)}) collective-permute-start(bf16[40,1280]{1,0:T(8,128)(2,1)S(1)} %constant_dynamic-slice_fusion.2), channel_id=1, source_target_pairs={{0,0},{56,1},{64,2},{120,3},{128,4},{184,5},{192,6},{248,7},{4,8},... | collective-permute-start | bytes 307208 | tf_op jit(solution)/shard_map/ppermute | solution.py:245
  10.5 2.0 %turn.1.refs_0_ = bf16[160,768]{1,0:T(8,128)(2,1)} custom-call(bf16[768,160]{1,0:T(8,128)(2,1)} %bitcast.86), custom_call_target="tpu_custom_call" | custom-call | flops 39321600 | bytes 491520 | tf_op jit(solution)/shard_map/turn/pallas_call | solution.py:308
  12.5 2.1 %collective-permute-start = (bf16[160,768]{1,0:T(8,128)(2,1)}, bf16[160,768]{1,0:T(8,128)(2,1)S(1)}, u32[]{:S(2)}, u32[]{:S(2)}) collective-permute-start(bf16[160,768]{1,0:T(8,128)(2,1)} %turn.1.refs_0_), channel_id=1, source_target_pairs={{0,1},{1,0},{2,3},{3,2},{4,5},{5,4},{6,7},{7,6},{8,9},{9,8},{10,11... | collective-permute-start | bytes 737288 | tf_op jit(solution)/shard_map/ppermute | solution.py:213
  16.2 2.5 %collective-permute-start.2 = (bf16[160,768]{1,0:T(8,128)(2,1)}, bf16[160,768]{1,0:T(8,128)(2,1)S(1)}, u32[]{:S(2)}, u32[]{:S(2)}) collective-permute-start(bf16[160,768]{1,0:T(8,128)(2,1)} %turn.1.refs_0_), channel_id=1, source_target_pairs={{0,2},{1,3},{2,4},{3,5},{4,6},{5,7},{6,0},{7,1},{8,10},{9,11},{10,... | collective-permute-start | bytes 737288 | tf_op jit(solution)/shard_map/ppermute | solution.py:214
  20.6 2.3 %convolution_convert_fusion = bf16[40,1024]{1,0:T(8,128)(2,1)S(1)} fusion(bf16[40,1280]{1,0:T(8,128)(2,1)S(1)} %collective-permute-done.1, bf16[1280,1024]{1,0:T(8,128)(2,1)} %param.20), kind=kOutput, calls=%fused_computation.7 | convolution fusion | flops 104898560 | bytes 2805760 | tf_op jit(solution)/shard_map/dot_general | solution.py:256
  22.9 4.3 %fusion.5.part_ref = bf16[2,80,1024]{2,1,0:T(8,128)(2,1)} fusion(bf16[1024,2,1024]{2,1,0:T(2,128)(2,1)} %param.21, bf16[40,1024]{1,0:T(8,128)(2,1)S(1)} %convolution_convert_fusion, bf16[40,1024]{1,0:T(8,128)(2,1)S(1)} %constant_dynamic-slice_fusion.3), kind=kOutput, calls=%fused_computation.6 | convolution fusion | flops 336035840 | bytes 4685824 | tf_op jit(solution)/shard_map/rk,kcn->crn/dot_general | solution.py:259
  29.9 1.9 %collective-permute-start.6 = (bf16[160,768]{1,0:T(8,128)(2,1)S(1)}, bf16[160,768]{1,0:T(8,128)(2,1)S(1)}, u32[]{:S(2)}, u32[]{:S(2)}) collective-permute-start(bf16[160,768]{1,0:T(8,128)(2,1)S(1)} %collective-permute-done.refs_1_), channel_id=1, source_target_pairs={{0,6},{1,7},{2,0},{3,1},{4,2},{5,3},{6,4},{7,5},{8,14},{9,15},{10,... | collective-permute-start | bytes 737288 | tf_op jit(solution)/shard_map/ppermute | solution.py:216
  32.3 7.8 %all-to-all-start = ((bf16[8,80,256]{2,1,0:T(8,128)(2,1)}), bf16[8,80,256]{2,1,0:T(8,128)(2,1)S(1)}, u32[]{:S(2)}, u32[]{:S(2)}) async-start(bf16[8,80,256]{2,1,0:T(8,128)(2,1)} %heads.1), calls=%async_computation | async-start | bytes 655360 | tf_op jit(solution)/shard_map/all_to_all | solution.py:343
  43.5 5.6 %qkv.1 = (bf16[160,768]{1,0:T(8,128)(2,1)}, bf16[320,768]{1,0:T(8,128)(2,1)}) custom-call(s32[3]{0:T(128)} %pad_add_fusion.at_ref.pipe_ref, bf16[160,768]{1,0:T(8,128)(2,1)} %turn.1.refs_0_, bf16[160,768]{1,0:T(8,128)(2,1)} %copy-done.2, bf16[160,768]{1,0:T(8,128)(2,1)} %copy-done.3, bf16[160,768]{1,0:T(8,128)(2,1)} %copy-done.4, ...), custom_call_target="tpu_custom_call" | custom-call | flops 943718400 | bytes 6291456 | tf_op jit(solution)/shard_map/qkv/pallas_call | solution.py:317
  49.1 4.0 %collective-permute-start.8 = (bf16[320,768]{1,0:T(8,128)(2,1)}, bf16[320,768]{1,0:T(8,128)(2,1)S(1)}, u32[]{:S(2)}, u32[]{:S(2)}) collective-permute-start(bf16[320,768]{1,0:T(8,128)(2,1)} %get-tuple-element.20.own_ref), channel_id=1, source_target_pairs={{0,8},{8,0},{1,9},{9,1},{2,10},{10,2},{3,11},{11,3},{4,12},{12,4},... | collective-permute-start | bytes 1474568 | tf_op jit(solution)/shard_map/ppermute | solution.py:332
  53.1 2.6 %collective-permute-start.16 = (bf16[80,256]{1,0:T(8,128)(2,1)S(1)}, bf16[80,256]{1,0:T(8,128)(2,1)S(1)}, u32[]{:S(2)}, u32[]{:S(2)}) collective-permute-start(bf16[80,256]{1,0:T(8,128)(2,1)S(1)} %reduce_sum.62), channel_id=1, source_target_pairs={{0,16},{16,32},{32,48},{48,0},{64,80},{80,96},{96,112},{112,64},{1... | collective-permute-start | bytes 122888 | tf_op jit(solution)/shard_map/ppermute | solution.py:280
  56.3 2.3 %collective-permute-start.18 = (bf16[80,256]{1,0:T(8,128)(2,1)S(1)}, bf16[80,256]{1,0:T(8,128)(2,1)S(1)}, u32[]{:S(2)}, u32[]{:S(2)}) collective-permute-start(bf16[80,256]{1,0:T(8,128)(2,1)S(1)} %reduce_sum.62), channel_id=1, source_target_pairs={{0,48},{16,0},{32,16},{48,32},{64,112},{80,64},{96,80},{112,96},{1... | collective-permute-start | bytes 122888 | tf_op jit(solution)/shard_map/ppermute | solution.py:280
  60.5 5.2 %encoder_attend.1.refs_8_ = bf16[160,768]{1,0:T(8,128)(2,1)} custom-call(s32[192]{0:T(256)} %count_ref.1, s32[3]{0:T(128)} %pad_add_fusion.at_ref.pipe_ref, bf16[160,768]{1,0:T(8,128)(2,1)} %get-tuple-element.19.q_ref, bf16[320,768]{1,0:T(8,128)(2,1)} %get-tuple-element.20.own_ref, bf16[320,768]{1,0:T(8,128)(2,1)} %copy-done.10), custom_call_target="tpu_custom_call" | custom-call | flops 125829120 | bytes 2097152 | tf_op jit(solution)/shard_map/encoder_attend/pallas_call | solution.py:333
  70.6 4.9 %collective-permute-start.9 = (bf16[160,768]{1,0:T(8,128)(2,1)}, bf16[160,768]{1,0:T(8,128)(2,1)}, u32[]{:S(2)}, u32[]{:S(2)}) collective-permute-start(bf16[160,768]{1,0:T(8,128)(2,1)} %encoder_attend.1.refs_8_), channel_id=1, source_target_pairs={{0,1},{1,0},{2,3},{3,2},{4,5},{5,4},{6,7},{7,6},{8,9},{9,8},{10,11... | collective-permute-start | bytes 737288 | tf_op jit(solution)/shard_map/ppermute | solution.py:213
  75.6 3.4 %collective-permute-start.19 = (bf16[4,80,256]{2,1,0:T(8,128)(2,1)S(1)}, bf16[4,80,256]{2,1,0:T(8,128)(2,1)S(1)}, u32[]{:S(2)}, u32[]{:S(2)}) collective-permute-start(bf16[4,80,256]{2,1,0:T(8,128)(2,1)S(1)} %pad_maximum_fusion.2), channel_id=1, source_target_pairs={{0,8},{8,0},{1,9},{9,1},{2,10},{10,2},{3,11},{11,3},{4,12},{12,4},... | collective-permute-start | bytes 491528 | tf_op jit(solution)/shard_map/ppermute | solution.py:348
  80.9 2.0 %collective-permute-start.22 = (bf16[2,4,80,256]{3,2,1,0:T(8,128)(2,1)S(1)}, bf16[2,4,80,256]{3,2,1,0:T(8,128)(2,1)S(1)}, u32[]{:S(2)}, u32[]{:S(2)}) collective-permute-start(bf16[2,4,80,256]{3,2,1,0:T(8,128)(2,1)S(1)} %pad_maximum_fusion.1), channel_id=1, source_target_pairs={{0,192},{16,208},{32,224},{48,240},{64,0},{80,16},{96,32},{112,48}... | collective-permute-start | bytes 983048 | tf_op jit(solution)/shard_map/ppermute | solution.py:280
  83.3 2.4 %collective-permute-start.14 = (bf16[160,768]{1,0:T(8,128)(2,1)}, bf16[160,768]{1,0:T(8,128)(2,1)}, u32[]{:S(2)}, u32[]{:S(2)}) collective-permute-start(bf16[160,768]{1,0:T(8,128)(2,1)} %collective-permute-done.9.refs_9_), channel_id=1, source_target_pairs={{0,6},{1,7},{2,0},{3,1},{4,2},{5,3},{6,4},{7,5},{8,14},{9,15},{10,... | collective-permute-start | bytes 737288 | tf_op jit(solution)/shard_map/ppermute | solution.py:216
  88.4 8.8 %collective-permute-done.20 = bf16[2,4,80,256]{3,2,1,0:T(8,128)(2,1)S(1)} collective-permute-done((bf16[2,4,80,256]{3,2,1,0:T(8,128)(2,1)S(1)}, bf16[2,4,80,256]{3,2,1,0:T(8,128)(2,1)S(1)}, u32[]{:S(2)}, u32[]{:S(2)}) %collective-permute-start.20) | collective-permute-done | bytes 327712 | tf_op jit(solution)/shard_map/ppermute | solution.py:280
  101.0 4.4 %collective-permute-done.15.refs_15_ = bf16[160,768]{1,0:T(8,128)(2,1)} collective-permute-done((bf16[160,768]{1,0:T(8,128)(2,1)}, bf16[160,768]{1,0:T(8,128)(2,1)}, u32[]{:S(2)}, u32[]{:S(2)}) %collective-permute-start.15) | collective-permute-done | bytes 245792 | tf_op jit(solution)/shard_map/ppermute | solution.py:216
  105.3 6.3 %memory.1 = bf16[2048,256]{1,0:T(8,128)(2,1)} custom-call(s32[3]{0:T(128)} %pad_add_fusion.at_ref.pipe_ref, s32[32]{0:T(128)} %select_reduce_fusion.2.pick_ref, bf16[160,768]{1,0:T(8,128)(2,1)} %turn.1.refs_0_, bf16[160,768]{1,0:T(8,128)(2,1)} %copy-done.2, bf16[160,768]{1,0:T(8,128)(2,1)} %copy-done.3, bf16[160,768]{1,0:T(8,128)(2,1)} %copy-done.4, ...), custom_call_target="tpu_custom_call" | custom-call | flops 1006632960 | bytes 6291456 | tf_op jit(solution)/shard_map/memory/pallas_call | solution.py:381
  111.7 4.5 %all-to-all-start.1 = ((bf16[16,128,256]{2,1,0:T(8,128)(2,1)}), bf16[16,128,256]{2,1,0:T(8,128)(2,1)S(1)}, u32[]{:S(2)}, u32[]{:S(2)}) async-start(bf16[16,128,256]{2,1,0:T(8,128)(2,1)} %bitcast.80), calls=%async_computation.1 | async-start | bytes 2097152 | tf_op jit(solution)/shard_map/all_to_all | solution.py:396
  122.6 2.8 %self_attend.1 = bf16[2,32,1024]{2,1,0:T(8,128)(2,1)} custom-call(s32[512,1]{1,0:T(8,128)} %reshape_reshape.8.len_ref, bf16[32,16,128]{2,1,0:T(8,128)(2,1)} %copy_bitcast_fusion.q_ref, bf16[32,48,256]{2,1,0:T(8,128)(2,1)} %maximum_maximum_fusion.kv_ref), custom_call_target="tpu_custom_call" | custom-call | flops 33554432 | bytes 4194304 | tf_op jit(solution)/shard_map/self_attend/pallas_call | solution.py:424
  126.1 17.1 %all-to-all-done.1 = bf16[16,128,256]{2,1,0:T(8,128)(2,1)S(1)} async-done(((bf16[16,128,256]{2,1,0:T(8,128)(2,1)}), bf16[16,128,256]{2,1,0:T(8,128)(2,1)S(1)}, u32[]{:S(2)}, u32[]{:S(2)}) %all-to-all-start.1) | async-done | bytes 1048608 | tf_op jit(solution)/shard_map/all_to_all | solution.py:396
  147.4 3.4 %cross_attend.1 = bf16[2,32,1024]{2,1,0:T(8,128)(2,1)} custom-call(s32[32]{0:T(128)} %get-tuple-element.33.slot_ref, s32[3]{0:T(128)} %pad_add_fusion.at_ref.pipe_ref, s32[512,1]{1,0:T(8,128)} %copy.46.count_ref, bf16[32,16,128]{2,1,0:T(8,128)(2,1)} %copy_bitcast_fusion.1.q_ref, bf16[2048,256]{1,0:T(8,128)(2,1)} %bitcast.79, ...), custom_call_target="tpu_custom_call" | custom-call | flops 33554432 | bytes 4194304 | tf_op jit(solution)/shard_map/cross_attend/pallas_call | solution.py:437
  (131 shorter events, 36.8 us)
Async XLA Ops:
  1.6 14.6 %collective-permute-start.1 = (bf16[40,1280]{1,0:T(8,128)(2,1)S(1)}, bf16[40,1280]{1,0:T(8,128)(2,1)S(1)}, u32[]{:S(2)}, u32[]{:S(2)}) collective-permute-start(bf16[40,1280]{1,0:T(8,128)(2,1)S(1)} %constant_dynamic-slice_fusion.2), channel_id=1, source_target_pairs={{0,0},{56,1},{64,2},{120,3},{128,4},{184,5},{192,6},{248,7},{4,8},... | collective-permute-start | bytes 307208 | tf_op jit(solution)/shard_map/ppermute | solution.py:245
  12.5 16.5 %collective-permute-start = (bf16[160,768]{1,0:T(8,128)(2,1)}, bf16[160,768]{1,0:T(8,128)(2,1)S(1)}, u32[]{:S(2)}, u32[]{:S(2)}) collective-permute-start(bf16[160,768]{1,0:T(8,128)(2,1)} %turn.1.refs_0_), channel_id=1, source_target_pairs={{0,1},{1,0},{2,3},{3,2},{4,5},{5,4},{6,7},{7,6},{8,9},{9,8},{10,11... | collective-permute-start | bytes 737288 | tf_op jit(solution)/shard_map/ppermute | solution.py:213
  16.2 15.5 %collective-permute-start.2 = (bf16[160,768]{1,0:T(8,128)(2,1)}, bf16[160,768]{1,0:T(8,128)(2,1)S(1)}, u32[]{:S(2)}, u32[]{:S(2)}) collective-permute-start(bf16[160,768]{1,0:T(8,128)(2,1)} %turn.1.refs_0_), channel_id=1, source_target_pairs={{0,2},{1,3},{2,4},{3,5},{4,6},{5,7},{6,0},{7,1},{8,10},{9,11},{10,... | collective-permute-start | bytes 737288 | tf_op jit(solution)/shard_map/ppermute | solution.py:214
  18.7 23.2 %collective-permute-start.3 = (bf16[160,768]{1,0:T(8,128)(2,1)}, bf16[160,768]{1,0:T(8,128)(2,1)S(1)}, u32[]{:S(2)}, u32[]{:S(2)}) collective-permute-start(bf16[160,768]{1,0:T(8,128)(2,1)} %turn.1.refs_0_), channel_id=1, source_target_pairs={{0,6},{1,7},{2,0},{3,1},{4,2},{5,3},{6,4},{7,5},{8,14},{9,15},{10,... | collective-permute-start | bytes 737288 | tf_op jit(solution)/shard_map/ppermute | solution.py:214
  19.5 22.4 %collective-permute-start.4 = (bf16[160,768]{1,0:T(8,128)(2,1)}, bf16[160,768]{1,0:T(8,128)(2,1)S(1)}, u32[]{:S(2)}, u32[]{:S(2)}) collective-permute-start(bf16[160,768]{1,0:T(8,128)(2,1)} %turn.1.refs_0_), channel_id=1, source_target_pairs={{0,4},{1,5},{2,6},{3,7},{4,0},{5,1},{6,2},{7,3},{8,12},{9,13},{10,... | collective-permute-start | bytes 737288 | tf_op jit(solution)/shard_map/ppermute | solution.py:214
  29.0 12.9 %collective-permute-start.5 = (bf16[160,768]{1,0:T(8,128)(2,1)S(1)}, bf16[160,768]{1,0:T(8,128)(2,1)S(1)}, u32[]{:S(2)}, u32[]{:S(2)}) collective-permute-start(bf16[160,768]{1,0:T(8,128)(2,1)S(1)} %collective-permute-done.refs_1_), channel_id=1, source_target_pairs={{0,2},{1,3},{2,4},{3,5},{4,6},{5,7},{6,0},{7,1},{8,10},{9,11},{10,... | collective-permute-start | bytes 737288 | tf_op jit(solution)/shard_map/ppermute | solution.py:216
  29.9 12.1 %collective-permute-start.6 = (bf16[160,768]{1,0:T(8,128)(2,1)S(1)}, bf16[160,768]{1,0:T(8,128)(2,1)S(1)}, u32[]{:S(2)}, u32[]{:S(2)}) collective-permute-start(bf16[160,768]{1,0:T(8,128)(2,1)S(1)} %collective-permute-done.refs_1_), channel_id=1, source_target_pairs={{0,6},{1,7},{2,0},{3,1},{4,2},{5,3},{6,4},{7,5},{8,14},{9,15},{10,... | collective-permute-start | bytes 737288 | tf_op jit(solution)/shard_map/ppermute | solution.py:216
  31.7 10.3 %collective-permute-start.7 = (bf16[160,768]{1,0:T(8,128)(2,1)S(1)}, bf16[160,768]{1,0:T(8,128)(2,1)S(1)}, u32[]{:S(2)}, u32[]{:S(2)}) collective-permute-start(bf16[160,768]{1,0:T(8,128)(2,1)S(1)} %collective-permute-done.refs_1_), channel_id=1, source_target_pairs={{0,4},{1,5},{2,6},{3,7},{4,0},{5,1},{6,2},{7,3},{8,12},{9,13},{10,... | collective-permute-start | bytes 737288 | tf_op jit(solution)/shard_map/ppermute | solution.py:216
  32.3 20.7 %all-to-all-start = ((bf16[8,80,256]{2,1,0:T(8,128)(2,1)}), bf16[8,80,256]{2,1,0:T(8,128)(2,1)S(1)}, u32[]{:S(2)}, u32[]{:S(2)}) async-start(bf16[8,80,256]{2,1,0:T(8,128)(2,1)} %heads.1), calls=%async_computation | async-start | bytes 655360 | tf_op jit(solution)/shard_map/all_to_all | solution.py:343
  49.1 10.7 %collective-permute-start.8 = (bf16[320,768]{1,0:T(8,128)(2,1)}, bf16[320,768]{1,0:T(8,128)(2,1)S(1)}, u32[]{:S(2)}, u32[]{:S(2)}) collective-permute-start(bf16[320,768]{1,0:T(8,128)(2,1)} %get-tuple-element.20.own_ref), channel_id=1, source_target_pairs={{0,8},{8,0},{1,9},{9,1},{2,10},{10,2},{3,11},{11,3},{4,12},{12,4},... | collective-permute-start | bytes 1474568 | tf_op jit(solution)/shard_map/ppermute | solution.py:332
  53.1 5.5 %collective-permute-start.16 = (bf16[80,256]{1,0:T(8,128)(2,1)S(1)}, bf16[80,256]{1,0:T(8,128)(2,1)S(1)}, u32[]{:S(2)}, u32[]{:S(2)}) collective-permute-start(bf16[80,256]{1,0:T(8,128)(2,1)S(1)} %reduce_sum.62), channel_id=1, source_target_pairs={{0,16},{16,32},{32,48},{48,0},{64,80},{80,96},{96,112},{112,64},{1... | collective-permute-start | bytes 122888 | tf_op jit(solution)/shard_map/ppermute | solution.py:280
  65.8 14.4 %collective-permute-start.10 = (bf16[160,768]{1,0:T(8,128)(2,1)}, bf16[160,768]{1,0:T(8,128)(2,1)S(1)}, u32[]{:S(2)}, u32[]{:S(2)}) collective-permute-start(bf16[160,768]{1,0:T(8,128)(2,1)} %encoder_attend.1.refs_8_), channel_id=1, source_target_pairs={{0,2},{1,3},{2,4},{3,5},{4,6},{5,7},{6,0},{7,1},{8,10},{9,11},{10,... | collective-permute-start | bytes 737288 | tf_op jit(solution)/shard_map/ppermute | solution.py:214
  67.6 13.3 %collective-permute-start.11 = (bf16[160,768]{1,0:T(8,128)(2,1)}, bf16[160,768]{1,0:T(8,128)(2,1)S(1)}, u32[]{:S(2)}, u32[]{:S(2)}) collective-permute-start(bf16[160,768]{1,0:T(8,128)(2,1)} %encoder_attend.1.refs_8_), channel_id=1, source_target_pairs={{0,6},{1,7},{2,0},{3,1},{4,2},{5,3},{6,4},{7,5},{8,14},{9,15},{10,... | collective-permute-start | bytes 737288 | tf_op jit(solution)/shard_map/ppermute | solution.py:214
  69.4 13.5 %collective-permute-start.12 = (bf16[160,768]{1,0:T(8,128)(2,1)}, bf16[160,768]{1,0:T(8,128)(2,1)S(1)}, u32[]{:S(2)}, u32[]{:S(2)}) collective-permute-start(bf16[160,768]{1,0:T(8,128)(2,1)} %encoder_attend.1.refs_8_), channel_id=1, source_target_pairs={{0,4},{1,5},{2,6},{3,7},{4,0},{5,1},{6,2},{7,3},{8,12},{9,13},{10,... | collective-permute-start | bytes 737288 | tf_op jit(solution)/shard_map/ppermute | solution.py:214
  70.6 12.3 %collective-permute-start.9 = (bf16[160,768]{1,0:T(8,128)(2,1)}, bf16[160,768]{1,0:T(8,128)(2,1)}, u32[]{:S(2)}, u32[]{:S(2)}) collective-permute-start(bf16[160,768]{1,0:T(8,128)(2,1)} %encoder_attend.1.refs_8_), channel_id=1, source_target_pairs={{0,1},{1,0},{2,3},{3,2},{4,5},{5,4},{6,7},{7,6},{8,9},{9,8},{10,11... | collective-permute-start | bytes 737288 | tf_op jit(solution)/shard_map/ppermute | solution.py:213
  75.6 4.4 %collective-permute-start.19 = (bf16[4,80,256]{2,1,0:T(8,128)(2,1)S(1)}, bf16[4,80,256]{2,1,0:T(8,128)(2,1)S(1)}, u32[]{:S(2)}, u32[]{:S(2)}) collective-permute-start(bf16[4,80,256]{2,1,0:T(8,128)(2,1)S(1)} %pad_maximum_fusion.2), channel_id=1, source_target_pairs={{0,8},{8,0},{1,9},{9,1},{2,10},{10,2},{3,11},{11,3},{4,12},{12,4},... | collective-permute-start | bytes 491528 | tf_op jit(solution)/shard_map/ppermute | solution.py:348
  80.0 17.2 %collective-permute-start.20 = (bf16[2,4,80,256]{3,2,1,0:T(8,128)(2,1)S(1)}, bf16[2,4,80,256]{3,2,1,0:T(8,128)(2,1)S(1)}, u32[]{:S(2)}, u32[]{:S(2)}) collective-permute-start(bf16[2,4,80,256]{3,2,1,0:T(8,128)(2,1)S(1)} %pad_maximum_fusion.1), channel_id=1, source_target_pairs={{0,64},{16,80},{32,96},{48,112},{64,128},{80,144},{96,160},{112,17... | collective-permute-start | bytes 983048 | tf_op jit(solution)/shard_map/ppermute | solution.py:280
  80.1 18.6 %collective-permute-start.21 = (bf16[2,4,80,256]{3,2,1,0:T(8,128)(2,1)S(1)}, bf16[2,4,80,256]{3,2,1,0:T(8,128)(2,1)S(1)}, u32[]{:S(2)}, u32[]{:S(2)}) collective-permute-start(bf16[2,4,80,256]{3,2,1,0:T(8,128)(2,1)S(1)} %pad_maximum_fusion.1), channel_id=1, source_target_pairs={{0,128},{16,144},{32,160},{48,176},{64,192},{80,208},{96,224},{112... | collective-permute-start | bytes 983048 | tf_op jit(solution)/shard_map/ppermute | solution.py:280
  80.9 17.8 %collective-permute-start.22 = (bf16[2,4,80,256]{3,2,1,0:T(8,128)(2,1)S(1)}, bf16[2,4,80,256]{3,2,1,0:T(8,128)(2,1)S(1)}, u32[]{:S(2)}, u32[]{:S(2)}) collective-permute-start(bf16[2,4,80,256]{3,2,1,0:T(8,128)(2,1)S(1)} %pad_maximum_fusion.1), channel_id=1, source_target_pairs={{0,192},{16,208},{32,224},{48,240},{64,0},{80,16},{96,32},{112,48}... | collective-permute-start | bytes 983048 | tf_op jit(solution)/shard_map/ppermute | solution.py:280
  82.9 18.0 %collective-permute-start.13 = (bf16[160,768]{1,0:T(8,128)(2,1)}, bf16[160,768]{1,0:T(8,128)(2,1)}, u32[]{:S(2)}, u32[]{:S(2)}) collective-permute-start(bf16[160,768]{1,0:T(8,128)(2,1)} %collective-permute-done.9.refs_9_), channel_id=1, source_target_pairs={{0,2},{1,3},{2,4},{3,5},{4,6},{5,7},{6,0},{7,1},{8,10},{9,11},{10,... | collective-permute-start | bytes 737288 | tf_op jit(solution)/shard_map/ppermute | solution.py:216
  83.3 17.7 %collective-permute-start.14 = (bf16[160,768]{1,0:T(8,128)(2,1)}, bf16[160,768]{1,0:T(8,128)(2,1)}, u32[]{:S(2)}, u32[]{:S(2)}) collective-permute-start(bf16[160,768]{1,0:T(8,128)(2,1)} %collective-permute-done.9.refs_9_), channel_id=1, source_target_pairs={{0,6},{1,7},{2,0},{3,1},{4,2},{5,3},{6,4},{7,5},{8,14},{9,15},{10,... | collective-permute-start | bytes 737288 | tf_op jit(solution)/shard_map/ppermute | solution.py:216
  97.3 8.1 %collective-permute-start.15 = (bf16[160,768]{1,0:T(8,128)(2,1)}, bf16[160,768]{1,0:T(8,128)(2,1)}, u32[]{:S(2)}, u32[]{:S(2)}) collective-permute-start(bf16[160,768]{1,0:T(8,128)(2,1)} %collective-permute-done.9.refs_9_), channel_id=1, source_target_pairs={{0,4},{1,5},{2,6},{3,7},{4,0},{5,1},{6,2},{7,3},{8,12},{9,13},{10,... | collective-permute-start | bytes 737288 | tf_op jit(solution)/shard_map/ppermute | solution.py:216
  111.7 31.5 %all-to-all-start.1 = ((bf16[16,128,256]{2,1,0:T(8,128)(2,1)}), bf16[16,128,256]{2,1,0:T(8,128)(2,1)S(1)}, u32[]{:S(2)}, u32[]{:S(2)}) async-start(bf16[16,128,256]{2,1,0:T(8,128)(2,1)} %bitcast.80), calls=%async_computation.1 | async-start | bytes 2097152 | tf_op jit(solution)/shard_map/all_to_all | solution.py:396
  143.2 4.2 %collective-permute-start.23 = (bf16[2048,256]{1,0:T(8,128)(2,1)S(1)}, bf16[2048,256]{1,0:T(8,128)(2,1)}, u32[]{:S(2)}, u32[]{:S(2)}) collective-permute-start(bf16[2048,256]{1,0:T(8,128)(2,1)S(1)} %bitcast.78), channel_id=1, source_target_pairs={{0,8},{8,0},{1,9},{9,1},{2,10},{10,2},{3,11},{11,3},{4,12},{12,4},... | collective-permute-start | bytes 3145736 | tf_op jit(solution)/shard_map/ppermute | solution.py:435
  (24 other events, 207.0 us)
